TPU v7x, 32 devices: a whole 2x2x4 slice. The times are simulated.
32 devices in a mesh: rows: 8 (over z, x), blk: 4 (over y, core).
Axes of the slice: x: 2, y: 2, z: 4, core: 2. Of those that a mesh axis runs over, the one named last changes fastest.
Arguments:
- tokens: bfloat16 [32, 1024, 512], P('rows', 'blk'), may hold values from -6 to 6
- seg_lengths: int32 [32, 8], P('rows'), may hold values from 1 to 1017, as said below
- ln1_gain: float32 [512], replicated, may hold values from 0.25 to 1.75
- ln1_bias: float32 [512], replicated, may hold values from -1 to 1
- w_qkv: bfloat16 [512, 1536], replicated, may hold values from -0.25 to 0.25
- b_qv: float32 [1024], replicated, may hold values from -1 to 1
- w_o: bfloat16 [512, 512], replicated, may hold values from -1 to 1
- b_o: float32 [512], replicated, may hold values from -1 to 1
- ln2_gain: float32 [512], replicated, may hold values from 0.25 to 1.75
- ln2_bias: float32 [512], replicated, may hold values from -1 to 1
- w_up: bfloat16 [512, 1024], replicated, may hold values from -0.25 to 0.25
- b_up: float32 [1024], replicated, may hold values from -1 to 1
- w_down: bfloat16 [1024, 512], replicated, may hold values from -0.1875 to 0.1875
- b_down: float32 [512], replicated, may hold values from -1 to 1
- cotangent: bfloat16 [32, 1024, 512], P('rows', 'blk'), may hold values from -6 to 6
Outputs:
- output: bfloat16 [32, 1024, 512], P('rows', 'blk')
- input_grad: float32 [32, 1024, 512], P('rows', 'blk')
- grad_ln1_gain: float32 [512], replicated
- grad_ln1_bias: float32 [512], replicated
- grad_w_qkv: float32 [512, 1536], replicated
- grad_b_qv: float32 [1024], replicated
- grad_w_o: float32 [512, 512], replicated
- grad_b_o: float32 [512], replicated
- grad_ln2_gain: float32 [512], replicated
- grad_ln2_bias: float32 [512], replicated
- grad_w_up: float32 [512, 1024], replicated
- grad_b_up: float32 [1024], replicated
- grad_w_down: float32 [1024, 512], replicated
- grad_b_down: float32 [512], replicated
Inputs may be any that keep to these rules, and one draw needn't show every extreme that they name: `seg_lengths`: each row's 8 cell lengths sum to 1024; in each aligned block of 4 rows that starts at a multiple of 4, one row holds a cell of exactly 1017 tokens.
All inputs are finite; a program needn't handle non-finite values.
Results may differ from a plain program's by a relative error of at most 0.009.
Values may be sent and summed in bfloat16 or wider, within the bound.
No kernel may reach another device: no remote copies, remote signals or barrier semaphores. Data moves between devices by JAX's collectives and lax.ppermute only.
A program may use at most 192 MiB of HBM per device.

v0:
```python
import functools

import jax
import jax.numpy as jnp
from jax import lax
from jax.experimental import pallas as pl
from jax.experimental.pallas import tpu as pltpu
from jax.sharding import PartitionSpec as P

HEADS = 8
norm_eps = 1e-05
neg_big = -1e30
BOTH = ("rows", "blk")
F32 = jnp.float32
BF16 = jnp.bfloat16
TILE = 256
LANES = 128
MIB = 1024 * 1024
B_FLOPS = 1e9
L_FLOPS = 1e9
MID_TILE = 512
MID_MIB = 28
LAST_MIB = 26


def mm(lhs, rhs):
    return lax.dot_general(lhs, rhs, (((1,), (0,)), ((), ())), preferred_element_type=F32)


def mm_nt(lhs, rhs):
    return lax.dot_general(lhs, rhs, (((1,), (1,)), ((), ())), preferred_element_type=F32)


def mm_tn(lhs, rhs):
    return lax.dot_general(lhs, rhs, (((0,), (0,)), ((), ())), preferred_element_type=F32)


def cell_start(ends_ref, positions):
    start = jnp.zeros_like(positions)
    for c in range(ends_ref.shape[0]):
        start = jnp.where(ends_ref[c] <= positions, ends_ref[c], start)
    return start


def norm_parts(values):
    average = jnp.mean(values, axis=-1, keepdims=True)
    centered = values - average
    variance = jnp.mean(centered * centered, axis=-1, keepdims=True)
    scale = lax.rsqrt(variance + norm_eps)
    return centered * scale, scale


def norm_pull(e, n, scale, gain):
    f = e * gain
    return (
        f
        - jnp.mean(f, axis=-1, keepdims=True)
        - n * jnp.mean(f * n, axis=-1, keepdims=True)
    ) * scale


def head_lanes(shape, half):
    lane = lax.broadcasted_iota(jnp.int32, shape, len(shape) - 1)
    return (lane < LANES // 2) if half == 0 else (lane >= LANES // 2)


def only_head(values, half):
    return jnp.where(head_lanes(values.shape, half), values, jnp.zeros_like(values))


def in_order(blk_ref, pieces, whole_ref):
    size = pieces[0].shape[0]
    for flip, piece_ref in enumerate(pieces):
        at = jnp.bitwise_xor(blk_ref[0], flip) * size
        whole_ref[pl.ds(pl.multiple_of(at, size), size), :] = piece_ref[...]


def forward_kernel(
    ends_ref, blk_ref, x0_ref, x1_ref, x2_ref, x3_ref, gain_ref, bias_ref, w_ref, b_ref,
    x_ref, q_ref, k_ref, v_ref, n1_ref, att_ref, lse_ref,
    mask_ref,
):
    in_order(blk_ref, (x0_ref, x1_ref, x2_ref, x3_ref), x_ref)
    t, width = x_ref.shape
    pairs = width // LANES
    scale_qk = (width // HEADS) ** (-0.5)
    for low in range(0, t, 512):
        rows = slice(low, low + 512)
        n, _ = norm_parts(x_ref[rows].astype(F32))
        n1 = (n * gain_ref[...] + bias_ref[...]).astype(BF16)
        n1_ref[rows] = n1
        q = mm(n1, w_ref[:, :width]) + b_ref[:, :width]
        q = (q.astype(BF16).astype(F32) * scale_qk).astype(BF16)
        k = mm(n1, w_ref[:, width : 2 * width]).astype(BF16)
        v = (mm(n1, w_ref[:, 2 * width :]) + b_ref[:, width:]).astype(BF16)
        for g in range(pairs):
            cols = slice(g * LANES, (g + 1) * LANES)
            q_ref[g, rows, :] = q[:, cols]
            k_ref[g, rows, :] = k[:, cols]
            v_ref[g, rows, :] = v[:, cols]
    for low in range(0, t, TILE):
        reach = low + TILE
        rows = slice(low, reach)
        q_pos = low + lax.broadcasted_iota(jnp.int32, (TILE, 1), 0)
        k_pos = lax.broadcasted_iota(jnp.int32, (TILE, reach), 1)
        start = cell_start(ends_ref, q_pos)
        mask_ref[:, :reach] = jnp.where((k_pos <= q_pos) & (k_pos >= start), 0.0, neg_big)
        lse_all = jnp.zeros((TILE, LANES), F32)
        lane = lax.broadcasted_iota(jnp.int32, lse_all.shape, 1)
        for g in range(pairs):
            qp = q_ref[g, rows, :]
            kp = k_ref[g, :reach, :]
            vp = v_ref[g, :reach, :]
            outs = []
            for half in range(2):
                s = mm_nt(only_head(qp, half), kp) + mask_ref[:, :reach]
                top = jnp.max(s, axis=-1, keepdims=True)
                p = jnp.exp(s - top)
                total = jnp.sum(p, axis=-1, keepdims=True)
                outs.append(mm(p.astype(BF16), vp) / total)
                lse_all = jnp.where(lane == 2 * g + half, top + jnp.log(total), lse_all)
            att_ref[g, rows, :] = jnp.where(head_lanes(outs[0].shape, 0), outs[0], outs[1])
        lse_ref[:, rows] = jnp.transpose(lse_all)[:HEADS]


def whole(shape):
    return pl.BlockSpec(shape, lambda i: (0,) * len(shape))


def by_row(cols, tile=TILE):
    return pl.BlockSpec((tile, cols), lambda i: (i, 0))


def by_pair(pairs, tile=TILE):
    return pl.BlockSpec((pairs, tile, LANES), lambda i: (0, i, 0))


def heads_row(tile=TILE):
    return pl.BlockSpec((HEADS, tile), lambda i: (0, i))


SMEM_SPEC = pl.BlockSpec(memory_space=pltpu.SMEM)


def in_hbm(*arrays):
    return [pltpu.with_memory_space_constraint(a, pltpu.HBM) for a in arrays]


def params(mib):
    return pltpu.CompilerParams(dimension_semantics=("arbitrary",), vmem_limit_bytes=mib * MIB)


def cost(flops, moved):
    return pl.CostEstimate(flops=int(flops), bytes_accessed=int(moved), transcendentals=0)


def forward_call(ends, blk, pieces, gain, bias, w_qkv, b_qv):
    size, d = pieces[0].shape
    t = size * len(pieces)
    pairs = d // LANES
    return pl.pallas_call(
        forward_kernel,
        grid=(1,),
        in_specs=[SMEM_SPEC, SMEM_SPEC]
        + [whole((size, d))] * len(pieces)
        + [whole((1, d)), whole((1, d)), whole(w_qkv.shape), whole((1, 2 * d))],
        out_specs=[
            whole((t, d)), whole((pairs, t, LANES)), whole((pairs, t, LANES)), whole((pairs, t, LANES)), whole((t, d)),
            whole((pairs, t, LANES)), whole((HEADS, t)),
        ],
        out_shape=[
            jax.ShapeDtypeStruct((t, d), BF16),
            pltpu.HBM((pairs, t, LANES), BF16),
            pltpu.HBM((pairs, t, LANES), BF16),
            pltpu.HBM((pairs, t, LANES), BF16),
            pltpu.HBM((t, d), BF16),
            jax.ShapeDtypeStruct((pairs, t, LANES), F32),
            jax.ShapeDtypeStruct((HEADS, t), F32),
        ],
        scratch_shapes=[pltpu.VMEM((TILE, t), F32)],
        compiler_params=params(34),
        cost_estimate=cost(20e9, 10e6),
        name="forward",
    )(ends, blk, *pieces, gain[None], bias[None], w_qkv, b_qv[None])


def split_halves(core_ref, whole_ref, keep_ref, send_ref):
    half = keep_ref.shape[0]
    core = core_ref[0]
    keep_ref[...] = whole_ref[pl.ds(pl.multiple_of(core * half, half), half), :]
    send_ref[...] = whole_ref[pl.ds(pl.multiple_of((1 - core) * half, half), half), :].astype(BF16)


def middle_kernel(
    core_ref, blk_ref, att_ref, x_ref, c0_ref, c1_ref, c2_ref, c3_ref, wo_ref, bo_ref, gain_ref, bias_ref, wup_ref, bup_ref, wdown_ref, bdown_ref,
    out_ref, gmid_ref, gatt_ref, delta_ref, keep_ref, send_ref, vec_ref,
    cot_ref, gw_ref, hidden_ref, gpre_ref, n2_ref, attb_ref, gbr_ref,
):
    pairs = att_ref.shape[0]
    t, d = x_ref.shape
    ff = wup_ref.shape[-1]
    c0 = 0.7978845608028654
    c1 = 0.044715

    def col(values):
        return jnp.sum(values, axis=0, keepdims=True)

    in_order(blk_ref, (c0_ref, c1_ref, c2_ref, c3_ref), cot_ref)
    vec_ref[...] = jnp.zeros_like(vec_ref)
    head = lax.broadcasted_iota(jnp.int32, (HEADS, d), 0)
    lane = lax.broadcasted_iota(jnp.int32, (HEADS, d), 1)
    ones = jnp.where(lane // (d // HEADS) == head, 1.0, 0.0).astype(BF16)
    def tile(step, carry):
        rows = pl.ds(pl.multiple_of(step * MID_TILE, MID_TILE), MID_TILE)
        att = jnp.concatenate([att_ref[g, rows, :] for g in range(pairs)], axis=-1)
        att_b = att.astype(BF16)
        attb_ref[rows, :] = att_b
        middle = x_ref[rows, :].astype(F32) + mm(att_b, wo_ref[...]) + bo_ref[...]
        n, scale = norm_parts(middle)
        n2 = (n * gain_ref[...] + bias_ref[...]).astype(BF16)
        n2_ref[rows, :] = n2
        pre = mm(n2, wup_ref[...]) + bup_ref[...]
        sq = pre * pre
        th = jnp.tanh(c0 * (pre + c1 * (sq * pre)))
        half_one = 0.5 * (1.0 + th)
        hidden = (pre * half_one).astype(BF16)
        hidden_ref[rows, :] = hidden
        slope = half_one + (0.5 * pre) * (1.0 - th * th) * (c0 + (3.0 * c0 * c1) * sq)
        out_ref[rows, :] = (middle + mm(hidden, wdown_ref[...]) + bdown_ref[...]).astype(BF16)
        cot = cot_ref[rows, :]
        cot_f = cot.astype(F32)
        gpre = (mm_nt(cot, wdown_ref[...]) * slope).astype(BF16)
        gpre_ref[rows, :] = gpre
        e = mm_nt(gpre, wup_ref[...])
        gmid = cot_f + norm_pull(e, n, scale, gain_ref[...])
        gmid_ref[rows, :] = gmid
        gbr = gmid.astype(BF16)
        gbr_ref[rows, :] = gbr
        gatt = mm_nt(gbr, wo_ref[...]).astype(BF16)
        for g in range(pairs):
            gatt_ref[g, rows, :] = gatt[:, g * LANES : (g + 1) * LANES]
        prod = gatt.astype(F32) * att
        hi = prod.astype(BF16)
        lo = (prod - hi.astype(F32)).astype(BF16)
        delta_ref[:, rows] = mm_nt(ones, hi) + mm_nt(ones, lo)
        gsum = col(gpre.astype(F32))
        vec_ref[0:1] += col(cot_f)
        vec_ref[1:2] += gsum[:, :d]
        vec_ref[2:3] += gsum[:, d:]
        vec_ref[3:4] += col(e * n)
        vec_ref[4:5] += col(e)
        vec_ref[5:6] += col(gbr.astype(F32))
        return carry

    lax.fori_loop(0, t // MID_TILE, tile, 0)
    gw_ref[:ff] = mm_tn(hidden_ref[...], cot_ref[...])
    gw_ref[ff : ff + d] = mm_tn(n2_ref[...], gpre_ref[:, :d])
    gw_ref[ff + d : ff + 2 * d] = mm_tn(n2_ref[...], gpre_ref[:, d:])
    gw_ref[ff + 2 * d :] = mm_tn(attb_ref[...], gbr_ref[...])
    split_halves(core_ref, gw_ref, keep_ref, send_ref)


def middle_call(core, blk, att, x, cots, w_o, b_o, gain, bias, w_up, b_up, w_down, b_down):
    t, d = x.shape
    pairs = d // LANES
    ff = w_up.shape[1]
    half = (ff + 3 * d) // 2
    return pl.pallas_call(
        middle_kernel,
        grid=(1,),
        in_specs=[
            SMEM_SPEC, SMEM_SPEC,
            by_pair(pairs, t), by_row(d, t), *[whole(c.shape) for c in cots], whole((d, d)), whole((1, d)), whole((1, d)), whole((1, d)),
            whole((d, ff)), whole((1, ff)), whole((ff, d)), whole((1, d)),
        ],
        out_specs=[
            by_row(d, t), by_row(d, t), by_pair(pairs, t), heads_row(t), whole((half, d)), whole((half, d)),
            whole((8, d)),
        ],
        out_shape=[
            pltpu.HBM((t, d), BF16),
            pltpu.HBM((t, d), F32),
            pltpu.HBM((pairs, t, LANES), BF16),
            jax.ShapeDtypeStruct((HEADS, t), F32),
            jax.ShapeDtypeStruct((half, d), F32),
            jax.ShapeDtypeStruct((half, d), BF16),
            jax.ShapeDtypeStruct((8, d), F32),
        ],
        scratch_shapes=[
            pltpu.VMEM((t, d), BF16),
            pltpu.VMEM((2 * half, d), F32),
            pltpu.VMEM((t, ff), BF16),
            pltpu.VMEM((t, ff), BF16),
            pltpu.VMEM((t, d), BF16),
            pltpu.VMEM((t, d), BF16),
            pltpu.VMEM((t, d), BF16),
        ],
        compiler_params=params(28),
        cost_estimate=cost(15e9, 20e6),
        name="middle",
    )(core, blk, att, x, *cots, w_o, b_o[None], gain[None], bias[None], w_up, b_up[None], w_down, b_down[None])


def backward_kernel(first, ends_ref, q_ref, k_ref, v_ref, g_ref, lse_ref, delta_ref, dq_ref, dk_ref, dv_ref, acc_ref):
    pair = pl.program_id(0) + first
    t = q_ref.shape[1]
    scale_qk = (LANES // 2) ** (-0.5)
    pos_row = lax.broadcasted_iota(jnp.int32, (1, t), 1)
    start_row = cell_start(ends_ref, pos_row)
    acc_ref[...] = jnp.zeros_like(acc_ref)
    jobs = [(j, half) for j in range(t // TILE) for half in range(2)]
    lses = [lse_ref[pl.ds(2 * pair + half, 1), :] for half in range(2)]
    deltas = [delta_ref[pl.ds(2 * pair + half, 1), :] for half in range(2)]
    kts = {}
    outs = {}

    def scores(job):
        j, half = job
        low = j * TILE
        km = only_head(k_ref[0, low : low + TILE, :], half)
        vm = only_head(v_ref[0, low : low + TILE, :], half)
        return mm_nt(km, q_ref[0, low:, :]), mm_nt(vm, g_ref[0, low:, :])

    def rest(job, s, dp):
        j, half = job
        low = j * TILE
        k_pos = low + lax.broadcasted_iota(jnp.int32, (TILE, t - low), 0)
        high = low + TILE
        diag = (k_pos[:, :TILE] >= start_row[:, low:high]) & (k_pos[:, :TILE] <= pos_row[:, low:high])
        p = jnp.exp(jnp.where(diag, s[:, :TILE] - lses[half][:, low:high], neg_big))
        if high < t:
            far = k_pos[:, TILE:] >= start_row[:, high:]
            p = jnp.concatenate([p, jnp.exp(jnp.where(far, s[:, TILE:] - lses[half][:, high:], neg_big))], axis=1)
        ds = (p * (dp - deltas[half][:, low:])).astype(BF16)
        dv = mm(p.astype(BF16), g_ref[0, low:, :])
        dk = mm(ds, q_ref[0, low:, :])
        kt = jnp.transpose(k_ref[0, low : low + TILE, :])
        rows = slice(half * 64, half * 64 + 64)
        acc_ref[rows, low:] += mm(kt[rows], ds)
        if half == 0:
            outs[j] = (dk, dv)
        else:
            first_lanes = head_lanes(dk.shape, 0)
            dk_ref[0, low : low + TILE, :] = jnp.where(first_lanes, outs[j][0], dk).astype(BF16)
            dv_ref[0, low : low + TILE, :] = jnp.where(first_lanes, outs[j][1], dv).astype(BF16)

    ready = scores(jobs[0])
    for at, job in enumerate(jobs):
        now = ready
        if at + 1 < len(jobs):
            ready = scores(jobs[at + 1])
        rest(job, *now)
    dq_ref[0] = jnp.transpose((acc_ref[...] * scale_qk)).astype(BF16)


def backward_call(ends, q, k, v, gatt, lse, delta, first, count):
    pairs, t, _ = q.shape
    spec = pl.BlockSpec((1, t, LANES), lambda i: (i + first, 0, 0))
    out = pl.BlockSpec((1, t, LANES), lambda i: (i, 0, 0))
    return pl.pallas_call(
        functools.partial(backward_kernel, first),
        grid=(count,),
        in_specs=[SMEM_SPEC, spec, spec, spec, spec, whole((HEADS, t)), whole((HEADS, t))],
        out_specs=[out, out, out],
        out_shape=[pltpu.HBM((count, t, LANES), BF16)] * 3,
        scratch_shapes=[pltpu.VMEM((LANES, t), F32)],
        compiler_params=params(28),
        cost_estimate=cost(count * B_FLOPS, count * 1e5),
        name="backward",
    )(ends, *in_hbm(q, k, v, gatt), lse, delta)


VEC_ROWS = 128


def last_kernel(*refs):
    core_ref = refs[0]
    grads = refs[1:4]
    n1_ref, x_ref, gmid_ref, gain_ref, w_ref, vecmid_ref, gin_ref, keep_ref, send_ref, gw_ref = refs[4:]
    pairs = grads[0].shape[0]
    d = x_ref.shape[-1]
    half = keep_ref.shape[0]
    gqkv = jnp.concatenate([grads[part][g] for part in range(3) for g in range(pairs)], axis=-1)
    gw = mm_tn(n1_ref[...], gqkv)
    blocks = 3 * pairs
    for p in range(blocks):
        at = (p // (blocks // 2)) * half + (p % (blocks // 2)) * d
        gw_ref[at : at + d] = gw[:, p * LANES : (p + 1) * LANES]
    e = mm_nt(gqkv, w_ref[...])
    n, scale = norm_parts(x_ref[...].astype(F32))
    gin_ref[...] = (gmid_ref[...] + norm_pull(e, n, scale, gain_ref[...])).astype(BF16)

    def col(values):
        return jnp.sum(values, axis=0, keepdims=True)

    rows = [vecmid_ref[r : r + 1] for r in range(6)]
    rows += [col(e * n), col(e), col(gqkv[:, :d].astype(F32)), col(gqkv[:, 2 * d :].astype(F32))]
    base = half - VEC_ROWS
    gw_ref[base:half] = jnp.zeros((VEC_ROWS, LANES), F32)
    gw_ref[half + base :] = jnp.zeros((VEC_ROWS, LANES), F32)
    for r, row in enumerate(rows):
        for g in range(d // LANES):
            at = base + r * (d // LANES) + g
            gw_ref[at : at + 1] = row[:, g * LANES : (g + 1) * LANES]
    split_halves(core_ref, gw_ref, keep_ref, send_ref)


def last_call(core, grads, n1, x, gmid, gain, w_qkv, vec_mid):
    t, d = x.shape
    half = 3 * d * d // LANES // 2 + VEC_ROWS
    return pl.pallas_call(
        last_kernel,
        grid=(1,),
        in_specs=[SMEM_SPEC]
        + [whole(a.shape) for a in grads]
        + [by_row(d, t), by_row(d, t), by_row(d, t), whole((1, d)), whole(w_qkv.shape), whole((8, d))],
        out_specs=[by_row(d, t), whole((half, LANES)), whole((half, LANES))],
        out_shape=[
            pltpu.HBM((t, d), BF16),
            jax.ShapeDtypeStruct((half, LANES), F32),
            jax.ShapeDtypeStruct((half, LANES), BF16),
        ],
        scratch_shapes=[pltpu.VMEM((2 * half, LANES), F32)],
        compiler_params=params(28),
        cost_estimate=cost(L_FLOPS, 1e5),
        name="last",
    )(core, *in_hbm(*grads), n1, x, gmid, gain[None], w_qkv, vec_mid)


def ordered_halves(core_ref, own_ref, got_ref, write):
    pl.when(core_ref[0] == 0)(functools.partial(write, own_ref, got_ref))
    pl.when(core_ref[0] == 1)(functools.partial(write, got_ref, own_ref))


def finish_mid_kernel(core_ref, own_ref, got_ref, down_ref, up_ref, wo_ref):
    ff, d = down_ref.shape
    half = own_ref.shape[0]

    def write(low_ref, high_ref):
        def take(first, last):
            if last <= half:
                return low_ref[first:last].astype(F32)
            if first >= half:
                return high_ref[first - half : last - half].astype(F32)
            return jnp.concatenate([take(first, half), take(half, last)], axis=0)

        down_ref[...] = take(0, ff)
        up_ref[:, :d] = take(ff, ff + d)
        up_ref[:, d:] = take(ff + d, ff + 2 * d)
        wo_ref[...] = take(ff + 2 * d, ff + 3 * d)

    ordered_halves(core_ref, own_ref, got_ref, write)


def copy_kernel(in_ref, out_ref):
    out_ref[...] = in_ref[...].astype(out_ref.dtype)


def copy_call(order, values, dtype):
    parts, rows, d = values.shape
    spec = pl.BlockSpec((1, rows, d), lambda i: (i, 0, 0))
    return pl.pallas_call(
        lambda order_ref, in_ref, out_ref: copy_kernel(in_ref, out_ref),
        grid=(parts,),
        in_specs=[SMEM_SPEC, spec],
        out_specs=spec,
        out_shape=jax.ShapeDtypeStruct(values.shape, dtype),
        compiler_params=params(28),
        cost_estimate=cost(1e7, 1e5),
        name="copy",
    )(order, values)


def finish_last_kernel(core_ref, own_ref, got_ref, qkv_ref, *vec_refs):
    d = qkv_ref.shape[0]
    half = own_ref.shape[0]
    blocks = qkv_ref.shape[1] // LANES

    def write(low_ref, high_ref):
        for p in range(blocks):
            ref = (low_ref, high_ref)[p // (blocks // 2)]
            at = (p % (blocks // 2)) * d
            qkv_ref[:, p * LANES : (p + 1) * LANES] = ref[at : at + d].astype(F32)
        at = half - VEC_ROWS
        for ref in vec_refs:
            for g in range(ref.shape[1] // LANES):
                ref[:, g * LANES : (g + 1) * LANES] = low_ref[at : at + 1].astype(F32)
                at += 1

    ordered_halves(core_ref, own_ref, got_ref, write)


def finish_call(kernel, core, own, got, shapes, name):
    return pl.pallas_call(
        kernel,
        grid=(1,),
        in_specs=[SMEM_SPEC, whole(own.shape), whole(got.shape)],
        out_specs=[whole(shape) for shape in shapes],
        out_shape=[jax.ShapeDtypeStruct(shape, F32) for shape in shapes],
        compiler_params=params(28),
        cost_estimate=cost(1e8, 8e6),
        name=name,
    )(core, own, got)


def send_xor(values, flip):
    count = lax.axis_size(BOTH)
    return lax.ppermute(values, BOTH, [(i, i ^ flip) for i in range(count)])


def add_kernel(place_ref, *refs):
    outs = place_ref.shape[0]
    terms, results = refs[:-outs], refs[-outs:]
    size = results[0].shape[0]
    for flip, result in enumerate(results):
        rows = pl.ds(pl.multiple_of(jnp.bitwise_xor(place_ref[0], flip) * size, size), size)
        total = terms[0][rows, :].astype(F32)
        for term in terms[1:]:
            total = total + term[rows, :].astype(F32)
        result[...] = total.astype(result.dtype)


def add_call(place, parts, terms, own_dtype):
    rows, lanes = terms[0].shape
    shape = (rows // parts, lanes)
    places = jnp.broadcast_to(place, (parts,)).astype(jnp.int32)
    return pl.pallas_call(
        add_kernel,
        grid=(1,),
        in_specs=[SMEM_SPEC] + [whole(a.shape) for a in terms],
        out_specs=[whole(shape)] * parts,
        out_shape=[jax.ShapeDtypeStruct(shape, own_dtype if p == 0 else BF16) for p in range(parts)],
        compiler_params=params(28),
        cost_estimate=cost(1e8, 4e6),
        name="add",
    )(places, *terms)


def join_kernel(place_ref, *refs):
    out_ref = refs[-1]
    for flip, ref in enumerate(refs[:-1]):
        size = ref.shape[0]
        rows = pl.ds(pl.multiple_of(jnp.bitwise_xor(place_ref[0], flip) * size, size), size)
        out_ref[rows, :] = ref[...]


def join_call(place, pieces):
    rows, lanes = pieces[0].shape
    shape = (rows * len(pieces), lanes)
    return pl.pallas_call(
        join_kernel,
        grid=(1,),
        in_specs=[SMEM_SPEC] + [whole(p.shape) for p in pieces],
        out_specs=whole(shape),
        out_shape=jax.ShapeDtypeStruct(shape, pieces[0].dtype),
        compiler_params=params(28),
        cost_estimate=cost(1e8, 2e6),
        name="join",
    )(place[None].astype(jnp.int32), *pieces)


def swap_parts(parts, shift):
    return [send_xor(part, (flip + 1) << shift) for flip, part in enumerate(parts)]


def spread(part, shift, parts):
    return [send_xor(part, flip << shift) for flip in range(1, parts)]


def after(values, *others):
    return lax.optimization_barrier((values,) + others)[0]


def row_device(
    tokens, seg_lengths, ln1_gain, ln1_bias, w_qkv, b_qv, w_o, b_o, ln2_gain, ln2_bias,
    w_up, b_up, w_down, b_down, cotangent,
):
    row_count, slice_len, d = tokens.shape
    row = lax.axis_index("blk")
    me = lax.axis_index("rows") * lax.axis_size("blk") + row
    place_core = me & 1
    place_plane = (me >> 1) & 3
    place_deep = me >> 3
    core = place_core[None].astype(jnp.int32)
    blk = row[None].astype(jnp.int32)
    ends = jnp.cumsum(seg_lengths, axis=1)
    ends = lax.dynamic_index_in_dim(ends, row, 0, keepdims=False).astype(jnp.int32)

    def cut(values):
        return [lax.dynamic_index_in_dim(values, row ^ flip, 0, keepdims=False) for flip in range(row_count)]

    def swap(pieces):
        return [pieces[0]] + swap_parts(pieces[1:], 0)

    x = swap(cut(tokens))
    cot = cut(cotangent)
    cot = lax.optimization_barrier(tuple(cot) + tuple(x))[:row_count]
    cot = swap(list(cot))
    x, q, k, v, n1, att, lse = forward_call(ends, blk, x, ln1_gain, ln1_bias, w_qkv, b_qv)
    out, gmid, gatt, delta, keep, send, vec_mid = middle_call(
        core, blk, att, x, cot, w_o, b_o, ln2_gain, ln2_bias, w_up, b_up, w_down, b_down
    )

    def home(values):
        return lax.all_to_all(values.reshape(tokens.shape), "blk", 0, 0, tiled=True)

    own, *parts = add_call(place_plane, 4, [keep, send_xor(send, 1)], F32)
    grads = backward_call(after(ends, own), q, k, v, gatt, lse, delta, 0, d // LANES)
    own, *parts = add_call(after(place_deep, grads[0]), 4, [own] + swap_parts(parts, 1), F32)
    first = [own] + swap_parts(parts, 3)
    gin, keep, send = last_call(after(core, own), grads, n1, x, gmid, ln1_gain, w_qkv, vec_mid)
    output = home(after(out, send))
    (first,) = add_call(0, 1, first, BF16)
    send, first = lax.optimization_barrier((send, first))
    first_z = spread(first, 3, 2)
    own, *parts = add_call(place_plane, 4, [keep, send_xor(send, 1)], F32)
    first = join_call(after(place_deep & 1, own), [first] + first_z)
    first_z = spread(first, 4, 2)
    second = swap_parts(parts, 1)
    own, *parts = add_call(place_deep, 4, [own] + second, F32)
    first = join_call(place_deep >> 1, [first] + first_z)
    first, gin, output = lax.optimization_barrier((first, gin, output, own))[:3]
    gin = home(gin)
    (second,) = add_call(0, 1, [own] + swap_parts(parts, 3), BF16)
    first = join_call(after(place_plane & 1, second), [first] + spread(first, 1, 2))
    second = join_call(after(place_deep, gin), [second] + spread(second, 3, 4))
    first = join_call(after(place_plane >> 1, second), [first] + spread(first, 2, 2))
    order, output, gin = lax.optimization_barrier((core, output, gin, second))[:3]
    output = copy_call(order, output, BF16)
    input_grad = copy_call(order, gin, F32)
    second = join_call(after(place_plane, output, input_grad), [second] + spread(second, 1, 4))
    gw_down, gw_up, gw_o = finish_call(
        finish_mid_kernel, core, first, send_xor(first, 1), [w_down.shape, w_up.shape, w_o.shape], "finish_mid"
    )
    gw_qkv, *vecs = finish_call(
        finish_last_kernel, after(core, gw_down), second, send_xor(second, 1),
        [w_qkv.shape] + [(1, size) for size in (d, 2 * d, d, d, d, d, d, 2 * d)], "finish_last",
    )
    vecs = [vec.reshape(-1) for vec in vecs]
    g_down_b, g_up_b, g_ln2_gain, g_ln2_bias, g_o_b, g_ln1_gain, g_ln1_bias, g_qv_b = vecs
    return (
        output, input_grad, g_ln1_gain, g_ln1_bias, gw_qkv, g_qv_b, gw_o, g_o_b, g_ln2_gain, g_ln2_bias,
        gw_up, g_up_b, gw_down, g_down_b,
    )


def layer_norm(values, gain_vec, bias_vec):
    average = jnp.mean(values, axis=-1, keepdims=True)
    centered = values - average
    variance = jnp.mean(centered * centered, axis=-1, keepdims=True)
    return centered * lax.rsqrt(variance + norm_eps) * gain_vec + bias_vec


def segment_of(cell_ends, positions):
    return jnp.sum((cell_ends[:, None, :] <= positions[None, :, None]).astype(jnp.int32), axis=-1)


def block_scores(query_heads, key_heads, query_pos, key_pos, query_seg, key_seg, scale_qk):
    raw_scores = (
        jnp.einsum("rqhd,rkhd->rqhk", query_heads, key_heads, preferred_element_type=jnp.float32)
        * scale_qk
    )
    causal = key_pos[None, :] <= query_pos[:, None]
    same_cell = query_seg[:, :, None] == key_seg[:, None, :]
    allowed = (causal[None] & same_cell)[:, :, None, :]
    return (jnp.where(allowed, raw_scores, neg_big), allowed)


def block_active(query_pos, key_pos, query_seg, key_seg):
    return (key_pos[0] <= query_pos[-1]) & jnp.any(key_seg[:, -1] >= query_seg[:, 0])


def backward_block(
    query_heads,
    grad_heads,
    log_total,
    delta_sum,
    key_heads,
    value_heads,
    query_pos,
    key_pos,
    query_seg,
    key_seg,
    scale_qk,
):
    scores, allowed = block_scores(
        query_heads, key_heads, query_pos, key_pos, query_seg, key_seg, scale_qk
    )
    softmaxed = jnp.where(allowed, jnp.exp(scores - log_total[..., None]), 0.0)
    grad_probs = jnp.einsum(
        "rqhd,rkhd->rqhk", grad_heads, value_heads, preferred_element_type=jnp.float32
    )
    grad_scores = (softmaxed * (grad_probs - delta_sum[..., None])).astype(jnp.bfloat16)
    grad_query = (
        jnp.einsum("rqhk,rkhd->rqhd", grad_scores, key_heads, preferred_element_type=jnp.float32)
        * scale_qk
    )
    grad_key = (
        jnp.einsum("rqhk,rqhd->rkhd", grad_scores, query_heads, preferred_element_type=jnp.float32)
        * scale_qk
    )
    grad_value = jnp.einsum(
        "rqhk,rqhd->rkhd",
        softmaxed.astype(jnp.bfloat16),
        grad_heads,
        preferred_element_type=jnp.float32,
    )
    return (grad_query, grad_key, grad_value)


def unchanged(old_state):
    return old_state


def general_device(
    tokens,
    seg_lengths,
    ln1_gain,
    ln1_bias,
    w_qkv,
    b_qv,
    w_o,
    b_o,
    ln2_gain,
    ln2_bias,
    w_up,
    b_up,
    w_down,
    b_down,
    cotangent,
):
    row_count, slice_len, width_all = tokens.shape
    head_size = width_all // HEADS
    scale_qk = head_size ** (-0.5)
    head_shape = (row_count, slice_len, HEADS, head_size)
    stat_shape = (row_count, slice_len, HEADS)
    full_length = lax.axis_size("blk") * slice_len
    offsets = jnp.arange(slice_len, dtype=jnp.int32)
    query_pos = lax.axis_index("blk") * slice_len + offsets
    cell_ends = jnp.cumsum(seg_lengths, axis=1)
    query_seg = segment_of(cell_ends, query_pos)

    def take_block(piece, block_index):
        return lax.dynamic_slice_in_dim(piece, block_index * slice_len, slice_len, 1).reshape(
            head_shape
        )

    inputs = tokens.astype(jnp.float32)
    normed_val, first_pull = jax.vjp(layer_norm, inputs, ln1_gain, ln1_bias)
    normed_one = normed_val.astype(jnp.bfloat16)
    projected = jnp.dot(normed_one, w_qkv, preferred_element_type=jnp.float32)
    query_b = (projected[..., :width_all] + b_qv[:width_all]).astype(jnp.bfloat16)
    key_b = projected[..., width_all : 2 * width_all].astype(jnp.bfloat16)
    value_b = (projected[..., 2 * width_all :] + b_qv[width_all:]).astype(jnp.bfloat16)
    query_heads = query_b.reshape(head_shape)
    start_state = (
        jnp.full(stat_shape, neg_big, jnp.float32),
        jnp.zeros(stat_shape, jnp.float32),
        jnp.zeros(head_shape, jnp.float32),
    )
    key_piece = lax.all_gather(key_b, "blk", axis=1, tiled=True)
    value_piece = lax.all_gather(value_b, "blk", axis=1, tiled=True)

    def forward_block_step(block_index, inner_state):
        key_pos = block_index * slice_len + offsets
        key_seg = segment_of(cell_ends, key_pos)
        key_heads = take_block(key_piece, block_index)
        value_heads = take_block(value_piece, block_index)

        def forward_update(old_state):
            running_top, running_total, running_sum = old_state
            scores, allowed = block_scores(
                query_heads, key_heads, query_pos, key_pos, query_seg, key_seg, scale_qk
            )
            new_top = jnp.maximum(running_top, jnp.max(scores, axis=-1))
            factor = jnp.exp(running_top - new_top)
            weights_now = jnp.where(allowed, jnp.exp(scores - new_top[..., None]), 0.0)
            new_total = running_total * factor + jnp.sum(weights_now, axis=-1)
            new_sum = running_sum * factor[..., None] + jnp.einsum(
                "rqhk,rkhd->rqhd",
                weights_now.astype(jnp.bfloat16),
                value_heads,
                preferred_element_type=jnp.float32,
            )
            return (new_top, new_total, new_sum)

        return lax.cond(
            block_active(query_pos, key_pos, query_seg, key_seg),
            forward_update,
            unchanged,
            inner_state,
        )

    running_top, running_total, running_sum = lax.fori_loop(
        0, key_piece.shape[1] // slice_len, forward_block_step, start_state
    )
    attn_f32 = (running_sum / running_total[..., None]).reshape(row_count, slice_len, width_all)
    log_total = running_top + jnp.log(running_total)
    attn_b = attn_f32.astype(jnp.bfloat16)
    middle = inputs + jnp.dot(attn_b, w_o, preferred_element_type=jnp.float32) + b_o
    normed_two_val, second_pull = jax.vjp(layer_norm, middle, ln2_gain, ln2_bias)
    normed_two = normed_two_val.astype(jnp.bfloat16)
    hidden_pre = jnp.dot(normed_two, w_up, preferred_element_type=jnp.float32) + b_up
    hidden_val, gelu_pull = jax.vjp(jax.nn.gelu, hidden_pre)
    hidden_b = hidden_val.astype(jnp.bfloat16)
    output = (
        middle + jnp.dot(hidden_b, w_down, preferred_element_type=jnp.float32) + b_down
    ).astype(jnp.bfloat16)
    grad_out = cotangent.astype(jnp.float32)
    grad_w_down = jnp.einsum("rcf,rcd->fd", hidden_b, cotangent, preferred_element_type=jnp.float32)
    grad_b_down = jnp.sum(grad_out, axis=(0, 1))
    grad_hidden = jnp.einsum("rcd,fd->rcf", cotangent, w_down, preferred_element_type=jnp.float32)
    (grad_pre,) = gelu_pull(grad_hidden)
    grad_pre_b = grad_pre.astype(jnp.bfloat16)
    grad_w_up = jnp.einsum(
        "rcd,rcf->df", normed_two, grad_pre_b, preferred_element_type=jnp.float32
    )
    grad_b_up = jnp.sum(grad_pre_b.astype(jnp.float32), axis=(0, 1))
    grad_normed_two = jnp.einsum(
        "rcf,df->rcd", grad_pre_b, w_up, preferred_element_type=jnp.float32
    )
    grad_mid_norm, grad_ln2_gain, grad_ln2_bias = second_pull(grad_normed_two)
    grad_middle = grad_out + grad_mid_norm
    grad_branch_b = grad_middle.astype(jnp.bfloat16)
    grad_w_o = jnp.einsum("rce,rcd->ed", attn_b, grad_branch_b, preferred_element_type=jnp.float32)
    grad_b_o = jnp.sum(grad_branch_b.astype(jnp.float32), axis=(0, 1))
    grad_attn_b = jnp.einsum(
        "rcd,ed->rce", grad_branch_b, w_o, preferred_element_type=jnp.float32
    ).astype(jnp.bfloat16)
    delta_sum = jnp.sum((grad_attn_b.astype(jnp.float32) * attn_f32).reshape(head_shape), axis=-1)
    grad_heads = grad_attn_b.reshape(head_shape)
    whole_shape = (row_count, full_length, HEADS, head_size)
    back_state = (
        jnp.zeros(head_shape, jnp.float32),
        jnp.zeros(whole_shape, jnp.float32),
        jnp.zeros(whole_shape, jnp.float32),
    )
    backward_key_piece = lax.all_gather(key_b, "blk", axis=1, tiled=True)
    backward_value_piece = lax.all_gather(value_b, "blk", axis=1, tiled=True)

    def backward_block_step(block_index, inner_state):
        key_pos = block_index * slice_len + offsets
        key_seg = segment_of(cell_ends, key_pos)
        key_heads = take_block(backward_key_piece, block_index)
        value_heads = take_block(backward_value_piece, block_index)

        def backward_update(old_state):
            grad_query, grad_key, grad_value = backward_block(
                query_heads,
                grad_heads,
                log_total,
                delta_sum,
                key_heads,
                value_heads,
                query_pos,
                key_pos,
                query_seg,
                key_seg,
                scale_qk,
            )
            at_row = block_index * slice_len
            return (
                old_state[0] + grad_query,
                lax.dynamic_update_slice_in_dim(old_state[1], grad_key, at_row, 1),
                lax.dynamic_update_slice_in_dim(old_state[2], grad_value, at_row, 1),
            )

        return lax.cond(
            block_active(query_pos, key_pos, query_seg, key_seg),
            backward_update,
            unchanged,
            inner_state,
        )

    back_result = lax.fori_loop(
        0, backward_key_piece.shape[1] // slice_len, backward_block_step, back_state
    )
    grad_query_sum = back_result[0]
    grad_key_sum, grad_value_sum = (
        lax.psum_scatter(
            back_result[1].astype(jnp.bfloat16), "blk", scatter_dimension=1, tiled=True
        ).astype(jnp.float32),
        lax.psum_scatter(
            back_result[2].astype(jnp.bfloat16), "blk", scatter_dimension=1, tiled=True
        ).astype(jnp.float32),
    )
    flat_shape = (row_count, slice_len, width_all)
    grad_qkv_b = jnp.concatenate(
        [
            grad_query_sum.reshape(flat_shape),
            grad_key_sum.reshape(flat_shape),
            grad_value_sum.reshape(flat_shape),
        ],
        axis=-1,
    ).astype(jnp.bfloat16)
    grad_w_qkv = jnp.einsum(
        "rcd,rce->de", normed_one, grad_qkv_b, preferred_element_type=jnp.float32
    )
    column_sums = jnp.sum(grad_qkv_b.astype(jnp.float32), axis=(0, 1))
    grad_b_qv = jnp.concatenate([column_sums[:width_all], column_sums[2 * width_all :]])
    grad_normed_one = jnp.einsum(
        "rce,de->rcd", grad_qkv_b, w_qkv, preferred_element_type=jnp.float32
    )
    grad_in_norm, grad_ln1_gain, grad_ln1_bias = first_pull(grad_normed_one)
    input_grad = grad_middle + grad_in_norm
    grads = (
        grad_ln1_gain,
        grad_ln1_bias,
        grad_w_qkv,
        grad_b_qv,
        grad_w_o,
        grad_b_o,
        grad_ln2_gain,
        grad_ln2_bias,
        grad_w_up,
        grad_b_up,
        grad_w_down,
        grad_b_down,
    )
    summed = lax.psum(
        (
            grads[0],
            grads[1],
            grads[2],
            grads[3],
            grads[4],
            grads[5],
            grads[6],
            grads[7],
            grads[8],
            grads[9],
            grads[10],
            grads[11],
        ),
        ("rows", "blk"),
    )
    return (
        output,
        input_grad,
        summed[0],
        summed[1],
        summed[2],
        summed[3],
        summed[4],
        summed[5],
        summed[6],
        summed[7],
        summed[8],
        summed[9],
        summed[10],
        summed[11],
    )


def device_function(tokens, *rest):
    d = tokens.shape[2]
    whole_rows = (
        lax.axis_size("blk") == tokens.shape[0] == 4
        and lax.axis_size("rows") == 8
        and tokens.shape[1] == TILE
        and d == 512
    )
    return (row_device if whole_rows else general_device)(tokens, *rest)


def solution(mesh):
    in_specs = (
        P("rows", "blk", None),
        P("rows", None),
        P(),
        P(),
        P(),
        P(),
        P(),
        P(),
        P(),
        P(),
        P(),
        P(),
        P(),
        P(),
        P("rows", "blk", None),
    )
    out_specs = (
        P("rows", "blk", None),
        P("rows", "blk", None),
        P(),
        P(),
        P(),
        P(),
        P(),
        P(),
        P(),
        P(),
        P(),
        P(),
        P(),
        P(),
    )
    return jax.shard_map(
        device_function, mesh=mesh, in_specs=in_specs, out_specs=out_specs, check_vma=False
    )
```

profile of v0, /device:TPU:1, one launch (start us, length us, event | category | flops | bytes accessed | tf_op | source)
XLA Modules:
  0.0 163.1 jit_solution(14053253196348989197)
XLA Ops:
  2.2 2.7 %collective-permute-start.1 = (bf16[256,512]{1,0:T(8,128)(2,1)S(1)}, bf16[256,512]{1,0:T(8,128)(2,1)S(1)}, u32[]{:S(2)}, u32[]{:S(2)}) collective-permute-start(bf16[256,512]{1,0:T(8,128)(2,1)S(1)} %get-tuple-element.161), channel_id=1, source_target_pairs={{0,2},{1,3},{2,0},{3,1},{4,6},{5,7},{6,4},{7,5},{8,10},{9,11},{10,... | collective-permute-start | bytes 786440 | tf_op jit(solution)/shard_map/ppermute | solution.py:508
  6.4 5.1 %collective-permute-done.1.x2_ref = bf16[256,512]{1,0:T(8,128)(2,1)S(1)} collective-permute-done((bf16[256,512]{1,0:T(8,128)(2,1)S(1)}, bf16[256,512]{1,0:T(8,128)(2,1)S(1)}, u32[]{:S(2)}, u32[]{:S(2)}) %collective-permute-start.1) | collective-permute-done | bytes 262176 | tf_op jit(solution)/shard_map/ppermute | solution.py:508
  11.5 5.6 %collective-permute-done.2.x3_ref = bf16[256,512]{1,0:T(8,128)(2,1)S(1)} collective-permute-done((bf16[256,512]{1,0:T(8,128)(2,1)S(1)}, bf16[256,512]{1,0:T(8,128)(2,1)S(1)}, u32[]{:S(2)}, u32[]{:S(2)}) %collective-permute-start.2) | collective-permute-done | bytes 262176 | tf_op jit(solution)/shard_map/ppermute | solution.py:508
  19.4 14.3 %forward.1 = (bf16[1024,512]{1,0:T(8,128)(2,1)S(1)}, bf16[4,1024,128]{2,1,0:T(8,128)(2,1)}, bf16[4,1024,128]{2,1,0:T(8,128)(2,1)}, bf16[4,1024,128]{2,1,0:T(8,12...) custom-call(s32[8]{0:T(128)S(1)} %fusion.ends_ref, s32[1]{0:T(128)} %bitcast.3.blk_ref, ...), custom_call_target="tpu_custom_call" | custom-call | flops 20000000000 | bytes 10000000 | tf_op jit(solution)/shard_map/forward/pallas_call | solution.py:161
  33.8 13.7 %middle.1 = (bf16[1024,512]{1,0:T(8,128)(2,1)}, f32[1024,512]{1,0:T(8,128)}, bf16[4,1024,128]{2,1,0:T(8,128)(2,1)}, f32[8,1024]{1,0:T(8,128)S(1)}, f32[1280,512]...) custom-call(s32[1]{0:T(128)} %bitcast.core_ref.refs_0_.order_ref, s32[1]{0:T(128)} %bitcast.3.blk_ref, ...), custom_call_target="tpu_custom_call" | custom-call | flops 15000000512 | bytes 20000000 | tf_op jit(solution)/shard_map/middle/pallas_call | solution.py:268
  47.6 3.3 %collective-permute-done.6.refs_1_ = bf16[1280,512]{1,0:T(8,128)(2,1)} collective-permute-done((bf16[1280,512]{1,0:T(8,128)(2,1)}, bf16[1280,512]{1,0:T(8,128)(2,1)}, u32[]{:S(2)}, u32[]{:S(2)}) %collective-permute-start.6) | collective-permute-done | bytes 1310752 | tf_op jit(solution)/shard_map/ppermute | solution.py:508
  50.9 1.5 add.33
  52.5 1.5 collective-permute-start.7
  55.2 17.1 %backward.1 = (bf16[4,1024,128]{2,1,0:T(8,128)(2,1)}, bf16[4,1024,128]{2,1,0:T(8,128)(2,1)}, bf16[4,1024,128]{2,1,0:T(8,128)(2,1)}) custom-call(s32[8]{0:T(128)S(1)} %fusion.ends_ref, bf16[4,1024,128]{2,1,0:T(8,128)(2,1)} %get-tuple-element.94.q_ref, bf16[4,1024,128]{2,1,0:T(8,128)(2,1)} %get-tuple-element.95.k_ref, ...), custom_call_target="tpu_custom_call" | custom-call | flops 4000000000 | bytes 400000 | tf_op jit(solution)/shard_map/backward/pallas_call | solution.py:360
  73.1 1.5 collective-permute-start.10
  74.5 2.3 %collective-permute-start.11 = (bf16[80,512]{1,0:T(8,128)(2,1)S(1)}, bf16[80,512]{1,0:T(8,128)(2,1)S(1)}, u32[]{:S(2)}, u32[]{:S(2)}) collective-permute-start(bf16[80,512]{1,0:T(8,128)(2,1)S(1)} %get-tuple-element.115), channel_id=1, source_target_pairs={{0,16},{1,17},{2,18},{3,19},{4,20},{5,21},{6,22},{7,23},{8,24},{9,... | collective-permute-start | bytes 245768 | tf_op jit(solution)/shard_map/ppermute | solution.py:508
  76.9 7.6 %last.1 = (bf16[1024,512]{1,0:T(8,128)(2,1)}, f32[3200,128]{1,0:T(8,128)S(1)}, bf16[3200,128]{1,0:T(8,128)(2,1)}) custom-call(s32[1]{0:T(128)} %bitcast.core_ref.refs_0_.order_ref, bf16[4,1024,128]{2,1,0:T(8,128)(2,1)} %get-tuple-element.100.refs_1_, bf16[4,1024,128]{2,1,0:T(8,128)(2,1)} %get-tuple-element.107.refs_2_, ...), custom_call_target="tpu_custom_call" | custom-call | flops 1000000000 | bytes 100000 | tf_op jit(solution)/shard_map/last/pallas_call | solution.py:411
  85.2 1.6 collective-permute-start.13
  86.8 3.5 %all-to-all-start = ((bf16[4,256,512]{2,1,0:T(8,128)(2,1)}), bf16[4,256,512]{2,1,0:T(8,128)(2,1)S(1)}, u32[]{:S(2)}, u32[]{:S(2)}) async-start(bf16[4,256,512]{2,1,0:T(8,128)(2,1)} %bitcast.53), calls=%async_computation | async-start | bytes 2097152 | tf_op jit(solution)/shard_map/all_to_all | solution.py:605
  90.9 1.4 add.36
  97.5 3.3 %collective-permute-start.15 = (bf16[160,512]{1,0:T(8,128)(2,1)S(1)}, bf16[160,512]{1,0:T(8,128)(2,1)S(1)}, u32[]{:S(2)}, u32[]{:S(2)}) collective-permute-start(bf16[160,512]{1,0:T(8,128)(2,1)S(1)} %join.6.refs_0_), channel_id=1, source_target_pairs={{0,16},{1,17},{2,18},{3,19},{4,20},{5,21},{6,22},{7,23},{8,24},{9,... | collective-permute-start | bytes 491528 | tf_op jit(solution)/shard_map/ppermute | solution.py:508
  100.8 8.0 %collective-permute-done.15.refs_1_ = bf16[160,512]{1,0:T(8,128)(2,1)S(1)} collective-permute-done((bf16[160,512]{1,0:T(8,128)(2,1)S(1)}, bf16[160,512]{1,0:T(8,128)(2,1)S(1)}, u32[]{:S(2)}, u32[]{:S(2)}) %collective-permute-start.15) | collective-permute-done | bytes 163872 | tf_op jit(solution)/shard_map/ppermute | solution.py:508
  108.8 3.9 %collective-permute-done.16.refs_1_ = bf16[800,128]{1,0:T(8,128)(2,1)S(1)} collective-permute-done((bf16[800,128]{1,0:T(8,128)(2,1)}, bf16[800,128]{1,0:T(8,128)(2,1)S(1)}, u32[]{:S(2)}, u32[]{:S(2)}) %collective-permute-start.16) | collective-permute-done | bytes 204832 | tf_op jit(solution)/shard_map/ppermute | solution.py:508
  114.7 4.4 %all-to-all-start.1 = ((bf16[4,256,512]{2,1,0:T(8,128)(2,1)}), bf16[4,256,512]{2,1,0:T(8,128)(2,1)S(1)}, u32[]{:S(2)}, u32[]{:S(2)}) async-start(bf16[4,256,512]{2,1,0:T(8,128)(2,1)} %bitcast.54), calls=%async_computation.1 | async-start | bytes 2097152 | tf_op jit(solution)/shard_map/all_to_all | solution.py:605
  119.7 3.2 %collective-permute-start.20 = (bf16[200,128]{1,0:T(8,128)(2,1)S(1)}, bf16[200,128]{1,0:T(8,128)(2,1)S(1)}, u32[]{:S(2)}, u32[]{:S(2)}) collective-permute-start(bf16[200,128]{1,0:T(8,128)(2,1)S(1)} %get-tuple-element.132), channel_id=1, source_target_pairs={{0,16},{1,17},{2,18},{3,19},{4,20},{5,21},{6,22},{7,23},{8,24},{9,... | collective-permute-start | bytes 153608 | tf_op jit(solution)/shard_map/ppermute | solution.py:508
  122.9 2.0 %collective-permute-done.20.refs_2_ = bf16[200,128]{1,0:T(8,128)(2,1)S(1)} collective-permute-done((bf16[200,128]{1,0:T(8,128)(2,1)S(1)}, bf16[200,128]{1,0:T(8,128)(2,1)S(1)}, u32[]{:S(2)}, u32[]{:S(2)}) %collective-permute-start.20) | collective-permute-done | bytes 51232 | tf_op jit(solution)/shard_map/ppermute | solution.py:508
  124.9 2.8 %collective-permute-done.21.refs_3_ = bf16[200,128]{1,0:T(8,128)(2,1)S(1)} collective-permute-done((bf16[200,128]{1,0:T(8,128)(2,1)S(1)}, bf16[200,128]{1,0:T(8,128)(2,1)S(1)}, u32[]{:S(2)}, u32[]{:S(2)}) %collective-permute-start.21) | collective-permute-done | bytes 51232 | tf_op jit(solution)/shard_map/ppermute | solution.py:508
  130.4 2.1 %collective-permute-start.24 = (bf16[200,128]{1,0:T(8,128)(2,1)S(1)}, bf16[200,128]{1,0:T(8,128)(2,1)}, u32[]{:S(2)}, u32[]{:S(2)}) collective-permute-start(bf16[200,128]{1,0:T(8,128)(2,1)S(1)} %add.38.refs_0_), channel_id=1, source_target_pairs={{0,24},{1,25},{2,26},{3,27},{4,28},{5,29},{6,30},{7,31},{8,16},{9,... | collective-permute-start | bytes 153608 | tf_op jit(solution)/shard_map/ppermute | solution.py:508
  132.6 1.5 all-to-all-done.1.in_ref
  134.1 1.5 collective-permute-done.24.refs_3_
  136.4 5.8 %collective-permute-done.26.refs_1_ = bf16[640,512]{1,0:T(8,128)(2,1)S(1)} collective-permute-done((bf16[640,512]{1,0:T(8,128)(2,1)S(1)}, bf16[640,512]{1,0:T(8,128)(2,1)S(1)}, u32[]{:S(2)}, u32[]{:S(2)}) %collective-permute-start.26) | collective-permute-done | bytes 655392 | tf_op jit(solution)/shard_map/ppermute | solution.py:508
  142.4 2.7 %collective-permute-start.27 = (bf16[1280,512]{1,0:T(8,128)(2,1)S(1)}, bf16[1280,512]{1,0:T(8,128)(2,1)S(1)}, u32[]{:S(2)}, u32[]{:S(2)}) collective-permute-start(bf16[1280,512]{1,0:T(8,128)(2,1)S(1)} %join.10.own_ref), channel_id=1, source_target_pairs={{0,1},{1,0},{2,3},{3,2},{4,5},{5,4},{6,7},{7,6},{8,9},{9,8},{10,11... | collective-permute-start | bytes 3932168 | tf_op jit(solution)/shard_map/ppermute | solution.py:508
  147.8 1.8 %copy.32 = f32[4,256,512]{2,1,0:T(8,128)} custom-call(s32[1]{0:T(128)} %bitcast.core_ref.refs_0_.order_ref, bf16[4,256,512]{2,1,0:T(8,128)(2,1)S(1)} %all-to-all-done.1.in_ref), custom_call_target="tpu_custom_call" | custom-call | flops 10000000 | bytes 100000 | tf_op jit(solution)/shard_map/copy/pallas_call | solution.py:462
  149.6 1.5 copy.31
  152.9 4.2 %collective-permute-done.30.refs_3_ = bf16[800,128]{1,0:T(8,128)(2,1)S(1)} collective-permute-done((bf16[800,128]{1,0:T(8,128)(2,1)S(1)}, bf16[800,128]{1,0:T(8,128)(2,1)S(1)}, u32[]{:S(2)}, u32[]{:S(2)}) %collective-permute-start.30) | collective-permute-done | bytes 204832 | tf_op jit(solution)/shard_map/ppermute | solution.py:508
  158.3 2.7 %finish_mid.1 = (f32[1024,512]{1,0:T(8,128)}, f32[512,1024]{1,0:T(8,128)}, f32[512,512]{1,0:T(8,128)}) custom-call(s32[1]{0:T(128)} %bitcast.core_ref.refs_0_.order_ref, bf16[1280,512]{1,0:T(8,128)(2,1)S(1)} %join.10.own_ref, bf16[1280,512]{1,0:T(8,128)(2,1)S(1)} %collective-permute-done.27.got_ref), custom_call_target="tpu_custom_call" | custom-call | flops 100000000 | bytes 8000000 | tf_op jit(solution)/shard_map/finish_mid/pallas_call | solution.py:494
  161.0 2.1 %finish_last.1 = (f32[512,1536]{1,0:T(8,128)}, f32[1,512]{1,0:T(1,128)}, f32[1,1024]{1,0:T(1,128)}, f32[1,512]{1,0:T(1,128)}, f32[1,512]{1,0:T(1,128)}, /*index=...) custom-call(s32[1]{0:T(128)} %bitcast.core_ref.refs_0_.order_ref, ...), custom_call_target="tpu_custom_call" | custom-call | flops 100000000 | bytes 8000000 | tf_op jit(solution)/shard_map/finish_last/pallas_call | solution.py:494
  (107 shorter events, 25.8 us)
Async XLA Ops:
  2.1 4.3 %collective-permute-start = (bf16[256,512]{1,0:T(8,128)(2,1)S(1)}, bf16[256,512]{1,0:T(8,128)(2,1)S(1)}, u32[]{:S(2)}, u32[]{:S(2)}) collective-permute-start(bf16[256,512]{1,0:T(8,128)(2,1)S(1)} %get-tuple-element.159), channel_id=1, source_target_pairs={{0,1},{1,0},{2,3},{3,2},{4,5},{5,4},{6,7},{7,6},{8,9},{9,8},{10,11... | collective-permute-start | bytes 786440 | tf_op jit(solution)/shard_map/ppermute | solution.py:508
  2.2 9.3 %collective-permute-start.1 = (bf16[256,512]{1,0:T(8,128)(2,1)S(1)}, bf16[256,512]{1,0:T(8,128)(2,1)S(1)}, u32[]{:S(2)}, u32[]{:S(2)}) collective-permute-start(bf16[256,512]{1,0:T(8,128)(2,1)S(1)} %get-tuple-element.161), channel_id=1, source_target_pairs={{0,2},{1,3},{2,0},{3,1},{4,6},{5,7},{6,4},{7,5},{8,10},{9,11},{10,... | collective-permute-start | bytes 786440 | tf_op jit(solution)/shard_map/ppermute | solution.py:508
  4.9 12.2 %collective-permute-start.2 = (bf16[256,512]{1,0:T(8,128)(2,1)S(1)}, bf16[256,512]{1,0:T(8,128)(2,1)S(1)}, u32[]{:S(2)}, u32[]{:S(2)}) collective-permute-start(bf16[256,512]{1,0:T(8,128)(2,1)S(1)} %get-tuple-element.158), channel_id=1, source_target_pairs={{0,3},{1,2},{2,1},{3,0},{4,7},{5,6},{6,5},{7,4},{8,11},{9,10},{10,... | collective-permute-start | bytes 786440 | tf_op jit(solution)/shard_map/ppermute | solution.py:508
  17.1 16.6 %collective-permute-start.3 = (bf16[256,512]{1,0:T(8,128)(2,1)S(1)}, bf16[256,512]{1,0:T(8,128)(2,1)S(1)}, u32[]{:S(2)}, u32[]{:S(2)}) collective-permute-start(bf16[256,512]{1,0:T(8,128)(2,1)S(1)} %get-tuple-element.87), channel_id=1, source_target_pairs={{0,1},{1,0},{2,3},{3,2},{4,5},{5,4},{6,7},{7,6},{8,9},{9,8},{10,11... | collective-permute-start | bytes 786440 | tf_op jit(solution)/shard_map/ppermute | solution.py:508
  17.5 16.2 %collective-permute-start.4 = (bf16[256,512]{1,0:T(8,128)(2,1)S(1)}, bf16[256,512]{1,0:T(8,128)(2,1)S(1)}, u32[]{:S(2)}, u32[]{:S(2)}) collective-permute-start(bf16[256,512]{1,0:T(8,128)(2,1)S(1)} %get-tuple-element.88), channel_id=1, source_target_pairs={{0,2},{1,3},{2,0},{3,1},{4,6},{5,7},{6,4},{7,5},{8,10},{9,11},{10,... | collective-permute-start | bytes 786440 | tf_op jit(solution)/shard_map/ppermute | solution.py:508
  18.8 14.9 %collective-permute-start.5 = (bf16[256,512]{1,0:T(8,128)(2,1)S(1)}, bf16[256,512]{1,0:T(8,128)(2,1)S(1)}, u32[]{:S(2)}, u32[]{:S(2)}) collective-permute-start(bf16[256,512]{1,0:T(8,128)(2,1)S(1)} %get-tuple-element.89), channel_id=1, source_target_pairs={{0,3},{1,2},{2,1},{3,0},{4,7},{5,6},{6,5},{7,4},{8,11},{9,10},{10,... | collective-permute-start | bytes 786440 | tf_op jit(solution)/shard_map/ppermute | solution.py:508
  52.5 19.8 %collective-permute-start.7 = (bf16[320,512]{1,0:T(8,128)(2,1)S(1)}, bf16[320,512]{1,0:T(8,128)(2,1)S(1)}, u32[]{:S(2)}, u32[]{:S(2)}) collective-permute-start(bf16[320,512]{1,0:T(8,128)(2,1)S(1)} %get-tuple-element.102), channel_id=1, source_target_pairs={{0,2},{1,3},{2,0},{3,1},{4,6},{5,7},{6,4},{7,5},{8,10},{9,11},{10,... | collective-permute-start | bytes 983048 | tf_op jit(solution)/shard_map/ppermute | solution.py:508
  53.9 18.4 %collective-permute-start.8 = (bf16[320,512]{1,0:T(8,128)(2,1)S(1)}, bf16[320,512]{1,0:T(8,128)(2,1)S(1)}, u32[]{:S(2)}, u32[]{:S(2)}) collective-permute-start(bf16[320,512]{1,0:T(8,128)(2,1)S(1)} %get-tuple-element.103), channel_id=1, source_target_pairs={{0,4},{1,5},{2,6},{3,7},{4,0},{5,1},{6,2},{7,3},{8,12},{9,13},{10,... | collective-permute-start | bytes 983048 | tf_op jit(solution)/shard_map/ppermute | solution.py:508
  55.2 17.2 %collective-permute-start.9 = (bf16[320,512]{1,0:T(8,128)(2,1)S(1)}, bf16[320,512]{1,0:T(8,128)(2,1)S(1)}, u32[]{:S(2)}, u32[]{:S(2)}) collective-permute-start(bf16[320,512]{1,0:T(8,128)(2,1)S(1)} %get-tuple-element.104), channel_id=1, source_target_pairs={{0,6},{1,7},{2,4},{3,5},{4,2},{5,3},{6,0},{7,1},{8,14},{9,15},{10,... | collective-permute-start | bytes 983048 | tf_op jit(solution)/shard_map/ppermute | solution.py:508
  73.1 11.4 %collective-permute-start.10 = (bf16[80,512]{1,0:T(8,128)(2,1)S(1)}, bf16[80,512]{1,0:T(8,128)(2,1)S(1)}, u32[]{:S(2)}, u32[]{:S(2)}) collective-permute-start(bf16[80,512]{1,0:T(8,128)(2,1)S(1)} %get-tuple-element.114), channel_id=1, source_target_pairs={{0,8},{1,9},{2,10},{3,11},{4,12},{5,13},{6,14},{7,15},{8,0},{9,1},... | collective-permute-start | bytes 245768 | tf_op jit(solution)/shard_map/ppermute | solution.py:508
  74.5 9.9 %collective-permute-start.11 = (bf16[80,512]{1,0:T(8,128)(2,1)S(1)}, bf16[80,512]{1,0:T(8,128)(2,1)S(1)}, u32[]{:S(2)}, u32[]{:S(2)}) collective-permute-start(bf16[80,512]{1,0:T(8,128)(2,1)S(1)} %get-tuple-element.115), channel_id=1, source_target_pairs={{0,16},{1,17},{2,18},{3,19},{4,20},{5,21},{6,22},{7,23},{8,24},{9,... | collective-permute-start | bytes 245768 | tf_op jit(solution)/shard_map/ppermute | solution.py:508
  76.9 7.6 %collective-permute-start.12 = (bf16[80,512]{1,0:T(8,128)(2,1)S(1)}, bf16[80,512]{1,0:T(8,128)(2,1)S(1)}, u32[]{:S(2)}, u32[]{:S(2)}) collective-permute-start(bf16[80,512]{1,0:T(8,128)(2,1)S(1)} %get-tuple-element.116), channel_id=1, source_target_pairs={{0,24},{1,25},{2,26},{3,27},{4,28},{5,29},{6,30},{7,31},{8,16},{9,... | collective-permute-start | bytes 245768 | tf_op jit(solution)/shard_map/ppermute | solution.py:508
  85.2 5.7 %collective-permute-start.13 = (bf16[3200,128]{1,0:T(8,128)(2,1)}, bf16[3200,128]{1,0:T(8,128)(2,1)S(1)}, u32[]{:S(2)}, u32[]{:S(2)}) collective-permute-start(bf16[3200,128]{1,0:T(8,128)(2,1)} %get-tuple-element.117), channel_id=1, source_target_pairs={{0,1},{1,0},{2,3},{3,2},{4,5},{5,4},{6,7},{7,6},{8,9},{9,8},{10,11... | collective-permute-start | bytes 2457608 | tf_op jit(solution)/shard_map/ppermute | solution.py:508
  86.8 27.6 %all-to-all-start = ((bf16[4,256,512]{2,1,0:T(8,128)(2,1)}), bf16[4,256,512]{2,1,0:T(8,128)(2,1)S(1)}, u32[]{:S(2)}, u32[]{:S(2)}) async-start(bf16[4,256,512]{2,1,0:T(8,128)(2,1)} %bitcast.53), calls=%async_computation | async-start | bytes 2097152 | tf_op jit(solution)/shard_map/all_to_all | solution.py:605
  90.3 5.5 %collective-permute-start.14 = (bf16[80,512]{1,0:T(8,128)(2,1)}, bf16[80,512]{1,0:T(8,128)(2,1)}, u32[]{:S(2)}, u32[]{:S(2)}) collective-permute-start(bf16[80,512]{1,0:T(8,128)(2,1)} %copy-done.8), channel_id=1, source_target_pairs={{0,8},{1,9},{2,10},{3,11},{4,12},{5,13},{6,14},{7,15},{8,0},{9,1},... | collective-permute-start | bytes 245768 | tf_op jit(solution)/shard_map/ppermute | solution.py:508
  93.1 19.6 %collective-permute-start.16 = (bf16[800,128]{1,0:T(8,128)(2,1)}, bf16[800,128]{1,0:T(8,128)(2,1)S(1)}, u32[]{:S(2)}, u32[]{:S(2)}) collective-permute-start(bf16[800,128]{1,0:T(8,128)(2,1)} %get-tuple-element.124), channel_id=1, source_target_pairs={{0,2},{1,3},{2,0},{3,1},{4,6},{5,7},{6,4},{7,5},{8,10},{9,11},{10,... | collective-permute-start | bytes 614408 | tf_op jit(solution)/shard_map/ppermute | solution.py:508
  94.4 18.3 %collective-permute-start.17 = (bf16[800,128]{1,0:T(8,128)(2,1)}, bf16[800,128]{1,0:T(8,128)(2,1)S(1)}, u32[]{:S(2)}, u32[]{:S(2)}) collective-permute-start(bf16[800,128]{1,0:T(8,128)(2,1)} %get-tuple-element.125), channel_id=1, source_target_pairs={{0,4},{1,5},{2,6},{3,7},{4,0},{5,1},{6,2},{7,3},{8,12},{9,13},{10,... | collective-permute-start | bytes 614408 | tf_op jit(solution)/shard_map/ppermute | solution.py:508
  95.6 17.1 %collective-permute-start.18 = (bf16[800,128]{1,0:T(8,128)(2,1)}, bf16[800,128]{1,0:T(8,128)(2,1)S(1)}, u32[]{:S(2)}, u32[]{:S(2)}) collective-permute-start(bf16[800,128]{1,0:T(8,128)(2,1)} %get-tuple-element.126), channel_id=1, source_target_pairs={{0,6},{1,7},{2,4},{3,5},{4,2},{5,3},{6,0},{7,1},{8,14},{9,15},{10,... | collective-permute-start | bytes 614408 | tf_op jit(solution)/shard_map/ppermute | solution.py:508
  97.5 11.2 %collective-permute-start.15 = (bf16[160,512]{1,0:T(8,128)(2,1)S(1)}, bf16[160,512]{1,0:T(8,128)(2,1)S(1)}, u32[]{:S(2)}, u32[]{:S(2)}) collective-permute-start(bf16[160,512]{1,0:T(8,128)(2,1)S(1)} %join.6.refs_0_), channel_id=1, source_target_pairs={{0,16},{1,17},{2,18},{3,19},{4,20},{5,21},{6,22},{7,23},{8,24},{9,... | collective-permute-start | bytes 491528 | tf_op jit(solution)/shard_map/ppermute | solution.py:508
  114.4 13.3 %collective-permute-start.25 = (bf16[320,512]{1,0:T(8,128)(2,1)S(1)}, bf16[320,512]{1,0:T(8,128)(2,1)S(1)}, u32[]{:S(2)}, u32[]{:S(2)}) collective-permute-start(bf16[320,512]{1,0:T(8,128)(2,1)S(1)} %join.7.refs_0_), channel_id=1, source_target_pairs={{0,2},{1,3},{2,0},{3,1},{4,6},{5,7},{6,4},{7,5},{8,10},{9,11},{10,... | collective-permute-start | bytes 983048 | tf_op jit(solution)/shard_map/ppermute | solution.py:508
  114.7 19.3 %all-to-all-start.1 = ((bf16[4,256,512]{2,1,0:T(8,128)(2,1)}), bf16[4,256,512]{2,1,0:T(8,128)(2,1)S(1)}, u32[]{:S(2)}, u32[]{:S(2)}) async-start(bf16[4,256,512]{2,1,0:T(8,128)(2,1)} %bitcast.54), calls=%async_computation.1 | async-start | bytes 2097152 | tf_op jit(solution)/shard_map/all_to_all | solution.py:605
  119.7 5.2 %collective-permute-start.20 = (bf16[200,128]{1,0:T(8,128)(2,1)S(1)}, bf16[200,128]{1,0:T(8,128)(2,1)S(1)}, u32[]{:S(2)}, u32[]{:S(2)}) collective-permute-start(bf16[200,128]{1,0:T(8,128)(2,1)S(1)} %get-tuple-element.132), channel_id=1, source_target_pairs={{0,16},{1,17},{2,18},{3,19},{4,20},{5,21},{6,22},{7,23},{8,24},{9,... | collective-permute-start | bytes 153608 | tf_op jit(solution)/shard_map/ppermute | solution.py:508
  122.9 4.8 %collective-permute-start.21 = (bf16[200,128]{1,0:T(8,128)(2,1)S(1)}, bf16[200,128]{1,0:T(8,128)(2,1)S(1)}, u32[]{:S(2)}, u32[]{:S(2)}) collective-permute-start(bf16[200,128]{1,0:T(8,128)(2,1)S(1)} %get-tuple-element.133), channel_id=1, source_target_pairs={{0,24},{1,25},{2,26},{3,27},{4,28},{5,29},{6,30},{7,31},{8,16},{9,... | collective-permute-start | bytes 153608 | tf_op jit(solution)/shard_map/ppermute | solution.py:508
  127.8 14.5 %collective-permute-start.26 = (bf16[640,512]{1,0:T(8,128)(2,1)S(1)}, bf16[640,512]{1,0:T(8,128)(2,1)S(1)}, u32[]{:S(2)}, u32[]{:S(2)}) collective-permute-start(bf16[640,512]{1,0:T(8,128)(2,1)S(1)} %join.9.refs_0_), channel_id=1, source_target_pairs={{0,4},{1,5},{2,6},{3,7},{4,0},{5,1},{6,2},{7,3},{8,12},{9,13},{10,... | collective-permute-start | bytes 1966088 | tf_op jit(solution)/shard_map/ppermute | solution.py:508
  129.0 5.0 %collective-permute-start.22 = (bf16[200,128]{1,0:T(8,128)(2,1)S(1)}, bf16[200,128]{1,0:T(8,128)(2,1)S(1)}, u32[]{:S(2)}, u32[]{:S(2)}) collective-permute-start(bf16[200,128]{1,0:T(8,128)(2,1)S(1)} %add.38.refs_0_), channel_id=1, source_target_pairs={{0,8},{1,9},{2,10},{3,11},{4,12},{5,13},{6,14},{7,15},{8,0},{9,1},... | collective-permute-start | bytes 153608 | tf_op jit(solution)/shard_map/ppermute | solution.py:508
  129.0 5.0 %collective-permute-start.23 = (bf16[200,128]{1,0:T(8,128)(2,1)S(1)}, bf16[200,128]{1,0:T(8,128)(2,1)}, u32[]{:S(2)}, u32[]{:S(2)}) collective-permute-start(bf16[200,128]{1,0:T(8,128)(2,1)S(1)} %add.38.refs_0_), channel_id=1, source_target_pairs={{0,16},{1,17},{2,18},{3,19},{4,20},{5,21},{6,22},{7,23},{8,24},{9,... | collective-permute-start | bytes 153608 | tf_op jit(solution)/shard_map/ppermute | solution.py:508
  130.4 5.1 %collective-permute-start.24 = (bf16[200,128]{1,0:T(8,128)(2,1)S(1)}, bf16[200,128]{1,0:T(8,128)(2,1)}, u32[]{:S(2)}, u32[]{:S(2)}) collective-permute-start(bf16[200,128]{1,0:T(8,128)(2,1)S(1)} %add.38.refs_0_), channel_id=1, source_target_pairs={{0,24},{1,25},{2,26},{3,27},{4,28},{5,29},{6,30},{7,31},{8,16},{9,... | collective-permute-start | bytes 153608 | tf_op jit(solution)/shard_map/ppermute | solution.py:508
  142.4 16.0 %collective-permute-start.27 = (bf16[1280,512]{1,0:T(8,128)(2,1)S(1)}, bf16[1280,512]{1,0:T(8,128)(2,1)S(1)}, u32[]{:S(2)}, u32[]{:S(2)}) collective-permute-start(bf16[1280,512]{1,0:T(8,128)(2,1)S(1)} %join.10.own_ref), channel_id=1, source_target_pairs={{0,1},{1,0},{2,3},{3,2},{4,5},{5,4},{6,7},{7,6},{8,9},{9,8},{10,11... | collective-permute-start | bytes 3932168 | tf_op jit(solution)/shard_map/ppermute | solution.py:508
  145.1 6.7 %collective-permute-start.28 = (bf16[800,128]{1,0:T(8,128)(2,1)S(1)}, bf16[800,128]{1,0:T(8,128)(2,1)S(1)}, u32[]{:S(2)}, u32[]{:S(2)}) collective-permute-start(bf16[800,128]{1,0:T(8,128)(2,1)S(1)} %join.8.refs_0_), channel_id=1, source_target_pairs={{0,2},{1,3},{2,0},{3,1},{4,6},{5,7},{6,4},{7,5},{8,10},{9,11},{10,... | collective-permute-start | bytes 614408 | tf_op jit(solution)/shard_map/ppermute | solution.py:508
  146.5 6.3 %collective-permute-start.29 = (bf16[800,128]{1,0:T(8,128)(2,1)S(1)}, bf16[800,128]{1,0:T(8,128)(2,1)S(1)}, u32[]{:S(2)}, u32[]{:S(2)}) collective-permute-start(bf16[800,128]{1,0:T(8,128)(2,1)S(1)} %join.8.refs_0_), channel_id=1, source_target_pairs={{0,4},{1,5},{2,6},{3,7},{4,0},{5,1},{6,2},{7,3},{8,12},{9,13},{10,... | collective-permute-start | bytes 614408 | tf_op jit(solution)/shard_map/ppermute | solution.py:508
  147.7 9.3 %collective-permute-start.30 = (bf16[800,128]{1,0:T(8,128)(2,1)S(1)}, bf16[800,128]{1,0:T(8,128)(2,1)S(1)}, u32[]{:S(2)}, u32[]{:S(2)}) collective-permute-start(bf16[800,128]{1,0:T(8,128)(2,1)S(1)} %join.8.refs_0_), channel_id=1, source_target_pairs={{0,6},{1,7},{2,4},{3,5},{4,2},{5,3},{6,0},{7,1},{8,14},{9,15},{10,... | collective-permute-start | bytes 614408 | tf_op jit(solution)/shard_map/ppermute | solution.py:508
  157.1 3.9 %collective-permute-start.31 = (bf16[3200,128]{1,0:T(8,128)(2,1)S(1)}, bf16[3200,128]{1,0:T(8,128)(2,1)S(1)}, u32[]{:S(2)}, u32[]{:S(2)}) collective-permute-start(bf16[3200,128]{1,0:T(8,128)(2,1)S(1)} %join.11.own_ref), channel_id=1, source_target_pairs={{0,1},{1,0},{2,3},{3,2},{4,5},{5,4},{6,7},{7,6},{8,9},{9,8},{10,11... | collective-permute-start | bytes 2457608 | tf_op jit(solution)/shard_map/ppermute | solution.py:508
  (24 other events, 288.2 us)
where the time goes:
time: 164 us; the launch traced here: 163 us
  Pallas kernels  67.2 us (41%)
  waiting for transfers between devices  45.4 us (28%)
  starting transfers between devices  43.3 us (26%)
  local copies, waits for them, and re-layouts  6 us (4%)
    ppermute x32, waiting for transfers between devices, send_xor(): return lax.ppermute(values, BOTH, [(i, i ^ flip) for i in range(count)])  43.9 us
    ppermute x32, starting transfers between devices, send_xor(): return lax.ppermute(values, BOTH, [(i, i ^ flip) for i in range(count)])  35.4 us
    pallas_call x1, Pallas kernels, backward_call(): pl.pallas_call(functools.partial(backward_kernel, first), grid=(count,),...  17.1 us
    pallas_call x1, Pallas kernels, forward_call(): pl.pallas_call(forward_kernel, grid=(1,), in_specs=[SMEM_SPEC, SMEM_SPEC]...  14.3 us
    pallas_call x1, Pallas kernels, middle_call(): pl.pallas_call(middle_kernel, grid=(1,), in_specs=[SMEM_SPEC, SMEM_SPEC,...  13.7 us
    all_to_all x2, starting transfers between devices, home(): return lax.all_to_all(values.reshape(tokens.shape), 'blk', 0, 0, tiled=True)  7.87 us
    pallas_call x1, Pallas kernels, last_call(): pl.pallas_call(last_kernel, grid=(1,), in_specs=[SMEM_SPEC] + [whole(a.sh...  7.58 us
    pallas_call x2, Pallas kernels, finish_call(): pl.pallas_call(kernel, grid=(1,), in_specs=[SMEM_SPEC, whole(own.shape),...  4.79 us
  transfers between devices with their start and end apart: 34, of which 13 were waited for; matrix products, arithmetic and copies ran while one was open for 1% of the time, Pallas kernels for 30%

commit v1 on v0

--- a/solution.py
+++ b/solution.py
@@ -184,6 +184,53 @@
     )(ends, blk, *pieces, gain[None], bias[None], w_qkv, b_qv[None])
 
 
+def leave(blk_ref, whole_ref, own_ref, near_ref, far_ref):
+    size = own_ref.shape[0]
+    for flip, dest in ((0, own_ref), (1, near_ref), (2, far_ref.at[:size]), (3, far_ref.at[size:])):
+        at = jnp.bitwise_xor(blk_ref[0], flip) * size
+        dest[...] = whole_ref[pl.ds(pl.multiple_of(at, size), size), :]
+
+
+def relay_kernel(near_ref, far_ref, out_ref):
+    size = near_ref.shape[0]
+    out_ref[:size] = near_ref[...]
+    out_ref[size:] = far_ref[size:]
+
+
+def relay_call(near, far):
+    return pl.pallas_call(
+        relay_kernel,
+        grid=(1,),
+        in_specs=[whole(near.shape), whole(far.shape)],
+        out_specs=whole(far.shape),
+        out_shape=jax.ShapeDtypeStruct(far.shape, far.dtype),
+        compiler_params=params(8),
+        cost_estimate=cost(1e7, 1e5),
+        name="relay",
+    )(near, far)
+
+
+def arrive_kernel(blk_ref, own_ref, near_ref, far_ref, out_ref):
+    size = own_ref.shape[0]
+    pieces = (own_ref[...], near_ref[:size], far_ref[:size], near_ref[size:])
+    for flip, piece in enumerate(pieces):
+        out_ref[jnp.bitwise_xor(blk_ref[0], flip)] = piece.astype(out_ref.dtype)
+
+
+def arrive_call(blk, own, near, far, dtype):
+    shape = (4,) + own.shape
+    return pl.pallas_call(
+        arrive_kernel,
+        grid=(1,),
+        in_specs=[SMEM_SPEC, whole(own.shape), whole(near.shape), whole(far.shape)],
+        out_specs=whole(shape),
+        out_shape=jax.ShapeDtypeStruct(shape, dtype),
+        compiler_params=params(12),
+        cost_estimate=cost(1e7, 1e5),
+        name="arrive",
+    )(blk, own, near, far)
+
+
 def split_halves(core_ref, whole_ref, keep_ref, send_ref):
     half = keep_ref.shape[0]
     core = core_ref[0]
@@ -193,8 +240,8 @@
 
 def middle_kernel(
     core_ref, blk_ref, att_ref, x_ref, c0_ref, c1_ref, c2_ref, c3_ref, wo_ref, bo_ref, gain_ref, bias_ref, wup_ref, bup_ref, wdown_ref, bdown_ref,
-    out_ref, gmid_ref, gatt_ref, delta_ref, keep_ref, send_ref, vec_ref,
-    cot_ref, gw_ref, hidden_ref, gpre_ref, n2_ref, attb_ref, gbr_ref,
+    o0_ref, o1_ref, o2_ref, gmid_ref, gatt_ref, delta_ref, keep_ref, send_ref, vec_ref,
+    cot_ref, out_ref, gw_ref, hidden_ref, gpre_ref, n2_ref, attb_ref, gbr_ref,
 ):
     pairs = att_ref.shape[0]
     t, d = x_ref.shape
@@ -253,6 +300,7 @@
         return carry
 
     lax.fori_loop(0, t // MID_TILE, tile, 0)
+    leave(blk_ref, out_ref, o0_ref, o1_ref, o2_ref)
     gw_ref[:ff] = mm_tn(hidden_ref[...], cot_ref[...])
     gw_ref[ff : ff + d] = mm_tn(n2_ref[...], gpre_ref[:, :d])
     gw_ref[ff + d : ff + 2 * d] = mm_tn(n2_ref[...], gpre_ref[:, d:])
@@ -274,11 +322,13 @@
             whole((d, ff)), whole((1, ff)), whole((ff, d)), whole((1, d)),
         ],
         out_specs=[
-            by_row(d, t), by_row(d, t), by_pair(pairs, t), heads_row(t), whole((half, d)), whole((half, d)),
+            whole((t // 4, d)), whole((t // 4, d)), whole((t // 2, d)), by_row(d, t), by_pair(pairs, t), heads_row(t), whole((half, d)), whole((half, d)),
             whole((8, d)),
         ],
         out_shape=[
-            pltpu.HBM((t, d), BF16),
+            pltpu.HBM((t // 4, d), BF16),
+            pltpu.HBM((t // 4, d), BF16),
+            pltpu.HBM((t // 2, d), BF16),
             pltpu.HBM((t, d), F32),
             pltpu.HBM((pairs, t, LANES), BF16),
             jax.ShapeDtypeStruct((HEADS, t), F32),
@@ -288,6 +338,7 @@
         ],
         scratch_shapes=[
             pltpu.VMEM((t, d), BF16),
+            pltpu.VMEM((t, d), BF16),
             pltpu.VMEM((2 * half, d), F32),
             pltpu.VMEM((t, ff), BF16),
             pltpu.VMEM((t, ff), BF16),
@@ -295,7 +346,7 @@
             pltpu.VMEM((t, d), BF16),
             pltpu.VMEM((t, d), BF16),
         ],
-        compiler_params=params(28),
+        compiler_params=params(30),
         cost_estimate=cost(15e9, 20e6),
         name="middle",
     )(core, blk, att, x, *cots, w_o, b_o[None], gain[None], bias[None], w_up, b_up[None], w_down, b_down[None])
@@ -374,9 +425,10 @@
 
 
 def last_kernel(*refs):
-    core_ref = refs[0]
-    grads = refs[1:4]
-    n1_ref, x_ref, gmid_ref, gain_ref, w_ref, vecmid_ref, gin_ref, keep_ref, send_ref, gw_ref = refs[4:]
+    core_ref, blk_ref = refs[:2]
+    grads = refs[2:5]
+    n1_ref, x_ref, gmid_ref, gain_ref, w_ref, vecmid_ref = refs[5:11]
+    g0_ref, g1_ref, g2_ref, keep_ref, send_ref, gw_ref, gin_ref = refs[11:]
     pairs = grads[0].shape[0]
     d = x_ref.shape[-1]
     half = keep_ref.shape[0]
@@ -389,6 +441,7 @@
     e = mm_nt(gqkv, w_ref[...])
     n, scale = norm_parts(x_ref[...].astype(F32))
     gin_ref[...] = (gmid_ref[...] + norm_pull(e, n, scale, gain_ref[...])).astype(BF16)
+    leave(blk_ref, gin_ref, g0_ref, g1_ref, g2_ref)
 
     def col(values):
         return jnp.sum(values, axis=0, keepdims=True)
@@ -405,26 +458,28 @@
     split_halves(core_ref, gw_ref, keep_ref, send_ref)
 
 
-def last_call(core, grads, n1, x, gmid, gain, w_qkv, vec_mid):
+def last_call(core, blk, grads, n1, x, gmid, gain, w_qkv, vec_mid):
     t, d = x.shape
     half = 3 * d * d // LANES // 2 + VEC_ROWS
     return pl.pallas_call(
         last_kernel,
         grid=(1,),
-        in_specs=[SMEM_SPEC]
+        in_specs=[SMEM_SPEC, SMEM_SPEC]
         + [whole(a.shape) for a in grads]
         + [by_row(d, t), by_row(d, t), by_row(d, t), whole((1, d)), whole(w_qkv.shape), whole((8, d))],
-        out_specs=[by_row(d, t), whole((half, LANES)), whole((half, LANES))],
+        out_specs=[whole((t // 4, d)), whole((t // 4, d)), whole((t // 2, d)), whole((half, LANES)), whole((half, LANES))],
         out_shape=[
-            pltpu.HBM((t, d), BF16),
+            pltpu.HBM((t // 4, d), BF16),
+            pltpu.HBM((t // 4, d), BF16),
+            pltpu.HBM((t // 2, d), BF16),
             jax.ShapeDtypeStruct((half, LANES), F32),
             jax.ShapeDtypeStruct((half, LANES), BF16),
         ],
-        scratch_shapes=[pltpu.VMEM((2 * half, LANES), F32)],
+        scratch_shapes=[pltpu.VMEM((2 * half, LANES), F32), pltpu.VMEM((t, d), BF16)],
         compiler_params=params(28),
         cost_estimate=cost(L_FLOPS, 1e5),
         name="last",
-    )(core, *in_hbm(*grads), n1, x, gmid, gain[None], w_qkv, vec_mid)
+    )(core, blk, *in_hbm(*grads), n1, x, gmid, gain[None], w_qkv, vec_mid)
 
 
 def ordered_halves(core_ref, own_ref, got_ref, write):
@@ -450,25 +505,6 @@
         wo_ref[...] = take(ff + 2 * d, ff + 3 * d)
 
     ordered_halves(core_ref, own_ref, got_ref, write)
-
-
-def copy_kernel(in_ref, out_ref):
-    out_ref[...] = in_ref[...].astype(out_ref.dtype)
-
-
-def copy_call(order, values, dtype):
-    parts, rows, d = values.shape
-    spec = pl.BlockSpec((1, rows, d), lambda i: (i, 0, 0))
-    return pl.pallas_call(
-        lambda order_ref, in_ref, out_ref: copy_kernel(in_ref, out_ref),
-        grid=(parts,),
-        in_specs=[SMEM_SPEC, spec],
-        out_specs=spec,
-        out_shape=jax.ShapeDtypeStruct(values.shape, dtype),
-        compiler_params=params(28),
-        cost_estimate=cost(1e7, 1e5),
-        name="copy",
-    )(order, values)
 
 
 def finish_last_kernel(core_ref, own_ref, got_ref, qkv_ref, *vec_refs):
@@ -597,38 +633,37 @@
     cot = lax.optimization_barrier(tuple(cot) + tuple(x))[:row_count]
     cot = swap(list(cot))
     x, q, k, v, n1, att, lse = forward_call(ends, blk, x, ln1_gain, ln1_bias, w_qkv, b_qv)
-    out, gmid, gatt, delta, keep, send, vec_mid = middle_call(
+    out, out_near, out_far, gmid, gatt, delta, keep, send, vec_mid = middle_call(
         core, blk, att, x, cot, w_o, b_o, ln2_gain, ln2_bias, w_up, b_up, w_down, b_down
     )
-
-    def home(values):
-        return lax.all_to_all(values.reshape(tokens.shape), "blk", 0, 0, tiled=True)
-
     own, *parts = add_call(place_plane, 4, [keep, send_xor(send, 1)], F32)
     grads = backward_call(after(ends, own), q, k, v, gatt, lse, delta, 0, d // LANES)
     own, *parts = add_call(after(place_deep, grads[0]), 4, [own] + swap_parts(parts, 1), F32)
+    out_far = send_xor(after(out_far, own), 2)
     first = [own] + swap_parts(parts, 3)
-    gin, keep, send = last_call(after(core, own), grads, n1, x, gmid, ln1_gain, w_qkv, vec_mid)
-    output = home(after(out, send))
+    gin, gin_near, gin_far, keep, send = last_call(
+        after(core, own), blk, grads, n1, x, gmid, ln1_gain, w_qkv, vec_mid
+    )
     (first,) = add_call(0, 1, first, BF16)
-    send, first = lax.optimization_barrier((send, first))
+    send, first, out_far = lax.optimization_barrier((send, first, out_far))
     first_z = spread(first, 3, 2)
     own, *parts = add_call(place_plane, 4, [keep, send_xor(send, 1)], F32)
     first = join_call(after(place_deep & 1, own), [first] + first_z)
     first_z = spread(first, 4, 2)
     second = swap_parts(parts, 1)
-    own, *parts = add_call(place_deep, 4, [own] + second, F32)
+    out_near = send_xor(relay_call(after(out_near, own), out_far), 1)
+    output = arrive_call(blk, out, out_near, out_far, BF16)
+    own, *parts = add_call(after(place_deep, output), 4, [own] + second, F32)
     first = join_call(place_deep >> 1, [first] + first_z)
-    first, gin, output = lax.optimization_barrier((first, gin, output, own))[:3]
-    gin = home(gin)
+    first, gin_far = lax.optimization_barrier((first, gin_far, own))[:2]
+    gin_far = send_xor(gin_far, 2)
     (second,) = add_call(0, 1, [own] + swap_parts(parts, 3), BF16)
     first = join_call(after(place_plane & 1, second), [first] + spread(first, 1, 2))
-    second = join_call(after(place_deep, gin), [second] + spread(second, 3, 4))
+    second = join_call(after(place_deep, gin_far), [second] + spread(second, 3, 4))
     first = join_call(after(place_plane >> 1, second), [first] + spread(first, 2, 2))
-    order, output, gin = lax.optimization_barrier((core, output, gin, second))[:3]
-    output = copy_call(order, output, BF16)
-    input_grad = copy_call(order, gin, F32)
-    second = join_call(after(place_plane, output, input_grad), [second] + spread(second, 1, 4))
+    gin_near = send_xor(relay_call(after(gin_near, second), gin_far), 1)
+    input_grad = arrive_call(blk, gin, gin_near, gin_far, F32)
+    second = join_call(after(place_plane, input_grad), [second] + spread(second, 1, 4))
     gw_down, gw_up, gw_o = finish_call(
         finish_mid_kernel, core, first, send_xor(first, 1), [w_down.shape, w_up.shape, w_o.shape], "finish_mid"
     )

time: 164 us -> 156 us (0.951)
  waiting for transfers between devices: 45.4 us -> 42.3 us
  Pallas kernels: 67.2 us -> 64.9 us
  starting transfers between devices: 43.3 us -> 41.3 us
    all_to_all x2 -> x0, starting transfers between devices: 7.87 us -> none  [home(): return lax.all_to_all(values.reshape(tokens.shape), 'blk', 0, 0, tiled=True)]
    ppermute x32 -> x36, starting transfers between devices: 35.4 us -> 41.3 us  [send_xor(): return lax.ppermute(values, BOTH, [(i, i ^ flip) for i in range(count)])]
    pallas_call x6, Pallas kernels: 1.96 us -> 0.25 us  [join_call(): pl.pallas_call(join_kernel, grid=(1,), in_specs=[SMEM_SPEC] + [whole(p.sh...]
    ppermute x32 -> x36, waiting for transfers between devices: 43.9 us -> 42.3 us  [send_xor(): return lax.ppermute(values, BOTH, [(i, i ^ flip) for i in range(count)])]
    pallas_call x3 -> x5, Pallas kernels: 10.9 us -> 10 us  [the longest x1 7.43 us: last_call(): pl.pallas_call(last_kernel, grid=(1,), in_specs=[SMEM_SPEC, SMEM_SPEC] +...]
    unnamed x44 -> x54, local copies, waits for them, and re-layouts: 3.36 us -> 3.27 us
  transfers between devices with their start and end apart: 34 -> 36, of which waited for: 13 -> 11; matrix products, arithmetic and copies ran while one was open for 1% -> 1% of each run, Pallas kernels for 30% -> 28%
where the time goes in v1:
time: 156 us
  Pallas kernels  64.9 us (42%)
  waiting for transfers between devices  42.3 us (27%)
  starting transfers between devices  41.3 us (26%)
  local copies, waits for them, and re-layouts  5.93 us (4%)
    ppermute x36, waiting for transfers between devices, send_xor(): return lax.ppermute(values, BOTH, [(i, i ^ flip) for i in range(count)])  42.3 us
    ppermute x36, starting transfers between devices, send_xor(): return lax.ppermute(values, BOTH, [(i, i ^ flip) for i in range(count)])  41.3 us
    pallas_call x1, Pallas kernels, backward_call(): pl.pallas_call(functools.partial(backward_kernel, first), grid=(count,),...  17.1 us
    pallas_call x1, Pallas kernels, forward_call(): pl.pallas_call(forward_kernel, grid=(1,), in_specs=[SMEM_SPEC, SMEM_SPEC]...  14.3 us
    pallas_call x1, Pallas kernels, middle_call(): pl.pallas_call(middle_kernel, grid=(1,), in_specs=[SMEM_SPEC, SMEM_SPEC,...  14 us
    pallas_call x1, Pallas kernels, last_call(): pl.pallas_call(last_kernel, grid=(1,), in_specs=[SMEM_SPEC, SMEM_SPEC] +...  7.43 us
    pallas_call x2, Pallas kernels, finish_call(): pl.pallas_call(kernel, grid=(1,), in_specs=[SMEM_SPEC, whole(own.shape),...  4.79 us
    pallas_call x6, Pallas kernels, add_call(): pl.pallas_call(add_kernel, grid=(1,), in_specs=[SMEM_SPEC] + [whole(a.sha...  4.43 us
  transfers between devices with their start and end apart: 36, of which 11 were waited for; matrix products, arithmetic and copies ran while one was open for 1% of the time, Pallas kernels for 28%

profile of v1, /device:TPU:1, one launch (start us, length us, event | category | flops | bytes accessed | tf_op | source)
XLA Modules:
  0.0 155.8 jit_solution(202787088401766495)
XLA Ops:
  0.7 1.4 dynamic-slice_bitcast_fusion.4
  2.2 2.7 %collective-permute-start.1 = (bf16[256,512]{1,0:T(8,128)(2,1)S(1)}, bf16[256,512]{1,0:T(8,128)(2,1)S(1)}, u32[]{:S(2)}, u32[]{:S(2)}) collective-permute-start(bf16[256,512]{1,0:T(8,128)(2,1)S(1)} %get-tuple-element.169), channel_id=1, source_target_pairs={{0,2},{1,3},{2,0},{3,1},{4,6},{5,7},{6,4},{7,5},{8,10},{9,11},{10,... | collective-permute-start | bytes 786440 | tf_op jit(solution)/shard_map/ppermute | solution.py:544
  6.4 5.1 %collective-permute-done.1.x2_ref = bf16[256,512]{1,0:T(8,128)(2,1)S(1)} collective-permute-done((bf16[256,512]{1,0:T(8,128)(2,1)S(1)}, bf16[256,512]{1,0:T(8,128)(2,1)S(1)}, u32[]{:S(2)}, u32[]{:S(2)}) %collective-permute-start.1) | collective-permute-done | bytes 262176 | tf_op jit(solution)/shard_map/ppermute | solution.py:544
  11.5 5.6 %collective-permute-done.2.x3_ref = bf16[256,512]{1,0:T(8,128)(2,1)S(1)} collective-permute-done((bf16[256,512]{1,0:T(8,128)(2,1)S(1)}, bf16[256,512]{1,0:T(8,128)(2,1)S(1)}, u32[]{:S(2)}, u32[]{:S(2)}) %collective-permute-start.2) | collective-permute-done | bytes 262176 | tf_op jit(solution)/shard_map/ppermute | solution.py:544
  19.4 14.3 %forward.1 = (bf16[1024,512]{1,0:T(8,128)(2,1)S(1)}, bf16[4,1024,128]{2,1,0:T(8,128)(2,1)}, bf16[4,1024,128]{2,1,0:T(8,128)(2,1)}, bf16[4,1024,128]{2,1,0:T(8,12...) custom-call(s32[8]{0:T(128)S(1)} %fusion.ends_ref, ...), custom_call_target="tpu_custom_call" | custom-call | flops 20000000000 | bytes 10000000 | tf_op jit(solution)/shard_map/forward/pallas_call | solution.py:161
  33.9 14.0 %middle.1 = (bf16[256,512]{1,0:T(8,128)(2,1)}, bf16[256,512]{1,0:T(8,128)(2,1)}, bf16[512,512]{1,0:T(8,128)(2,1)}, f32[1024,512]{1,0:T(8,128)}, bf16[4,1024,128]...) custom-call(s32[1]{0:T(128)} %bitcast.1.core_ref.refs_0_, ...), custom_call_target="tpu_custom_call" | custom-call | flops 15000000512 | bytes 20000000 | tf_op jit(solution)/shard_map/middle/pallas_call | solution.py:316
  47.9 3.3 %collective-permute-done.6.refs_1_ = bf16[1280,512]{1,0:T(8,128)(2,1)} collective-permute-done((bf16[1280,512]{1,0:T(8,128)(2,1)}, bf16[1280,512]{1,0:T(8,128)(2,1)}, u32[]{:S(2)}, u32[]{:S(2)}) %collective-permute-start.6) | collective-permute-done | bytes 1310752 | tf_op jit(solution)/shard_map/ppermute | solution.py:544
  51.2 1.5 add.33
  52.8 1.5 collective-permute-start.7
  55.5 17.1 %backward.1 = (bf16[4,1024,128]{2,1,0:T(8,128)(2,1)}, bf16[4,1024,128]{2,1,0:T(8,128)(2,1)}, bf16[4,1024,128]{2,1,0:T(8,128)(2,1)}) custom-call(s32[8]{0:T(128)S(1)} %fusion.ends_ref, bf16[4,1024,128]{2,1,0:T(8,128)(2,1)} %get-tuple-element.100.q_ref, bf16[4,1024,128]{2,1,0:T(8,128)(2,1)} %get-tuple-element.101.k_ref, ...), custom_call_target="tpu_custom_call" | custom-call | flops 4000000000 | bytes 400000 | tf_op jit(solution)/shard_map/backward/pallas_call | solution.py:411
  73.4 1.5 collective-permute-start.13
  74.8 1.3 collective-permute-start.10
  76.1 2.3 %collective-permute-start.11 = (bf16[80,512]{1,0:T(8,128)(2,1)S(1)}, bf16[80,512]{1,0:T(8,128)(2,1)S(1)}, u32[]{:S(2)}, u32[]{:S(2)}) collective-permute-start(bf16[80,512]{1,0:T(8,128)(2,1)S(1)} %get-tuple-element.121), channel_id=1, source_target_pairs={{0,16},{1,17},{2,18},{3,19},{4,20},{5,21},{6,22},{7,23},{8,24},{9,... | collective-permute-start | bytes 245768 | tf_op jit(solution)/shard_map/ppermute | solution.py:544
  78.5 7.4 %last.1 = (bf16[256,512]{1,0:T(8,128)(2,1)}, bf16[256,512]{1,0:T(8,128)(2,1)}, bf16[512,512]{1,0:T(8,128)(2,1)}, f32[3200,128]{1,0:T(8,128)S(1)}, bf16[3200,128]{1,0:T(8,128)(2,1)S(1)}) custom-call(s32[1]{0:T(128)} %bitcast.1.core_ref.refs_0_, s32[1]{0:T(128)} %bitcast.blk_ref.refs_1_, bf16[4,1024,128]{2,1,0:T(8,128)(2,1)} %get-tuple-element.106.refs_2_, ...), custom_call_target="tpu_custom_call" | custom-call | flops 1000000000 | bytes 100000 | tf_op jit(solution)/shard_map/last/pallas_call | solution.py:464
  86.0 2.1 %collective-permute-start.14 = (bf16[3200,128]{1,0:T(8,128)(2,1)S(1)}, bf16[3200,128]{1,0:T(8,128)(2,1)S(1)}, u32[]{:S(2)}, u32[]{:S(2)}) collective-permute-start(bf16[3200,128]{1,0:T(8,128)(2,1)S(1)} %get-tuple-element.125), channel_id=1, source_target_pairs={{0,1},{1,0},{2,3},{3,2},{4,5},{5,4},{6,7},{7,6},{8,9},{9,8},{10,11... | collective-permute-start | bytes 2457608 | tf_op jit(solution)/shard_map/ppermute | solution.py:544
  88.1 2.0 %collective-permute-done.14.refs_1_ = bf16[3200,128]{1,0:T(8,128)(2,1)S(1)} collective-permute-done((bf16[3200,128]{1,0:T(8,128)(2,1)S(1)}, bf16[3200,128]{1,0:T(8,128)(2,1)S(1)}, u32[]{:S(2)}, u32[]{:S(2)}) %collective-permute-start.14) | collective-permute-done | bytes 819232 | tf_op jit(solution)/shard_map/ppermute | solution.py:544
  90.1 1.5 add.36
  95.9 2.4 %collective-permute-start.17 = (bf16[160,512]{1,0:T(8,128)(2,1)S(1)}, bf16[160,512]{1,0:T(8,128)(2,1)S(1)}, u32[]{:S(2)}, u32[]{:S(2)}) collective-permute-start(bf16[160,512]{1,0:T(8,128)(2,1)S(1)} %join.6.refs_0_), channel_id=1, source_target_pairs={{0,16},{1,17},{2,18},{3,19},{4,20},{5,21},{6,22},{7,23},{8,24},{9,... | collective-permute-start | bytes 491528 | tf_op jit(solution)/shard_map/ppermute | solution.py:544
  99.0 6.5 %collective-permute-done.17.refs_1_ = bf16[160,512]{1,0:T(8,128)(2,1)S(1)} collective-permute-done((bf16[160,512]{1,0:T(8,128)(2,1)S(1)}, bf16[160,512]{1,0:T(8,128)(2,1)S(1)}, u32[]{:S(2)}, u32[]{:S(2)}) %collective-permute-start.17) | collective-permute-done | bytes 163872 | tf_op jit(solution)/shard_map/ppermute | solution.py:544
  111.0 1.4 collective-permute-start.22
  112.4 3.1 %collective-permute-start.23 = (bf16[200,128]{1,0:T(8,128)(2,1)S(1)}, bf16[200,128]{1,0:T(8,128)(2,1)S(1)}, u32[]{:S(2)}, u32[]{:S(2)}) collective-permute-start(bf16[200,128]{1,0:T(8,128)(2,1)S(1)} %get-tuple-element.142), channel_id=1, source_target_pairs={{0,16},{1,17},{2,18},{3,19},{4,20},{5,21},{6,22},{7,23},{8,24},{9,... | collective-permute-start | bytes 153608 | tf_op jit(solution)/shard_map/ppermute | solution.py:544
  115.5 2.0 %collective-permute-done.23.refs_2_ = bf16[200,128]{1,0:T(8,128)(2,1)S(1)} collective-permute-done((bf16[200,128]{1,0:T(8,128)(2,1)S(1)}, bf16[200,128]{1,0:T(8,128)(2,1)S(1)}, u32[]{:S(2)}, u32[]{:S(2)}) %collective-permute-start.23) | collective-permute-done | bytes 51232 | tf_op jit(solution)/shard_map/ppermute | solution.py:544
  117.5 2.8 %collective-permute-done.24.refs_3_ = bf16[200,128]{1,0:T(8,128)(2,1)S(1)} collective-permute-done((bf16[200,128]{1,0:T(8,128)(2,1)S(1)}, bf16[200,128]{1,0:T(8,128)(2,1)S(1)}, u32[]{:S(2)}, u32[]{:S(2)}) %collective-permute-start.24) | collective-permute-done | bytes 51232 | tf_op jit(solution)/shard_map/ppermute | solution.py:544
  120.4 1.3 collective-permute-start.30
  122.5 3.1 %collective-permute-start.26 = (bf16[200,128]{1,0:T(8,128)(2,1)S(1)}, bf16[200,128]{1,0:T(8,128)(2,1)S(1)}, u32[]{:S(2)}, u32[]{:S(2)}) collective-permute-start(bf16[200,128]{1,0:T(8,128)(2,1)S(1)} %add.38.refs_0_), channel_id=1, source_target_pairs={{0,16},{1,17},{2,18},{3,19},{4,20},{5,21},{6,22},{7,23},{8,24},{9,... | collective-permute-start | bytes 153608 | tf_op jit(solution)/shard_map/ppermute | solution.py:544
  125.7 7.0 %collective-permute-done.21.far_ref = bf16[512,512]{1,0:T(8,128)(2,1)S(1)} collective-permute-done((bf16[512,512]{1,0:T(8,128)(2,1)}, bf16[512,512]{1,0:T(8,128)(2,1)S(1)}, u32[]{:S(2)}, u32[]{:S(2)}) %collective-permute-start.21) | collective-permute-done | bytes 524320 | tf_op jit(solution)/shard_map/ppermute | solution.py:544
  132.8 3.6 %collective-permute-start.28 = (bf16[512,512]{1,0:T(8,128)(2,1)S(1)}, bf16[512,512]{1,0:T(8,128)(2,1)S(1)}, u32[]{:S(2)}, u32[]{:S(2)}) collective-permute-start(bf16[512,512]{1,0:T(8,128)(2,1)S(1)} %relay.3), channel_id=1, source_target_pairs={{0,1},{1,0},{2,3},{3,2},{4,5},{5,4},{6,7},{7,6},{8,9},{9,8},{10,11... | collective-permute-start | bytes 1572872 | tf_op jit(solution)/shard_map/ppermute | solution.py:544
  140.5 1.5 arrive.3
  141.9 2.5 %collective-permute-done.32.refs_1_ = bf16[800,128]{1,0:T(8,128)(2,1)S(1)} collective-permute-done((bf16[800,128]{1,0:T(8,128)(2,1)S(1)}, bf16[800,128]{1,0:T(8,128)(2,1)S(1)}, u32[]{:S(2)}, u32[]{:S(2)}) %collective-permute-start.32) | collective-permute-done | bytes 204832 | tf_op jit(solution)/shard_map/ppermute | solution.py:544
  144.5 5.2 %collective-permute-done.34.refs_3_ = bf16[800,128]{1,0:T(8,128)(2,1)S(1)} collective-permute-done((bf16[800,128]{1,0:T(8,128)(2,1)S(1)}, bf16[800,128]{1,0:T(8,128)(2,1)S(1)}, u32[]{:S(2)}, u32[]{:S(2)}) %collective-permute-start.34) | collective-permute-done | bytes 204832 | tf_op jit(solution)/shard_map/ppermute | solution.py:544
  151.0 2.7 %finish_mid.1 = (f32[1024,512]{1,0:T(8,128)}, f32[512,1024]{1,0:T(8,128)}, f32[512,512]{1,0:T(8,128)}) custom-call(s32[1]{0:T(128)} %bitcast.1.core_ref.refs_0_, bf16[1280,512]{1,0:T(8,128)(2,1)S(1)} %join.10.own_ref, bf16[1280,512]{1,0:T(8,128)(2,1)S(1)} %collective-permute-done.31.got_ref), custom_call_target="tpu_custom_call" | custom-call | flops 100000000 | bytes 8000000 | tf_op jit(solution)/shard_map/finish_mid/pallas_call | solution.py:530
  153.7 2.1 %finish_last.1 = (f32[512,1536]{1,0:T(8,128)}, f32[1,512]{1,0:T(1,128)}, f32[1,1024]{1,0:T(1,128)}, f32[1,512]{1,0:T(1,128)}, f32[1,512]{1,0:T(1,128)}, /*index=...) custom-call(s32[1]{0:T(128)} %bitcast.1.core_ref.refs_0_, ...), custom_call_target="tpu_custom_call" | custom-call | flops 100000000 | bytes 8000000 | tf_op jit(solution)/shard_map/finish_last/pallas_call | solution.py:530
  (123 shorter events, 22.8 us)
Async XLA Ops:
  2.1 4.3 %collective-permute-start = (bf16[256,512]{1,0:T(8,128)(2,1)S(1)}, bf16[256,512]{1,0:T(8,128)(2,1)S(1)}, u32[]{:S(2)}, u32[]{:S(2)}) collective-permute-start(bf16[256,512]{1,0:T(8,128)(2,1)S(1)} %get-tuple-element.167), channel_id=1, source_target_pairs={{0,1},{1,0},{2,3},{3,2},{4,5},{5,4},{6,7},{7,6},{8,9},{9,8},{10,11... | collective-permute-start | bytes 786440 | tf_op jit(solution)/shard_map/ppermute | solution.py:544
  2.2 9.3 %collective-permute-start.1 = (bf16[256,512]{1,0:T(8,128)(2,1)S(1)}, bf16[256,512]{1,0:T(8,128)(2,1)S(1)}, u32[]{:S(2)}, u32[]{:S(2)}) collective-permute-start(bf16[256,512]{1,0:T(8,128)(2,1)S(1)} %get-tuple-element.169), channel_id=1, source_target_pairs={{0,2},{1,3},{2,0},{3,1},{4,6},{5,7},{6,4},{7,5},{8,10},{9,11},{10,... | collective-permute-start | bytes 786440 | tf_op jit(solution)/shard_map/ppermute | solution.py:544
  4.9 12.2 %collective-permute-start.2 = (bf16[256,512]{1,0:T(8,128)(2,1)S(1)}, bf16[256,512]{1,0:T(8,128)(2,1)S(1)}, u32[]{:S(2)}, u32[]{:S(2)}) collective-permute-start(bf16[256,512]{1,0:T(8,128)(2,1)S(1)} %get-tuple-element.166), channel_id=1, source_target_pairs={{0,3},{1,2},{2,1},{3,0},{4,7},{5,6},{6,5},{7,4},{8,11},{9,10},{10,... | collective-permute-start | bytes 786440 | tf_op jit(solution)/shard_map/ppermute | solution.py:544
  17.1 16.6 %collective-permute-start.3 = (bf16[256,512]{1,0:T(8,128)(2,1)S(1)}, bf16[256,512]{1,0:T(8,128)(2,1)S(1)}, u32[]{:S(2)}, u32[]{:S(2)}) collective-permute-start(bf16[256,512]{1,0:T(8,128)(2,1)S(1)} %get-tuple-element.91), channel_id=1, source_target_pairs={{0,1},{1,0},{2,3},{3,2},{4,5},{5,4},{6,7},{7,6},{8,9},{9,8},{10,11... | collective-permute-start | bytes 786440 | tf_op jit(solution)/shard_map/ppermute | solution.py:544
  17.5 16.2 %collective-permute-start.4 = (bf16[256,512]{1,0:T(8,128)(2,1)S(1)}, bf16[256,512]{1,0:T(8,128)(2,1)S(1)}, u32[]{:S(2)}, u32[]{:S(2)}) collective-permute-start(bf16[256,512]{1,0:T(8,128)(2,1)S(1)} %get-tuple-element.92), channel_id=1, source_target_pairs={{0,2},{1,3},{2,0},{3,1},{4,6},{5,7},{6,4},{7,5},{8,10},{9,11},{10,... | collective-permute-start | bytes 786440 | tf_op jit(solution)/shard_map/ppermute | solution.py:544
  18.8 15.0 %collective-permute-start.5 = (bf16[256,512]{1,0:T(8,128)(2,1)S(1)}, bf16[256,512]{1,0:T(8,128)(2,1)S(1)}, u32[]{:S(2)}, u32[]{:S(2)}) collective-permute-start(bf16[256,512]{1,0:T(8,128)(2,1)S(1)} %get-tuple-element.93), channel_id=1, source_target_pairs={{0,3},{1,2},{2,1},{3,0},{4,7},{5,6},{6,5},{7,4},{8,11},{9,10},{10,... | collective-permute-start | bytes 786440 | tf_op jit(solution)/shard_map/ppermute | solution.py:544
  52.8 19.8 %collective-permute-start.7 = (bf16[320,512]{1,0:T(8,128)(2,1)S(1)}, bf16[320,512]{1,0:T(8,128)(2,1)S(1)}, u32[]{:S(2)}, u32[]{:S(2)}) collective-permute-start(bf16[320,512]{1,0:T(8,128)(2,1)S(1)} %get-tuple-element.108), channel_id=1, source_target_pairs={{0,2},{1,3},{2,0},{3,1},{4,6},{5,7},{6,4},{7,5},{8,10},{9,11},{10,... | collective-permute-start | bytes 983048 | tf_op jit(solution)/shard_map/ppermute | solution.py:544
  54.2 18.4 %collective-permute-start.8 = (bf16[320,512]{1,0:T(8,128)(2,1)S(1)}, bf16[320,512]{1,0:T(8,128)(2,1)S(1)}, u32[]{:S(2)}, u32[]{:S(2)}) collective-permute-start(bf16[320,512]{1,0:T(8,128)(2,1)S(1)} %get-tuple-element.109), channel_id=1, source_target_pairs={{0,4},{1,5},{2,6},{3,7},{4,0},{5,1},{6,2},{7,3},{8,12},{9,13},{10,... | collective-permute-start | bytes 983048 | tf_op jit(solution)/shard_map/ppermute | solution.py:544
  55.5 17.2 %collective-permute-start.9 = (bf16[320,512]{1,0:T(8,128)(2,1)S(1)}, bf16[320,512]{1,0:T(8,128)(2,1)S(1)}, u32[]{:S(2)}, u32[]{:S(2)}) collective-permute-start(bf16[320,512]{1,0:T(8,128)(2,1)S(1)} %get-tuple-element.110), channel_id=1, source_target_pairs={{0,6},{1,7},{2,4},{3,5},{4,2},{5,3},{6,0},{7,1},{8,14},{9,15},{10,... | collective-permute-start | bytes 983048 | tf_op jit(solution)/shard_map/ppermute | solution.py:544
  73.4 12.6 %collective-permute-start.13 = (bf16[512,512]{1,0:T(8,128)(2,1)S(1)}, bf16[512,512]{1,0:T(8,128)(2,1)S(1)}, u32[]{:S(2)}, u32[]{:S(2)}) collective-permute-start(bf16[512,512]{1,0:T(8,128)(2,1)S(1)} %copy-done.26), channel_id=1, source_target_pairs={{0,2},{1,3},{2,0},{3,1},{4,6},{5,7},{6,4},{7,5},{8,10},{9,11},{10,... | collective-permute-start | bytes 1572872 | tf_op jit(solution)/shard_map/ppermute | solution.py:544
  74.8 11.1 %collective-permute-start.10 = (bf16[80,512]{1,0:T(8,128)(2,1)S(1)}, bf16[80,512]{1,0:T(8,128)(2,1)S(1)}, u32[]{:S(2)}, u32[]{:S(2)}) collective-permute-start(bf16[80,512]{1,0:T(8,128)(2,1)S(1)} %get-tuple-element.120), channel_id=1, source_target_pairs={{0,8},{1,9},{2,10},{3,11},{4,12},{5,13},{6,14},{7,15},{8,0},{9,1},... | collective-permute-start | bytes 245768 | tf_op jit(solution)/shard_map/ppermute | solution.py:544
  76.1 9.8 %collective-permute-start.11 = (bf16[80,512]{1,0:T(8,128)(2,1)S(1)}, bf16[80,512]{1,0:T(8,128)(2,1)S(1)}, u32[]{:S(2)}, u32[]{:S(2)}) collective-permute-start(bf16[80,512]{1,0:T(8,128)(2,1)S(1)} %get-tuple-element.121), channel_id=1, source_target_pairs={{0,16},{1,17},{2,18},{3,19},{4,20},{5,21},{6,22},{7,23},{8,24},{9,... | collective-permute-start | bytes 245768 | tf_op jit(solution)/shard_map/ppermute | solution.py:544
  78.4 7.5 %collective-permute-start.12 = (bf16[80,512]{1,0:T(8,128)(2,1)S(1)}, bf16[80,512]{1,0:T(8,128)(2,1)S(1)}, u32[]{:S(2)}, u32[]{:S(2)}) collective-permute-start(bf16[80,512]{1,0:T(8,128)(2,1)S(1)} %get-tuple-element.122), channel_id=1, source_target_pairs={{0,24},{1,25},{2,26},{3,27},{4,28},{5,29},{6,30},{7,31},{8,16},{9,... | collective-permute-start | bytes 245768 | tf_op jit(solution)/shard_map/ppermute | solution.py:544
  91.6 16.5 %collective-permute-start.15 = (bf16[512,512]{1,0:T(8,128)(2,1)S(1)}, bf16[512,512]{1,0:T(8,128)(2,1)S(1)}, u32[]{:S(2)}, u32[]{:S(2)}) collective-permute-start(bf16[512,512]{1,0:T(8,128)(2,1)S(1)} %relay.2), channel_id=1, source_target_pairs={{0,1},{1,0},{2,3},{3,2},{4,5},{5,4},{6,7},{7,6},{8,9},{9,8},{10,11... | collective-permute-start | bytes 1572872 | tf_op jit(solution)/shard_map/ppermute | solution.py:544
  93.1 16.0 %collective-permute-start.18 = (bf16[800,128]{1,0:T(8,128)(2,1)}, bf16[800,128]{1,0:T(8,128)(2,1)S(1)}, u32[]{:S(2)}, u32[]{:S(2)}) collective-permute-start(bf16[800,128]{1,0:T(8,128)(2,1)} %get-tuple-element.135), channel_id=1, source_target_pairs={{0,2},{1,3},{2,0},{3,1},{4,6},{5,7},{6,4},{7,5},{8,10},{9,11},{10,... | collective-permute-start | bytes 614408 | tf_op jit(solution)/shard_map/ppermute | solution.py:544
  94.4 14.7 %collective-permute-start.19 = (bf16[800,128]{1,0:T(8,128)(2,1)}, bf16[800,128]{1,0:T(8,128)(2,1)S(1)}, u32[]{:S(2)}, u32[]{:S(2)}) collective-permute-start(bf16[800,128]{1,0:T(8,128)(2,1)} %get-tuple-element.136), channel_id=1, source_target_pairs={{0,4},{1,5},{2,6},{3,7},{4,0},{5,1},{6,2},{7,3},{8,12},{9,13},{10,... | collective-permute-start | bytes 614408 | tf_op jit(solution)/shard_map/ppermute | solution.py:544
  95.6 13.5 %collective-permute-start.20 = (bf16[800,128]{1,0:T(8,128)(2,1)}, bf16[800,128]{1,0:T(8,128)(2,1)S(1)}, u32[]{:S(2)}, u32[]{:S(2)}) collective-permute-start(bf16[800,128]{1,0:T(8,128)(2,1)} %get-tuple-element.137), channel_id=1, source_target_pairs={{0,6},{1,7},{2,4},{3,5},{4,2},{5,3},{6,0},{7,1},{8,14},{9,15},{10,... | collective-permute-start | bytes 614408 | tf_op jit(solution)/shard_map/ppermute | solution.py:544
  95.9 9.6 %collective-permute-start.17 = (bf16[160,512]{1,0:T(8,128)(2,1)S(1)}, bf16[160,512]{1,0:T(8,128)(2,1)S(1)}, u32[]{:S(2)}, u32[]{:S(2)}) collective-permute-start(bf16[160,512]{1,0:T(8,128)(2,1)S(1)} %join.6.refs_0_), channel_id=1, source_target_pairs={{0,16},{1,17},{2,18},{3,19},{4,20},{5,21},{6,22},{7,23},{8,24},{9,... | collective-permute-start | bytes 491528 | tf_op jit(solution)/shard_map/ppermute | solution.py:544
  109.8 10.6 %collective-permute-start.29 = (bf16[320,512]{1,0:T(8,128)(2,1)S(1)}, bf16[320,512]{1,0:T(8,128)(2,1)S(1)}, u32[]{:S(2)}, u32[]{:S(2)}) collective-permute-start(bf16[320,512]{1,0:T(8,128)(2,1)S(1)} %join.7.refs_0_), channel_id=1, source_target_pairs={{0,2},{1,3},{2,0},{3,1},{4,6},{5,7},{6,4},{7,5},{8,10},{9,11},{10,... | collective-permute-start | bytes 983048 | tf_op jit(solution)/shard_map/ppermute | solution.py:544
  111.0 4.5 %collective-permute-start.22 = (bf16[200,128]{1,0:T(8,128)(2,1)S(1)}, bf16[200,128]{1,0:T(8,128)(2,1)S(1)}, u32[]{:S(2)}, u32[]{:S(2)}) collective-permute-start(bf16[200,128]{1,0:T(8,128)(2,1)S(1)} %get-tuple-element.141), channel_id=1, source_target_pairs={{0,8},{1,9},{2,10},{3,11},{4,12},{5,13},{6,14},{7,15},{8,0},{9,1},... | collective-permute-start | bytes 153608 | tf_op jit(solution)/shard_map/ppermute | solution.py:544
  112.4 5.1 %collective-permute-start.23 = (bf16[200,128]{1,0:T(8,128)(2,1)S(1)}, bf16[200,128]{1,0:T(8,128)(2,1)S(1)}, u32[]{:S(2)}, u32[]{:S(2)}) collective-permute-start(bf16[200,128]{1,0:T(8,128)(2,1)S(1)} %get-tuple-element.142), channel_id=1, source_target_pairs={{0,16},{1,17},{2,18},{3,19},{4,20},{5,21},{6,22},{7,23},{8,24},{9,... | collective-permute-start | bytes 153608 | tf_op jit(solution)/shard_map/ppermute | solution.py:544
  115.5 4.9 %collective-permute-start.24 = (bf16[200,128]{1,0:T(8,128)(2,1)S(1)}, bf16[200,128]{1,0:T(8,128)(2,1)S(1)}, u32[]{:S(2)}, u32[]{:S(2)}) collective-permute-start(bf16[200,128]{1,0:T(8,128)(2,1)S(1)} %get-tuple-element.143), channel_id=1, source_target_pairs={{0,24},{1,25},{2,26},{3,27},{4,28},{5,29},{6,30},{7,31},{8,16},{9,... | collective-permute-start | bytes 153608 | tf_op jit(solution)/shard_map/ppermute | solution.py:544
  120.4 16.0 %collective-permute-start.30 = (bf16[640,512]{1,0:T(8,128)(2,1)S(1)}, bf16[640,512]{1,0:T(8,128)(2,1)S(1)}, u32[]{:S(2)}, u32[]{:S(2)}) collective-permute-start(bf16[640,512]{1,0:T(8,128)(2,1)S(1)} %join.9.refs_0_), channel_id=1, source_target_pairs={{0,4},{1,5},{2,6},{3,7},{4,0},{5,1},{6,2},{7,3},{8,12},{9,13},{10,... | collective-permute-start | bytes 1966088 | tf_op jit(solution)/shard_map/ppermute | solution.py:544
  121.7 11.0 %collective-permute-start.21 = (bf16[512,512]{1,0:T(8,128)(2,1)}, bf16[512,512]{1,0:T(8,128)(2,1)S(1)}, u32[]{:S(2)}, u32[]{:S(2)}) collective-permute-start(bf16[512,512]{1,0:T(8,128)(2,1)} %get-tuple-element.139), channel_id=1, source_target_pairs={{0,2},{1,3},{2,0},{3,1},{4,6},{5,7},{6,4},{7,5},{8,10},{9,11},{10,... | collective-permute-start | bytes 1572872 | tf_op jit(solution)/shard_map/ppermute | solution.py:544
  122.1 10.6 %collective-permute-start.25 = (bf16[200,128]{1,0:T(8,128)(2,1)S(1)}, bf16[200,128]{1,0:T(8,128)(2,1)S(1)}, u32[]{:S(2)}, u32[]{:S(2)}) collective-permute-start(bf16[200,128]{1,0:T(8,128)(2,1)S(1)} %add.38.refs_0_), channel_id=1, source_target_pairs={{0,8},{1,9},{2,10},{3,11},{4,12},{5,13},{6,14},{7,15},{8,0},{9,1},... | collective-permute-start | bytes 153608 | tf_op jit(solution)/shard_map/ppermute | solution.py:544
  122.5 10.2 %collective-permute-start.26 = (bf16[200,128]{1,0:T(8,128)(2,1)S(1)}, bf16[200,128]{1,0:T(8,128)(2,1)S(1)}, u32[]{:S(2)}, u32[]{:S(2)}) collective-permute-start(bf16[200,128]{1,0:T(8,128)(2,1)S(1)} %add.38.refs_0_), channel_id=1, source_target_pairs={{0,16},{1,17},{2,18},{3,19},{4,20},{5,21},{6,22},{7,23},{8,24},{9,... | collective-permute-start | bytes 153608 | tf_op jit(solution)/shard_map/ppermute | solution.py:544
  125.6 7.1 %collective-permute-start.27 = (bf16[200,128]{1,0:T(8,128)(2,1)S(1)}, bf16[200,128]{1,0:T(8,128)(2,1)S(1)}, u32[]{:S(2)}, u32[]{:S(2)}) collective-permute-start(bf16[200,128]{1,0:T(8,128)(2,1)S(1)} %add.38.refs_0_), channel_id=1, source_target_pairs={{0,24},{1,25},{2,26},{3,27},{4,28},{5,29},{6,30},{7,31},{8,16},{9,... | collective-permute-start | bytes 153608 | tf_op jit(solution)/shard_map/ppermute | solution.py:544
  132.8 7.7 %collective-permute-start.28 = (bf16[512,512]{1,0:T(8,128)(2,1)S(1)}, bf16[512,512]{1,0:T(8,128)(2,1)S(1)}, u32[]{:S(2)}, u32[]{:S(2)}) collective-permute-start(bf16[512,512]{1,0:T(8,128)(2,1)S(1)} %relay.3), channel_id=1, source_target_pairs={{0,1},{1,0},{2,3},{3,2},{4,5},{5,4},{6,7},{7,6},{8,9},{9,8},{10,11... | collective-permute-start | bytes 1572872 | tf_op jit(solution)/shard_map/ppermute | solution.py:544
  136.6 14.5 %collective-permute-start.31 = (bf16[1280,512]{1,0:T(8,128)(2,1)S(1)}, bf16[1280,512]{1,0:T(8,128)(2,1)S(1)}, u32[]{:S(2)}, u32[]{:S(2)}) collective-permute-start(bf16[1280,512]{1,0:T(8,128)(2,1)S(1)} %join.10.own_ref), channel_id=1, source_target_pairs={{0,1},{1,0},{2,3},{3,2},{4,5},{5,4},{6,7},{7,6},{8,9},{9,8},{10,11... | collective-permute-start | bytes 3932168 | tf_op jit(solution)/shard_map/ppermute | solution.py:544
  137.8 6.7 %collective-permute-start.32 = (bf16[800,128]{1,0:T(8,128)(2,1)S(1)}, bf16[800,128]{1,0:T(8,128)(2,1)S(1)}, u32[]{:S(2)}, u32[]{:S(2)}) collective-permute-start(bf16[800,128]{1,0:T(8,128)(2,1)S(1)} %join.8.refs_0_), channel_id=1, source_target_pairs={{0,2},{1,3},{2,0},{3,1},{4,6},{5,7},{6,4},{7,5},{8,10},{9,11},{10,... | collective-permute-start | bytes 614408 | tf_op jit(solution)/shard_map/ppermute | solution.py:544
  138.2 6.3 %collective-permute-start.33 = (bf16[800,128]{1,0:T(8,128)(2,1)S(1)}, bf16[800,128]{1,0:T(8,128)(2,1)S(1)}, u32[]{:S(2)}, u32[]{:S(2)}) collective-permute-start(bf16[800,128]{1,0:T(8,128)(2,1)S(1)} %join.8.refs_0_), channel_id=1, source_target_pairs={{0,4},{1,5},{2,6},{3,7},{4,0},{5,1},{6,2},{7,3},{8,12},{9,13},{10,... | collective-permute-start | bytes 614408 | tf_op jit(solution)/shard_map/ppermute | solution.py:544
  139.4 10.3 %collective-permute-start.34 = (bf16[800,128]{1,0:T(8,128)(2,1)S(1)}, bf16[800,128]{1,0:T(8,128)(2,1)S(1)}, u32[]{:S(2)}, u32[]{:S(2)}) collective-permute-start(bf16[800,128]{1,0:T(8,128)(2,1)S(1)} %join.8.refs_0_), channel_id=1, source_target_pairs={{0,6},{1,7},{2,4},{3,5},{4,2},{5,3},{6,0},{7,1},{8,14},{9,15},{10,... | collective-permute-start | bytes 614408 | tf_op jit(solution)/shard_map/ppermute | solution.py:544
  (31 other events, 374.6 us)

commit v2 on v1

--- a/solution.py
+++ b/solution.py
@@ -651,19 +651,19 @@
     first = join_call(after(place_deep & 1, own), [first] + first_z)
     first_z = spread(first, 4, 2)
     second = swap_parts(parts, 1)
+    own, *parts = add_call(place_deep, 4, [own] + second, F32)
     out_near = send_xor(relay_call(after(out_near, own), out_far), 1)
-    output = arrive_call(blk, out, out_near, out_far, BF16)
-    own, *parts = add_call(after(place_deep, output), 4, [own] + second, F32)
     first = join_call(place_deep >> 1, [first] + first_z)
     first, gin_far = lax.optimization_barrier((first, gin_far, own))[:2]
     gin_far = send_xor(gin_far, 2)
     (second,) = add_call(0, 1, [own] + swap_parts(parts, 3), BF16)
     first = join_call(after(place_plane & 1, second), [first] + spread(first, 1, 2))
-    second = join_call(after(place_deep, gin_far), [second] + spread(second, 3, 4))
+    second = join_call(place_deep, [second] + spread(second, 3, 4))
     first = join_call(after(place_plane >> 1, second), [first] + spread(first, 2, 2))
     gin_near = send_xor(relay_call(after(gin_near, second), gin_far), 1)
+    output = arrive_call(after(blk, second), out, out_near, out_far, BF16)
     input_grad = arrive_call(blk, gin, gin_near, gin_far, F32)
-    second = join_call(after(place_plane, input_grad), [second] + spread(second, 1, 4))
+    second = join_call(after(place_plane, output, input_grad), [second] + spread(second, 1, 4))
     gw_down, gw_up, gw_o = finish_call(
         finish_mid_kernel, core, first, send_xor(first, 1), [w_down.shape, w_up.shape, w_o.shape], "finish_mid"
     )

time: 156 us -> 151 us (0.968)
  waiting for transfers between devices: 42.3 us -> 36.2 us
  Pallas kernels: 64.9 us -> 66.5 us
    ppermute x36, waiting for transfers between devices: 42.3 us -> 36.2 us  [send_xor(): return lax.ppermute(values, BOTH, [(i, i ^ flip) for i in range(count)])]
    unnamed x54 -> x46, local copies, waits for them, and re-layouts: 3.27 us -> 1.09 us
    pallas_call x2, Pallas kernels: 0.07 us -> 1.65 us  [relay_call(): pl.pallas_call(relay_kernel, grid=(1,), in_specs=[whole(near.shape), whol...]
  transfers between devices with their start and end apart: 36 -> 36, of which waited for: 11 -> 12; matrix products, arithmetic and copies ran while one was open for 1% -> 1% of each run, Pallas kernels for 28% -> 32%
where the time goes in v2:
time: 151 us
  Pallas kernels  66.5 us (44%)
  starting transfers between devices  42.7 us (28%)
  waiting for transfers between devices  36.2 us (24%)
  local copies, waits for them, and re-layouts  4.44 us (3%)
    ppermute x36, starting transfers between devices, send_xor(): return lax.ppermute(values, BOTH, [(i, i ^ flip) for i in range(count)])  42.7 us
    ppermute x36, waiting for transfers between devices, send_xor(): return lax.ppermute(values, BOTH, [(i, i ^ flip) for i in range(count)])  36.2 us
    pallas_call x1, Pallas kernels, backward_call(): pl.pallas_call(functools.partial(backward_kernel, first), grid=(count,),...  17.1 us
    pallas_call x1, Pallas kernels, forward_call(): pl.pallas_call(forward_kernel, grid=(1,), in_specs=[SMEM_SPEC, SMEM_SPEC]...  14.4 us
    pallas_call x1, Pallas kernels, middle_call(): pl.pallas_call(middle_kernel, grid=(1,), in_specs=[SMEM_SPEC, SMEM_SPEC,...  13.6 us
    pallas_call x1, Pallas kernels, last_call(): pl.pallas_call(last_kernel, grid=(1,), in_specs=[SMEM_SPEC, SMEM_SPEC] +...  7.46 us
    pallas_call x2, Pallas kernels, finish_call(): pl.pallas_call(kernel, grid=(1,), in_specs=[SMEM_SPEC, whole(own.shape),...  4.79 us
    pallas_call x6, Pallas kernels, add_call(): pl.pallas_call(add_kernel, grid=(1,), in_specs=[SMEM_SPEC] + [whole(a.sha...  3.72 us
  transfers between devices with their start and end apart: 36, of which 12 were waited for; matrix products, arithmetic and copies ran while one was open for 1% of the time, Pallas kernels for 32%

profile of v2, /device:TPU:1, one launch (start us, length us, event | category | flops | bytes accessed | tf_op | source)
XLA Modules:
  0.0 151.2 jit_solution(14955651080130983216)
XLA Ops:
  0.7 2.1 %dynamic-slice_bitcast_fusion.4 = (bf16[256,512]{1,0:T(8,128)(2,1)S(1)}, bf16[256,512]{1,0:T(8,128)(2,1)}, bf16[256,512]{1,0:T(8,128)(2,1)S(1)}, bf16[256,512]{1,0:T(8,128)(2,1)S(1)}) fusion(bf16[4,256,512]{2,1,0:T(8,128)(2,1)} %param.15, s32[]{:T(128)S(6)} %select_n.22, s32[]{:T(128)S(6)} %select_n.20, s32[]{:T(128)S(6)} %select_n.19, s32[]{:T(128)S(6)} %select_n.21), kind=kLoop, calls=%fused_computation.4 | loop fusion | bytes 2097168 | tf_op jit(solution)/shard_map/jit(dynamic_index_in_dim)/squeeze | solution.py:626
  2.9 2.7 %collective-permute-start.1 = (bf16[256,512]{1,0:T(8,128)(2,1)S(1)}, bf16[256,512]{1,0:T(8,128)(2,1)S(1)}, u32[]{:S(2)}, u32[]{:S(2)}) collective-permute-start(bf16[256,512]{1,0:T(8,128)(2,1)S(1)} %get-tuple-element.167), channel_id=1, source_target_pairs={{0,2},{1,3},{2,0},{3,1},{4,6},{5,7},{6,4},{7,5},{8,10},{9,11},{10,... | collective-permute-start | bytes 786440 | tf_op jit(solution)/shard_map/ppermute | solution.py:544
  7.0 5.2 %collective-permute-done.1.x2_ref = bf16[256,512]{1,0:T(8,128)(2,1)S(1)} collective-permute-done((bf16[256,512]{1,0:T(8,128)(2,1)S(1)}, bf16[256,512]{1,0:T(8,128)(2,1)S(1)}, u32[]{:S(2)}, u32[]{:S(2)}) %collective-permute-start.1) | collective-permute-done | bytes 262176 | tf_op jit(solution)/shard_map/ppermute | solution.py:544
  12.2 5.6 %collective-permute-done.2.x3_ref = bf16[256,512]{1,0:T(8,128)(2,1)S(1)} collective-permute-done((bf16[256,512]{1,0:T(8,128)(2,1)S(1)}, bf16[256,512]{1,0:T(8,128)(2,1)S(1)}, u32[]{:S(2)}, u32[]{:S(2)}) %collective-permute-start.2) | collective-permute-done | bytes 262176 | tf_op jit(solution)/shard_map/ppermute | solution.py:544
  20.1 14.4 %forward.1 = (bf16[1024,512]{1,0:T(8,128)(2,1)S(1)}, bf16[4,1024,128]{2,1,0:T(8,128)(2,1)}, bf16[4,1024,128]{2,1,0:T(8,128)(2,1)}, bf16[4,1024,128]{2,1,0:T(8,12...) custom-call(s32[8]{0:T(128)S(1)} %fusion.ends_ref, ...), custom_call_target="tpu_custom_call" | custom-call | flops 20000000000 | bytes 10000000 | tf_op jit(solution)/shard_map/forward/pallas_call | solution.py:161
  34.6 13.6 %middle.1 = (bf16[256,512]{1,0:T(8,128)(2,1)}, bf16[256,512]{1,0:T(8,128)(2,1)}, bf16[512,512]{1,0:T(8,128)(2,1)}, f32[1024,512]{1,0:T(8,128)}, bf16[4,1024,128]...) custom-call(s32[1]{0:T(128)} %bitcast.2.core_ref.refs_0_, ...), custom_call_target="tpu_custom_call" | custom-call | flops 15000000512 | bytes 20000000 | tf_op jit(solution)/shard_map/middle/pallas_call | solution.py:316
  48.3 3.3 %collective-permute-done.6.refs_1_ = bf16[1280,512]{1,0:T(8,128)(2,1)} collective-permute-done((bf16[1280,512]{1,0:T(8,128)(2,1)}, bf16[1280,512]{1,0:T(8,128)(2,1)}, u32[]{:S(2)}, u32[]{:S(2)}) %collective-permute-start.6) | collective-permute-done | bytes 1310752 | tf_op jit(solution)/shard_map/ppermute | solution.py:544
  51.6 1.6 %add.33 = (f32[320,512]{1,0:T(8,128)S(1)}, bf16[320,512]{1,0:T(8,128)(2,1)S(1)}, bf16[320,512]{1,0:T(8,128)(2,1)S(1)}, bf16[320,512]{1,0:T(8,128)(2,1)S(1)}) custom-call(s32[4]{0:T(128)S(1)} %broadcast_in_dim.62.place_ref, f32[1280,512]{1,0:T(8,128)S(1)} %get-tuple-element.93.refs_0_, bf16[1280,512]{1,0:T(8,128)(2,1)} %collective-permute-done.6.refs_1_), custom_call_target="tpu_custom_call" | custom-call | flops 100000000 | bytes 4000000 | tf_op jit(solution)/shard_map/add/pallas_call | solution.py:563
  53.2 1.4 collective-permute-start.7
  55.9 17.1 %backward.1 = (bf16[4,1024,128]{2,1,0:T(8,128)(2,1)}, bf16[4,1024,128]{2,1,0:T(8,128)(2,1)}, bf16[4,1024,128]{2,1,0:T(8,128)(2,1)}) custom-call(s32[8]{0:T(128)S(1)} %fusion.ends_ref, bf16[4,1024,128]{2,1,0:T(8,128)(2,1)} %get-tuple-element.97.q_ref, bf16[4,1024,128]{2,1,0:T(8,128)(2,1)} %get-tuple-element.98.k_ref, ...), custom_call_target="tpu_custom_call" | custom-call | flops 4000000000 | bytes 400000 | tf_op jit(solution)/shard_map/backward/pallas_call | solution.py:411
  73.8 1.4 collective-permute-start.13
  75.2 1.3 collective-permute-start.10
  76.5 2.3 %collective-permute-start.11 = (bf16[80,512]{1,0:T(8,128)(2,1)S(1)}, bf16[80,512]{1,0:T(8,128)(2,1)S(1)}, u32[]{:S(2)}, u32[]{:S(2)}) collective-permute-start(bf16[80,512]{1,0:T(8,128)(2,1)S(1)} %get-tuple-element.118), channel_id=1, source_target_pairs={{0,16},{1,17},{2,18},{3,19},{4,20},{5,21},{6,22},{7,23},{8,24},{9,... | collective-permute-start | bytes 245768 | tf_op jit(solution)/shard_map/ppermute | solution.py:544
  78.8 7.5 %last.1 = (bf16[256,512]{1,0:T(8,128)(2,1)}, bf16[256,512]{1,0:T(8,128)(2,1)}, bf16[512,512]{1,0:T(8,128)(2,1)}, f32[3200,128]{1,0:T(8,128)S(1)}, bf16[3200,128]{1,0:T(8,128)(2,1)S(1)}) custom-call(s32[1]{0:T(128)} %bitcast.2.core_ref.refs_0_, s32[1]{0:T(128)} %bitcast.blk_ref.refs_1_, bf16[4,1024,128]{2,1,0:T(8,128)(2,1)} %get-tuple-element.103.refs_2_, ...), custom_call_target="tpu_custom_call" | custom-call | flops 1000000000 | bytes 100000 | tf_op jit(solution)/shard_map/last/pallas_call | solution.py:464
  86.4 2.1 %collective-permute-start.14 = (bf16[3200,128]{1,0:T(8,128)(2,1)S(1)}, bf16[3200,128]{1,0:T(8,128)(2,1)S(1)}, u32[]{:S(2)}, u32[]{:S(2)}) collective-permute-start(bf16[3200,128]{1,0:T(8,128)(2,1)S(1)} %get-tuple-element.122), channel_id=1, source_target_pairs={{0,1},{1,0},{2,3},{3,2},{4,5},{5,4},{6,7},{7,6},{8,9},{9,8},{10,11... | collective-permute-start | bytes 2457608 | tf_op jit(solution)/shard_map/ppermute | solution.py:544
  93.9 2.2 %collective-permute-start.26 = (bf16[160,512]{1,0:T(8,128)(2,1)S(1)}, bf16[160,512]{1,0:T(8,128)(2,1)S(1)}, u32[]{:S(2)}, u32[]{:S(2)}) collective-permute-start(bf16[160,512]{1,0:T(8,128)(2,1)S(1)} %join.7.refs_0_), channel_id=1, source_target_pairs={{0,16},{1,17},{2,18},{3,19},{4,20},{5,21},{6,22},{7,23},{8,24},{9,... | collective-permute-start | bytes 491528 | tf_op jit(solution)/shard_map/ppermute | solution.py:544
  96.1 7.4 %collective-permute-done.26.refs_1_ = bf16[160,512]{1,0:T(8,128)(2,1)S(1)} collective-permute-done((bf16[160,512]{1,0:T(8,128)(2,1)S(1)}, bf16[160,512]{1,0:T(8,128)(2,1)S(1)}, u32[]{:S(2)}, u32[]{:S(2)}) %collective-permute-start.26) | collective-permute-done | bytes 163872 | tf_op jit(solution)/shard_map/ppermute | solution.py:544
  105.2 1.5 collective-permute-start.18
  106.7 3.1 %collective-permute-start.19 = (bf16[200,128]{1,0:T(8,128)(2,1)S(1)}, bf16[200,128]{1,0:T(8,128)(2,1)S(1)}, u32[]{:S(2)}, u32[]{:S(2)}) collective-permute-start(bf16[200,128]{1,0:T(8,128)(2,1)S(1)} %get-tuple-element.129), channel_id=1, source_target_pairs={{0,16},{1,17},{2,18},{3,19},{4,20},{5,21},{6,22},{7,23},{8,24},{9,... | collective-permute-start | bytes 153608 | tf_op jit(solution)/shard_map/ppermute | solution.py:544
  109.8 2.0 %collective-permute-done.19.refs_2_ = bf16[200,128]{1,0:T(8,128)(2,1)S(1)} collective-permute-done((bf16[200,128]{1,0:T(8,128)(2,1)S(1)}, bf16[200,128]{1,0:T(8,128)(2,1)S(1)}, u32[]{:S(2)}, u32[]{:S(2)}) %collective-permute-start.19) | collective-permute-done | bytes 51232 | tf_op jit(solution)/shard_map/ppermute | solution.py:544
  111.9 2.8 %collective-permute-done.20.refs_3_ = bf16[200,128]{1,0:T(8,128)(2,1)S(1)} collective-permute-done((bf16[200,128]{1,0:T(8,128)(2,1)S(1)}, bf16[200,128]{1,0:T(8,128)(2,1)S(1)}, u32[]{:S(2)}, u32[]{:S(2)}) %collective-permute-start.20) | collective-permute-done | bytes 51232 | tf_op jit(solution)/shard_map/ppermute | solution.py:544
  114.8 1.3 collective-permute-start.30
  117.1 2.9 %collective-permute-start.24 = (bf16[512,512]{1,0:T(8,128)(2,1)}, bf16[512,512]{1,0:T(8,128)(2,1)S(1)}, u32[]{:S(2)}, u32[]{:S(2)}) collective-permute-start(bf16[512,512]{1,0:T(8,128)(2,1)} %relay.2), channel_id=1, source_target_pairs={{0,1},{1,0},{2,3},{3,2},{4,5},{5,4},{6,7},{7,6},{8,9},{9,8},{10,11... | collective-permute-start | bytes 1572872 | tf_op jit(solution)/shard_map/ppermute | solution.py:544
  120.1 2.6 %collective-permute-start.22 = (bf16[200,128]{1,0:T(8,128)(2,1)S(1)}, bf16[200,128]{1,0:T(8,128)(2,1)S(1)}, u32[]{:S(2)}, u32[]{:S(2)}) collective-permute-start(bf16[200,128]{1,0:T(8,128)(2,1)S(1)} %add.38.refs_0_), channel_id=1, source_target_pairs={{0,16},{1,17},{2,18},{3,19},{4,20},{5,21},{6,22},{7,23},{8,24},{9,... | collective-permute-start | bytes 153608 | tf_op jit(solution)/shard_map/ppermute | solution.py:544
  123.5 2.3 %collective-permute-start.23 = (bf16[200,128]{1,0:T(8,128)(2,1)S(1)}, bf16[200,128]{1,0:T(8,128)(2,1)S(1)}, u32[]{:S(2)}, u32[]{:S(2)}) collective-permute-start(bf16[200,128]{1,0:T(8,128)(2,1)S(1)} %add.38.refs_0_), channel_id=1, source_target_pairs={{0,24},{1,25},{2,26},{3,27},{4,28},{5,29},{6,30},{7,31},{8,16},{9,... | collective-permute-start | bytes 153608 | tf_op jit(solution)/shard_map/ppermute | solution.py:544
  125.8 2.5 %collective-permute-done.23.refs_3_ = bf16[200,128]{1,0:T(8,128)(2,1)S(1)} collective-permute-done((bf16[200,128]{1,0:T(8,128)(2,1)S(1)}, bf16[200,128]{1,0:T(8,128)(2,1)S(1)}, u32[]{:S(2)}, u32[]{:S(2)}) %collective-permute-start.23) | collective-permute-done | bytes 51232 | tf_op jit(solution)/shard_map/ppermute | solution.py:544
  130.1 2.3 %collective-permute-start.28 = (bf16[512,512]{1,0:T(8,128)(2,1)}, bf16[512,512]{1,0:T(8,128)(2,1)}, u32[]{:S(2)}, u32[]{:S(2)}) collective-permute-start(bf16[512,512]{1,0:T(8,128)(2,1)} %relay.3), channel_id=1, source_target_pairs={{0,1},{1,0},{2,3},{3,2},{4,5},{5,4},{6,7},{7,6},{8,9},{9,8},{10,11... | collective-permute-start | bytes 1572872 | tf_op jit(solution)/shard_map/ppermute | solution.py:544
  132.6 2.0 %collective-permute-start.32 = (bf16[800,128]{1,0:T(8,128)(2,1)S(1)}, bf16[800,128]{1,0:T(8,128)(2,1)S(1)}, u32[]{:S(2)}, u32[]{:S(2)}) collective-permute-start(bf16[800,128]{1,0:T(8,128)(2,1)S(1)} %join.6.refs_0_), channel_id=1, source_target_pairs={{0,2},{1,3},{2,0},{3,1},{4,6},{5,7},{6,4},{7,5},{8,10},{9,11},{10,... | collective-permute-start | bytes 614408 | tf_op jit(solution)/shard_map/ppermute | solution.py:544
  136.9 2.5 %arrive.3 = f32[4,256,512]{2,1,0:T(8,128)} custom-call(s32[1]{0:T(128)} %bitcast.blk_ref.refs_1_, bf16[256,512]{1,0:T(8,128)(2,1)S(1)} %copy-done.8, bf16[512,512]{1,0:T(8,128)(2,1)} %collective-permute-done.28.near_ref, bf16[512,512]{1,0:T(8,128)(2,1)S(1)} %collective-permute-done.27.far_ref), custom_call_target="tpu_custom_call" | custom-call | flops 10000000 | bytes 100000 | tf_op jit(solution)/shard_map/arrive/pallas_call | solution.py:222
  140.5 4.6 %collective-permute-done.34.refs_3_ = bf16[800,128]{1,0:T(8,128)(2,1)S(1)} collective-permute-done((bf16[800,128]{1,0:T(8,128)(2,1)S(1)}, bf16[800,128]{1,0:T(8,128)(2,1)S(1)}, u32[]{:S(2)}, u32[]{:S(2)}) %collective-permute-start.34) | collective-permute-done | bytes 204832 | tf_op jit(solution)/shard_map/ppermute | solution.py:544
  146.4 2.7 %finish_mid.1 = (f32[1024,512]{1,0:T(8,128)}, f32[512,1024]{1,0:T(8,128)}, f32[512,512]{1,0:T(8,128)}) custom-call(s32[1]{0:T(128)} %bitcast.2.core_ref.refs_0_, bf16[1280,512]{1,0:T(8,128)(2,1)S(1)} %join.10.own_ref, bf16[1280,512]{1,0:T(8,128)(2,1)S(1)} %collective-permute-done.31.got_ref), custom_call_target="tpu_custom_call" | custom-call | flops 100000000 | bytes 8000000 | tf_op jit(solution)/shard_map/finish_mid/pallas_call | solution.py:530
  149.1 2.1 %finish_last.1 = (f32[512,1536]{1,0:T(8,128)}, f32[1,512]{1,0:T(1,128)}, f32[1,1024]{1,0:T(1,128)}, f32[1,512]{1,0:T(1,128)}, f32[1,512]{1,0:T(1,128)}, /*index=...) custom-call(s32[1]{0:T(128)} %bitcast.2.core_ref.refs_0_, ...), custom_call_target="tpu_custom_call" | custom-call | flops 100000000 | bytes 8000000 | tf_op jit(solution)/shard_map/finish_last/pallas_call | solution.py:530
  (115 shorter events, 21.8 us)
Async XLA Ops:
  2.8 4.2 %collective-permute-start = (bf16[256,512]{1,0:T(8,128)(2,1)}, bf16[256,512]{1,0:T(8,128)(2,1)S(1)}, u32[]{:S(2)}, u32[]{:S(2)}) collective-permute-start(bf16[256,512]{1,0:T(8,128)(2,1)} %get-tuple-element.165), channel_id=1, source_target_pairs={{0,1},{1,0},{2,3},{3,2},{4,5},{5,4},{6,7},{7,6},{8,9},{9,8},{10,11... | collective-permute-start | bytes 786440 | tf_op jit(solution)/shard_map/ppermute | solution.py:544
  2.9 9.4 %collective-permute-start.1 = (bf16[256,512]{1,0:T(8,128)(2,1)S(1)}, bf16[256,512]{1,0:T(8,128)(2,1)S(1)}, u32[]{:S(2)}, u32[]{:S(2)}) collective-permute-start(bf16[256,512]{1,0:T(8,128)(2,1)S(1)} %get-tuple-element.167), channel_id=1, source_target_pairs={{0,2},{1,3},{2,0},{3,1},{4,6},{5,7},{6,4},{7,5},{8,10},{9,11},{10,... | collective-permute-start | bytes 786440 | tf_op jit(solution)/shard_map/ppermute | solution.py:544
  5.5 12.3 %collective-permute-start.2 = (bf16[256,512]{1,0:T(8,128)(2,1)S(1)}, bf16[256,512]{1,0:T(8,128)(2,1)S(1)}, u32[]{:S(2)}, u32[]{:S(2)}) collective-permute-start(bf16[256,512]{1,0:T(8,128)(2,1)S(1)} %get-tuple-element.164), channel_id=1, source_target_pairs={{0,3},{1,2},{2,1},{3,0},{4,7},{5,6},{6,5},{7,4},{8,11},{9,10},{10,... | collective-permute-start | bytes 786440 | tf_op jit(solution)/shard_map/ppermute | solution.py:544
  17.8 16.7 %collective-permute-start.3 = (bf16[256,512]{1,0:T(8,128)(2,1)S(1)}, bf16[256,512]{1,0:T(8,128)(2,1)S(1)}, u32[]{:S(2)}, u32[]{:S(2)}) collective-permute-start(bf16[256,512]{1,0:T(8,128)(2,1)S(1)} %get-tuple-element.90), channel_id=1, source_target_pairs={{0,1},{1,0},{2,3},{3,2},{4,5},{5,4},{6,7},{7,6},{8,9},{9,8},{10,11... | collective-permute-start | bytes 786440 | tf_op jit(solution)/shard_map/ppermute | solution.py:544
  18.2 16.3 %collective-permute-start.4 = (bf16[256,512]{1,0:T(8,128)(2,1)S(1)}, bf16[256,512]{1,0:T(8,128)(2,1)S(1)}, u32[]{:S(2)}, u32[]{:S(2)}) collective-permute-start(bf16[256,512]{1,0:T(8,128)(2,1)S(1)} %get-tuple-element.91), channel_id=1, source_target_pairs={{0,2},{1,3},{2,0},{3,1},{4,6},{5,7},{6,4},{7,5},{8,10},{9,11},{10,... | collective-permute-start | bytes 786440 | tf_op jit(solution)/shard_map/ppermute | solution.py:544
  19.5 15.0 %collective-permute-start.5 = (bf16[256,512]{1,0:T(8,128)(2,1)S(1)}, bf16[256,512]{1,0:T(8,128)(2,1)S(1)}, u32[]{:S(2)}, u32[]{:S(2)}) collective-permute-start(bf16[256,512]{1,0:T(8,128)(2,1)S(1)} %get-tuple-element.92), channel_id=1, source_target_pairs={{0,3},{1,2},{2,1},{3,0},{4,7},{5,6},{6,5},{7,4},{8,11},{9,10},{10,... | collective-permute-start | bytes 786440 | tf_op jit(solution)/shard_map/ppermute | solution.py:544
  53.2 19.8 %collective-permute-start.7 = (bf16[320,512]{1,0:T(8,128)(2,1)S(1)}, bf16[320,512]{1,0:T(8,128)(2,1)S(1)}, u32[]{:S(2)}, u32[]{:S(2)}) collective-permute-start(bf16[320,512]{1,0:T(8,128)(2,1)S(1)} %get-tuple-element.105), channel_id=1, source_target_pairs={{0,2},{1,3},{2,0},{3,1},{4,6},{5,7},{6,4},{7,5},{8,10},{9,11},{10,... | collective-permute-start | bytes 983048 | tf_op jit(solution)/shard_map/ppermute | solution.py:544
  54.6 18.4 %collective-permute-start.8 = (bf16[320,512]{1,0:T(8,128)(2,1)S(1)}, bf16[320,512]{1,0:T(8,128)(2,1)S(1)}, u32[]{:S(2)}, u32[]{:S(2)}) collective-permute-start(bf16[320,512]{1,0:T(8,128)(2,1)S(1)} %get-tuple-element.106), channel_id=1, source_target_pairs={{0,4},{1,5},{2,6},{3,7},{4,0},{5,1},{6,2},{7,3},{8,12},{9,13},{10,... | collective-permute-start | bytes 983048 | tf_op jit(solution)/shard_map/ppermute | solution.py:544
  55.8 17.2 %collective-permute-start.9 = (bf16[320,512]{1,0:T(8,128)(2,1)S(1)}, bf16[320,512]{1,0:T(8,128)(2,1)S(1)}, u32[]{:S(2)}, u32[]{:S(2)}) collective-permute-start(bf16[320,512]{1,0:T(8,128)(2,1)S(1)} %get-tuple-element.107), channel_id=1, source_target_pairs={{0,6},{1,7},{2,4},{3,5},{4,2},{5,3},{6,0},{7,1},{8,14},{9,15},{10,... | collective-permute-start | bytes 983048 | tf_op jit(solution)/shard_map/ppermute | solution.py:544
  73.8 12.6 %collective-permute-start.13 = (bf16[512,512]{1,0:T(8,128)(2,1)S(1)}, bf16[512,512]{1,0:T(8,128)(2,1)S(1)}, u32[]{:S(2)}, u32[]{:S(2)}) collective-permute-start(bf16[512,512]{1,0:T(8,128)(2,1)S(1)} %copy-done.22), channel_id=1, source_target_pairs={{0,2},{1,3},{2,0},{3,1},{4,6},{5,7},{6,4},{7,5},{8,10},{9,11},{10,... | collective-permute-start | bytes 1572872 | tf_op jit(solution)/shard_map/ppermute | solution.py:544
  75.2 11.1 %collective-permute-start.10 = (bf16[80,512]{1,0:T(8,128)(2,1)S(1)}, bf16[80,512]{1,0:T(8,128)(2,1)S(1)}, u32[]{:S(2)}, u32[]{:S(2)}) collective-permute-start(bf16[80,512]{1,0:T(8,128)(2,1)S(1)} %get-tuple-element.117), channel_id=1, source_target_pairs={{0,8},{1,9},{2,10},{3,11},{4,12},{5,13},{6,14},{7,15},{8,0},{9,1},... | collective-permute-start | bytes 245768 | tf_op jit(solution)/shard_map/ppermute | solution.py:544
  76.5 9.8 %collective-permute-start.11 = (bf16[80,512]{1,0:T(8,128)(2,1)S(1)}, bf16[80,512]{1,0:T(8,128)(2,1)S(1)}, u32[]{:S(2)}, u32[]{:S(2)}) collective-permute-start(bf16[80,512]{1,0:T(8,128)(2,1)S(1)} %get-tuple-element.118), channel_id=1, source_target_pairs={{0,16},{1,17},{2,18},{3,19},{4,20},{5,21},{6,22},{7,23},{8,24},{9,... | collective-permute-start | bytes 245768 | tf_op jit(solution)/shard_map/ppermute | solution.py:544
  78.8 7.5 %collective-permute-start.12 = (bf16[80,512]{1,0:T(8,128)(2,1)S(1)}, bf16[80,512]{1,0:T(8,128)(2,1)S(1)}, u32[]{:S(2)}, u32[]{:S(2)}) collective-permute-start(bf16[80,512]{1,0:T(8,128)(2,1)S(1)} %get-tuple-element.119), channel_id=1, source_target_pairs={{0,24},{1,25},{2,26},{3,27},{4,28},{5,29},{6,30},{7,31},{8,16},{9,... | collective-permute-start | bytes 245768 | tf_op jit(solution)/shard_map/ppermute | solution.py:544
  88.5 5.4 %collective-permute-start.25 = (bf16[80,512]{1,0:T(8,128)(2,1)S(1)}, bf16[80,512]{1,0:T(8,128)(2,1)S(1)}, u32[]{:S(2)}, u32[]{:S(2)}) collective-permute-start(bf16[80,512]{1,0:T(8,128)(2,1)S(1)} %add.35.refs_0_), channel_id=1, source_target_pairs={{0,8},{1,9},{2,10},{3,11},{4,12},{5,13},{6,14},{7,15},{8,0},{9,1},... | collective-permute-start | bytes 245768 | tf_op jit(solution)/shard_map/ppermute | solution.py:544
  91.2 12.3 %collective-permute-start.15 = (bf16[800,128]{1,0:T(8,128)(2,1)S(1)}, bf16[800,128]{1,0:T(8,128)(2,1)S(1)}, u32[]{:S(2)}, u32[]{:S(2)}) collective-permute-start(bf16[800,128]{1,0:T(8,128)(2,1)S(1)} %get-tuple-element.124), channel_id=1, source_target_pairs={{0,2},{1,3},{2,0},{3,1},{4,6},{5,7},{6,4},{7,5},{8,10},{9,11},{10,... | collective-permute-start | bytes 614408 | tf_op jit(solution)/shard_map/ppermute | solution.py:544
  92.3 11.2 %collective-permute-start.16 = (bf16[800,128]{1,0:T(8,128)(2,1)S(1)}, bf16[800,128]{1,0:T(8,128)(2,1)S(1)}, u32[]{:S(2)}, u32[]{:S(2)}) collective-permute-start(bf16[800,128]{1,0:T(8,128)(2,1)S(1)} %get-tuple-element.125), channel_id=1, source_target_pairs={{0,4},{1,5},{2,6},{3,7},{4,0},{5,1},{6,2},{7,3},{8,12},{9,13},{10,... | collective-permute-start | bytes 614408 | tf_op jit(solution)/shard_map/ppermute | solution.py:544
  93.5 10.0 %collective-permute-start.17 = (bf16[800,128]{1,0:T(8,128)(2,1)S(1)}, bf16[800,128]{1,0:T(8,128)(2,1)S(1)}, u32[]{:S(2)}, u32[]{:S(2)}) collective-permute-start(bf16[800,128]{1,0:T(8,128)(2,1)S(1)} %get-tuple-element.126), channel_id=1, source_target_pairs={{0,6},{1,7},{2,4},{3,5},{4,2},{5,3},{6,0},{7,1},{8,14},{9,15},{10,... | collective-permute-start | bytes 614408 | tf_op jit(solution)/shard_map/ppermute | solution.py:544
  93.9 9.6 %collective-permute-start.26 = (bf16[160,512]{1,0:T(8,128)(2,1)S(1)}, bf16[160,512]{1,0:T(8,128)(2,1)S(1)}, u32[]{:S(2)}, u32[]{:S(2)}) collective-permute-start(bf16[160,512]{1,0:T(8,128)(2,1)S(1)} %join.7.refs_0_), channel_id=1, source_target_pairs={{0,16},{1,17},{2,18},{3,19},{4,20},{5,21},{6,22},{7,23},{8,24},{9,... | collective-permute-start | bytes 491528 | tf_op jit(solution)/shard_map/ppermute | solution.py:544
  104.2 10.5 %collective-permute-start.29 = (bf16[320,512]{1,0:T(8,128)(2,1)S(1)}, bf16[320,512]{1,0:T(8,128)(2,1)S(1)}, u32[]{:S(2)}, u32[]{:S(2)}) collective-permute-start(bf16[320,512]{1,0:T(8,128)(2,1)S(1)} %join.8.refs_0_), channel_id=1, source_target_pairs={{0,2},{1,3},{2,0},{3,1},{4,6},{5,7},{6,4},{7,5},{8,10},{9,11},{10,... | collective-permute-start | bytes 983048 | tf_op jit(solution)/shard_map/ppermute | solution.py:544
  105.2 4.6 %collective-permute-start.18 = (bf16[200,128]{1,0:T(8,128)(2,1)S(1)}, bf16[200,128]{1,0:T(8,128)(2,1)S(1)}, u32[]{:S(2)}, u32[]{:S(2)}) collective-permute-start(bf16[200,128]{1,0:T(8,128)(2,1)S(1)} %get-tuple-element.128), channel_id=1, source_target_pairs={{0,8},{1,9},{2,10},{3,11},{4,12},{5,13},{6,14},{7,15},{8,0},{9,1},... | collective-permute-start | bytes 153608 | tf_op jit(solution)/shard_map/ppermute | solution.py:544
  106.7 5.2 %collective-permute-start.19 = (bf16[200,128]{1,0:T(8,128)(2,1)S(1)}, bf16[200,128]{1,0:T(8,128)(2,1)S(1)}, u32[]{:S(2)}, u32[]{:S(2)}) collective-permute-start(bf16[200,128]{1,0:T(8,128)(2,1)S(1)} %get-tuple-element.129), channel_id=1, source_target_pairs={{0,16},{1,17},{2,18},{3,19},{4,20},{5,21},{6,22},{7,23},{8,24},{9,... | collective-permute-start | bytes 153608 | tf_op jit(solution)/shard_map/ppermute | solution.py:544
  109.8 4.9 %collective-permute-start.20 = (bf16[200,128]{1,0:T(8,128)(2,1)S(1)}, bf16[200,128]{1,0:T(8,128)(2,1)S(1)}, u32[]{:S(2)}, u32[]{:S(2)}) collective-permute-start(bf16[200,128]{1,0:T(8,128)(2,1)S(1)} %get-tuple-element.130), channel_id=1, source_target_pairs={{0,24},{1,25},{2,26},{3,27},{4,28},{5,29},{6,30},{7,31},{8,16},{9,... | collective-permute-start | bytes 153608 | tf_op jit(solution)/shard_map/ppermute | solution.py:544
  114.8 17.6 %collective-permute-start.30 = (bf16[640,512]{1,0:T(8,128)(2,1)S(1)}, bf16[640,512]{1,0:T(8,128)(2,1)S(1)}, u32[]{:S(2)}, u32[]{:S(2)}) collective-permute-start(bf16[640,512]{1,0:T(8,128)(2,1)S(1)} %join.9.refs_0_), channel_id=1, source_target_pairs={{0,4},{1,5},{2,6},{3,7},{4,0},{5,1},{6,2},{7,3},{8,12},{9,13},{10,... | collective-permute-start | bytes 1966088 | tf_op jit(solution)/shard_map/ppermute | solution.py:544
  116.1 12.2 %collective-permute-start.27 = (bf16[512,512]{1,0:T(8,128)(2,1)}, bf16[512,512]{1,0:T(8,128)(2,1)S(1)}, u32[]{:S(2)}, u32[]{:S(2)}) collective-permute-start(bf16[512,512]{1,0:T(8,128)(2,1)} %get-tuple-element.142), channel_id=1, source_target_pairs={{0,2},{1,3},{2,0},{3,1},{4,6},{5,7},{6,4},{7,5},{8,10},{9,11},{10,... | collective-permute-start | bytes 1572872 | tf_op jit(solution)/shard_map/ppermute | solution.py:544
  117.1 17.7 %collective-permute-start.24 = (bf16[512,512]{1,0:T(8,128)(2,1)}, bf16[512,512]{1,0:T(8,128)(2,1)S(1)}, u32[]{:S(2)}, u32[]{:S(2)}) collective-permute-start(bf16[512,512]{1,0:T(8,128)(2,1)} %relay.2), channel_id=1, source_target_pairs={{0,1},{1,0},{2,3},{3,2},{4,5},{5,4},{6,7},{7,6},{8,9},{9,8},{10,11... | collective-permute-start | bytes 1572872 | tf_op jit(solution)/shard_map/ppermute | solution.py:544
  120.1 5.7 %collective-permute-start.22 = (bf16[200,128]{1,0:T(8,128)(2,1)S(1)}, bf16[200,128]{1,0:T(8,128)(2,1)S(1)}, u32[]{:S(2)}, u32[]{:S(2)}) collective-permute-start(bf16[200,128]{1,0:T(8,128)(2,1)S(1)} %add.38.refs_0_), channel_id=1, source_target_pairs={{0,16},{1,17},{2,18},{3,19},{4,20},{5,21},{6,22},{7,23},{8,24},{9,... | collective-permute-start | bytes 153608 | tf_op jit(solution)/shard_map/ppermute | solution.py:544
  123.5 4.8 %collective-permute-start.23 = (bf16[200,128]{1,0:T(8,128)(2,1)S(1)}, bf16[200,128]{1,0:T(8,128)(2,1)S(1)}, u32[]{:S(2)}, u32[]{:S(2)}) collective-permute-start(bf16[200,128]{1,0:T(8,128)(2,1)S(1)} %add.38.refs_0_), channel_id=1, source_target_pairs={{0,24},{1,25},{2,26},{3,27},{4,28},{5,29},{6,30},{7,31},{8,16},{9,... | collective-permute-start | bytes 153608 | tf_op jit(solution)/shard_map/ppermute | solution.py:544
  130.1 6.8 %collective-permute-start.28 = (bf16[512,512]{1,0:T(8,128)(2,1)}, bf16[512,512]{1,0:T(8,128)(2,1)}, u32[]{:S(2)}, u32[]{:S(2)}) collective-permute-start(bf16[512,512]{1,0:T(8,128)(2,1)} %relay.3), channel_id=1, source_target_pairs={{0,1},{1,0},{2,3},{3,2},{4,5},{5,4},{6,7},{7,6},{8,9},{9,8},{10,11... | collective-permute-start | bytes 1572872 | tf_op jit(solution)/shard_map/ppermute | solution.py:544
  132.5 13.9 %collective-permute-start.31 = (bf16[1280,512]{1,0:T(8,128)(2,1)S(1)}, bf16[1280,512]{1,0:T(8,128)(2,1)S(1)}, u32[]{:S(2)}, u32[]{:S(2)}) collective-permute-start(bf16[1280,512]{1,0:T(8,128)(2,1)S(1)} %join.10.own_ref), channel_id=1, source_target_pairs={{0,1},{1,0},{2,3},{3,2},{4,5},{5,4},{6,7},{7,6},{8,9},{9,8},{10,11... | collective-permute-start | bytes 3932168 | tf_op jit(solution)/shard_map/ppermute | solution.py:544
  132.6 7.1 %collective-permute-start.32 = (bf16[800,128]{1,0:T(8,128)(2,1)S(1)}, bf16[800,128]{1,0:T(8,128)(2,1)S(1)}, u32[]{:S(2)}, u32[]{:S(2)}) collective-permute-start(bf16[800,128]{1,0:T(8,128)(2,1)S(1)} %join.6.refs_0_), channel_id=1, source_target_pairs={{0,2},{1,3},{2,0},{3,1},{4,6},{5,7},{6,4},{7,5},{8,10},{9,11},{10,... | collective-permute-start | bytes 614408 | tf_op jit(solution)/shard_map/ppermute | solution.py:544
  134.6 5.9 %collective-permute-start.33 = (bf16[800,128]{1,0:T(8,128)(2,1)S(1)}, bf16[800,128]{1,0:T(8,128)(2,1)S(1)}, u32[]{:S(2)}, u32[]{:S(2)}) collective-permute-start(bf16[800,128]{1,0:T(8,128)(2,1)S(1)} %join.6.refs_0_), channel_id=1, source_target_pairs={{0,4},{1,5},{2,6},{3,7},{4,0},{5,1},{6,2},{7,3},{8,12},{9,13},{10,... | collective-permute-start | bytes 614408 | tf_op jit(solution)/shard_map/ppermute | solution.py:544
  134.9 10.2 %collective-permute-start.34 = (bf16[800,128]{1,0:T(8,128)(2,1)S(1)}, bf16[800,128]{1,0:T(8,128)(2,1)S(1)}, u32[]{:S(2)}, u32[]{:S(2)}) collective-permute-start(bf16[800,128]{1,0:T(8,128)(2,1)S(1)} %join.6.refs_0_), channel_id=1, source_target_pairs={{0,6},{1,7},{2,4},{3,5},{4,2},{5,3},{6,0},{7,1},{8,14},{9,15},{10,... | collective-permute-start | bytes 614408 | tf_op jit(solution)/shard_map/ppermute | solution.py:544
  (27 other events, 357.2 us)

commit v3 on v2

--- a/solution.py
+++ b/solution.py
@@ -413,7 +413,7 @@
         grid=(count,),
         in_specs=[SMEM_SPEC, spec, spec, spec, spec, whole((HEADS, t)), whole((HEADS, t))],
         out_specs=[out, out, out],
-        out_shape=[pltpu.HBM((count, t, LANES), BF16)] * 3,
+        out_shape=[jax.ShapeDtypeStruct((count, t, LANES), BF16)] * 3,
         scratch_shapes=[pltpu.VMEM((LANES, t), F32)],
         compiler_params=params(28),
         cost_estimate=cost(count * B_FLOPS, count * 1e5),
@@ -479,7 +479,7 @@
         compiler_params=params(28),
         cost_estimate=cost(L_FLOPS, 1e5),
         name="last",
-    )(core, blk, *in_hbm(*grads), n1, x, gmid, gain[None], w_qkv, vec_mid)
+    )(core, blk, *grads, n1, x, gmid, gain[None], w_qkv, vec_mid)
 
 
 def ordered_halves(core_ref, own_ref, got_ref, write):

time: 151 us -> 151 us (level)
  Pallas kernels: 66.5 us -> 64 us
    pallas_call x1, Pallas kernels: 7.46 us -> 5.58 us  [last_call(): pl.pallas_call(last_kernel, grid=(1,), in_specs=[SMEM_SPEC, SMEM_SPEC] +...]
  transfers between devices with their start and end apart: 36 -> 36, of which waited for: 12 -> 13; matrix products, arithmetic and copies ran while one was open for 1% -> 1% of each run, Pallas kernels for 32% -> 30%
where the time goes in v3:
time: 151 us
  Pallas kernels  64 us (42%)
  starting transfers between devices  43.4 us (29%)
  waiting for transfers between devices  37.4 us (25%)
  local copies, waits for them, and re-layouts  4.44 us (3%)
    ppermute x36, starting transfers between devices, send_xor(): return lax.ppermute(values, BOTH, [(i, i ^ flip) for i in range(count)])  43.4 us
    ppermute x36, waiting for transfers between devices, send_xor(): return lax.ppermute(values, BOTH, [(i, i ^ flip) for i in range(count)])  37.4 us
    pallas_call x1, Pallas kernels, backward_call(): pl.pallas_call(functools.partial(backward_kernel, first), grid=(count,),...  16.5 us
    pallas_call x1, Pallas kernels, forward_call(): pl.pallas_call(forward_kernel, grid=(1,), in_specs=[SMEM_SPEC, SMEM_SPEC]...  14.4 us
    pallas_call x1, Pallas kernels, middle_call(): pl.pallas_call(middle_kernel, grid=(1,), in_specs=[SMEM_SPEC, SMEM_SPEC,...  13.6 us
    pallas_call x1, Pallas kernels, last_call(): pl.pallas_call(last_kernel, grid=(1,), in_specs=[SMEM_SPEC, SMEM_SPEC] +...  5.58 us
    pallas_call x2, Pallas kernels, finish_call(): pl.pallas_call(kernel, grid=(1,), in_specs=[SMEM_SPEC, whole(own.shape),...  4.79 us
    pallas_call x6, Pallas kernels, add_call(): pl.pallas_call(add_kernel, grid=(1,), in_specs=[SMEM_SPEC] + [whole(a.sha...  3.72 us
  transfers between devices with their start and end apart: 36, of which 13 were waited for; matrix products, arithmetic and copies ran while one was open for 1% of the time, Pallas kernels for 30%

profile of v3, /device:TPU:1, one launch (start us, length us, event | category | flops | bytes accessed | tf_op | source)
XLA Modules:
  0.0 150.6 jit_solution(10769622530228982045)
XLA Ops:
  0.7 2.1 %dynamic-slice_bitcast_fusion.4 = (bf16[256,512]{1,0:T(8,128)(2,1)S(1)}, bf16[256,512]{1,0:T(8,128)(2,1)}, bf16[256,512]{1,0:T(8,128)(2,1)S(1)}, bf16[256,512]{1,0:T(8,128)(2,1)S(1)}) fusion(bf16[4,256,512]{2,1,0:T(8,128)(2,1)} %param.15, s32[]{:T(128)S(6)} %select_n.22, s32[]{:T(128)S(6)} %select_n.20, s32[]{:T(128)S(6)} %select_n.19, s32[]{:T(128)S(6)} %select_n.21), kind=kLoop, calls=%fused_computation.4 | loop fusion | bytes 2097168 | tf_op jit(solution)/shard_map/jit(dynamic_index_in_dim)/squeeze | solution.py:626
  2.9 2.7 %collective-permute-start.1 = (bf16[256,512]{1,0:T(8,128)(2,1)S(1)}, bf16[256,512]{1,0:T(8,128)(2,1)S(1)}, u32[]{:S(2)}, u32[]{:S(2)}) collective-permute-start(bf16[256,512]{1,0:T(8,128)(2,1)S(1)} %get-tuple-element.167), channel_id=1, source_target_pairs={{0,2},{1,3},{2,0},{3,1},{4,6},{5,7},{6,4},{7,5},{8,10},{9,11},{10,... | collective-permute-start | bytes 786440 | tf_op jit(solution)/shard_map/ppermute | solution.py:544
  7.0 5.2 %collective-permute-done.1.x2_ref = bf16[256,512]{1,0:T(8,128)(2,1)S(1)} collective-permute-done((bf16[256,512]{1,0:T(8,128)(2,1)S(1)}, bf16[256,512]{1,0:T(8,128)(2,1)S(1)}, u32[]{:S(2)}, u32[]{:S(2)}) %collective-permute-start.1) | collective-permute-done | bytes 262176 | tf_op jit(solution)/shard_map/ppermute | solution.py:544
  12.2 5.6 %collective-permute-done.2.x3_ref = bf16[256,512]{1,0:T(8,128)(2,1)S(1)} collective-permute-done((bf16[256,512]{1,0:T(8,128)(2,1)S(1)}, bf16[256,512]{1,0:T(8,128)(2,1)S(1)}, u32[]{:S(2)}, u32[]{:S(2)}) %collective-permute-start.2) | collective-permute-done | bytes 262176 | tf_op jit(solution)/shard_map/ppermute | solution.py:544
  20.1 14.4 %forward.1 = (bf16[1024,512]{1,0:T(8,128)(2,1)S(1)}, bf16[4,1024,128]{2,1,0:T(8,128)(2,1)}, bf16[4,1024,128]{2,1,0:T(8,128)(2,1)}, bf16[4,1024,128]{2,1,0:T(8,12...) custom-call(s32[8]{0:T(128)S(1)} %fusion.ends_ref, ...), custom_call_target="tpu_custom_call" | custom-call | flops 20000000000 | bytes 10000000 | tf_op jit(solution)/shard_map/forward/pallas_call | solution.py:161
  34.6 13.6 %middle.1 = (bf16[256,512]{1,0:T(8,128)(2,1)}, bf16[256,512]{1,0:T(8,128)(2,1)}, bf16[512,512]{1,0:T(8,128)(2,1)}, f32[1024,512]{1,0:T(8,128)}, bf16[4,1024,128]...) custom-call(s32[1]{0:T(128)} %bitcast.2.core_ref.refs_0_, ...), custom_call_target="tpu_custom_call" | custom-call | flops 15000000512 | bytes 20000000 | tf_op jit(solution)/shard_map/middle/pallas_call | solution.py:316
  48.3 3.3 %collective-permute-done.6.refs_1_ = bf16[1280,512]{1,0:T(8,128)(2,1)} collective-permute-done((bf16[1280,512]{1,0:T(8,128)(2,1)}, bf16[1280,512]{1,0:T(8,128)(2,1)}, u32[]{:S(2)}, u32[]{:S(2)}) %collective-permute-start.6) | collective-permute-done | bytes 1310752 | tf_op jit(solution)/shard_map/ppermute | solution.py:544
  51.6 1.6 %add.33 = (f32[320,512]{1,0:T(8,128)S(1)}, bf16[320,512]{1,0:T(8,128)(2,1)S(1)}, bf16[320,512]{1,0:T(8,128)(2,1)S(1)}, bf16[320,512]{1,0:T(8,128)(2,1)S(1)}) custom-call(s32[4]{0:T(128)S(1)} %broadcast_in_dim.62.place_ref, f32[1280,512]{1,0:T(8,128)S(1)} %get-tuple-element.93.refs_0_, bf16[1280,512]{1,0:T(8,128)(2,1)} %collective-permute-done.6.refs_1_), custom_call_target="tpu_custom_call" | custom-call | flops 100000000 | bytes 4000000 | tf_op jit(solution)/shard_map/add/pallas_call | solution.py:563
  53.2 1.4 collective-permute-start.7
  55.9 16.5 %backward.1 = (bf16[4,1024,128]{2,1,0:T(8,128)(2,1)S(1)}, bf16[4,1024,128]{2,1,0:T(8,128)(2,1)S(1)}, bf16[4,1024,128]{2,1,0:T(8,128)(2,1)S(1)}) custom-call(s32[8]{0:T(128)S(1)} %fusion.ends_ref, bf16[4,1024,128]{2,1,0:T(8,128)(2,1)} %get-tuple-element.97.q_ref, bf16[4,1024,128]{2,1,0:T(8,128)(2,1)} %get-tuple-element.98.k_ref, ...), custom_call_target="tpu_custom_call" | custom-call | flops 4000000000 | bytes 400000 | tf_op jit(solution)/shard_map/backward/pallas_call | solution.py:411
  73.2 1.4 collective-permute-start.13
  75.9 2.3 %collective-permute-start.11 = (bf16[80,512]{1,0:T(8,128)(2,1)S(1)}, bf16[80,512]{1,0:T(8,128)(2,1)S(1)}, u32[]{:S(2)}, u32[]{:S(2)}) collective-permute-start(bf16[80,512]{1,0:T(8,128)(2,1)S(1)} %get-tuple-element.118), channel_id=1, source_target_pairs={{0,16},{1,17},{2,18},{3,19},{4,20},{5,21},{6,22},{7,23},{8,24},{9,... | collective-permute-start | bytes 245768 | tf_op jit(solution)/shard_map/ppermute | solution.py:544
  78.2 5.6 %last.1 = (bf16[256,512]{1,0:T(8,128)(2,1)}, bf16[256,512]{1,0:T(8,128)(2,1)}, bf16[512,512]{1,0:T(8,128)(2,1)}, f32[3200,128]{1,0:T(8,128)S(1)}, bf16[3200,128]{1,0:T(8,128)(2,1)S(1)}) custom-call(s32[1]{0:T(128)} %bitcast.2.core_ref.refs_0_, s32[1]{0:T(128)} %bitcast.blk_ref.refs_1_, bf16[4,1024,128]{2,1,0:T(8,128)(2,1)S(1)} %get-tuple-element.103.refs_2_, ...), custom_call_target="tpu_custom_call" | custom-call | flops 1000000000 | bytes 100000 | tf_op jit(solution)/shard_map/last/pallas_call | solution.py:464
  83.9 1.8 %collective-permute-done.13.far_ref = bf16[512,512]{1,0:T(8,128)(2,1)S(1)} collective-permute-done((bf16[512,512]{1,0:T(8,128)(2,1)S(1)}, bf16[512,512]{1,0:T(8,128)(2,1)S(1)}, u32[]{:S(2)}, u32[]{:S(2)}) %collective-permute-start.13) | collective-permute-done | bytes 524320 | tf_op jit(solution)/shard_map/ppermute | solution.py:544
  85.7 1.9 %collective-permute-start.14 = (bf16[3200,128]{1,0:T(8,128)(2,1)S(1)}, bf16[3200,128]{1,0:T(8,128)(2,1)S(1)}, u32[]{:S(2)}, u32[]{:S(2)}) collective-permute-start(bf16[3200,128]{1,0:T(8,128)(2,1)S(1)} %get-tuple-element.122), channel_id=1, source_target_pairs={{0,1},{1,0},{2,3},{3,2},{4,5},{5,4},{6,7},{7,6},{8,9},{9,8},{10,11... | collective-permute-start | bytes 2457608 | tf_op jit(solution)/shard_map/ppermute | solution.py:544
  87.6 1.4 collective-permute-start.25
  93.0 2.5 %collective-permute-start.26 = (bf16[160,512]{1,0:T(8,128)(2,1)S(1)}, bf16[160,512]{1,0:T(8,128)(2,1)S(1)}, u32[]{:S(2)}, u32[]{:S(2)}) collective-permute-start(bf16[160,512]{1,0:T(8,128)(2,1)S(1)} %join.7.refs_0_), channel_id=1, source_target_pairs={{0,16},{1,17},{2,18},{3,19},{4,20},{5,21},{6,22},{7,23},{8,24},{9,... | collective-permute-start | bytes 491528 | tf_op jit(solution)/shard_map/ppermute | solution.py:544
  95.5 7.0 %collective-permute-done.26.refs_1_ = bf16[160,512]{1,0:T(8,128)(2,1)S(1)} collective-permute-done((bf16[160,512]{1,0:T(8,128)(2,1)S(1)}, bf16[160,512]{1,0:T(8,128)(2,1)S(1)}, u32[]{:S(2)}, u32[]{:S(2)}) %collective-permute-start.26) | collective-permute-done | bytes 163872 | tf_op jit(solution)/shard_map/ppermute | solution.py:544
  104.6 1.5 collective-permute-start.18
  106.1 3.1 %collective-permute-start.19 = (bf16[200,128]{1,0:T(8,128)(2,1)S(1)}, bf16[200,128]{1,0:T(8,128)(2,1)S(1)}, u32[]{:S(2)}, u32[]{:S(2)}) collective-permute-start(bf16[200,128]{1,0:T(8,128)(2,1)S(1)} %get-tuple-element.129), channel_id=1, source_target_pairs={{0,16},{1,17},{2,18},{3,19},{4,20},{5,21},{6,22},{7,23},{8,24},{9,... | collective-permute-start | bytes 153608 | tf_op jit(solution)/shard_map/ppermute | solution.py:544
  109.2 2.0 %collective-permute-done.19.refs_2_ = bf16[200,128]{1,0:T(8,128)(2,1)S(1)} collective-permute-done((bf16[200,128]{1,0:T(8,128)(2,1)S(1)}, bf16[200,128]{1,0:T(8,128)(2,1)S(1)}, u32[]{:S(2)}, u32[]{:S(2)}) %collective-permute-start.19) | collective-permute-done | bytes 51232 | tf_op jit(solution)/shard_map/ppermute | solution.py:544
  111.3 2.8 %collective-permute-done.20.refs_3_ = bf16[200,128]{1,0:T(8,128)(2,1)S(1)} collective-permute-done((bf16[200,128]{1,0:T(8,128)(2,1)S(1)}, bf16[200,128]{1,0:T(8,128)(2,1)S(1)}, u32[]{:S(2)}, u32[]{:S(2)}) %collective-permute-start.20) | collective-permute-done | bytes 51232 | tf_op jit(solution)/shard_map/ppermute | solution.py:544
  116.5 2.9 %collective-permute-start.24 = (bf16[512,512]{1,0:T(8,128)(2,1)}, bf16[512,512]{1,0:T(8,128)(2,1)S(1)}, u32[]{:S(2)}, u32[]{:S(2)}) collective-permute-start(bf16[512,512]{1,0:T(8,128)(2,1)} %relay.2), channel_id=1, source_target_pairs={{0,1},{1,0},{2,3},{3,2},{4,5},{5,4},{6,7},{7,6},{8,9},{9,8},{10,11... | collective-permute-start | bytes 1572872 | tf_op jit(solution)/shard_map/ppermute | solution.py:544
  119.5 2.6 %collective-permute-start.22 = (bf16[200,128]{1,0:T(8,128)(2,1)S(1)}, bf16[200,128]{1,0:T(8,128)(2,1)S(1)}, u32[]{:S(2)}, u32[]{:S(2)}) collective-permute-start(bf16[200,128]{1,0:T(8,128)(2,1)S(1)} %add.38.refs_0_), channel_id=1, source_target_pairs={{0,16},{1,17},{2,18},{3,19},{4,20},{5,21},{6,22},{7,23},{8,24},{9,... | collective-permute-start | bytes 153608 | tf_op jit(solution)/shard_map/ppermute | solution.py:544
  122.9 2.3 %collective-permute-start.23 = (bf16[200,128]{1,0:T(8,128)(2,1)S(1)}, bf16[200,128]{1,0:T(8,128)(2,1)S(1)}, u32[]{:S(2)}, u32[]{:S(2)}) collective-permute-start(bf16[200,128]{1,0:T(8,128)(2,1)S(1)} %add.38.refs_0_), channel_id=1, source_target_pairs={{0,24},{1,25},{2,26},{3,27},{4,28},{5,29},{6,30},{7,31},{8,16},{9,... | collective-permute-start | bytes 153608 | tf_op jit(solution)/shard_map/ppermute | solution.py:544
  125.2 2.5 %collective-permute-done.23.refs_3_ = bf16[200,128]{1,0:T(8,128)(2,1)S(1)} collective-permute-done((bf16[200,128]{1,0:T(8,128)(2,1)S(1)}, bf16[200,128]{1,0:T(8,128)(2,1)S(1)}, u32[]{:S(2)}, u32[]{:S(2)}) %collective-permute-start.23) | collective-permute-done | bytes 51232 | tf_op jit(solution)/shard_map/ppermute | solution.py:544
  129.5 2.3 %collective-permute-start.28 = (bf16[512,512]{1,0:T(8,128)(2,1)}, bf16[512,512]{1,0:T(8,128)(2,1)}, u32[]{:S(2)}, u32[]{:S(2)}) collective-permute-start(bf16[512,512]{1,0:T(8,128)(2,1)} %relay.3), channel_id=1, source_target_pairs={{0,1},{1,0},{2,3},{3,2},{4,5},{5,4},{6,7},{7,6},{8,9},{9,8},{10,11... | collective-permute-start | bytes 1572872 | tf_op jit(solution)/shard_map/ppermute | solution.py:544
  132.0 2.0 %collective-permute-start.32 = (bf16[800,128]{1,0:T(8,128)(2,1)S(1)}, bf16[800,128]{1,0:T(8,128)(2,1)S(1)}, u32[]{:S(2)}, u32[]{:S(2)}) collective-permute-start(bf16[800,128]{1,0:T(8,128)(2,1)S(1)} %join.6.refs_0_), channel_id=1, source_target_pairs={{0,2},{1,3},{2,0},{3,1},{4,6},{5,7},{6,4},{7,5},{8,10},{9,11},{10,... | collective-permute-start | bytes 614408 | tf_op jit(solution)/shard_map/ppermute | solution.py:544
  136.3 2.5 %arrive.3 = f32[4,256,512]{2,1,0:T(8,128)} custom-call(s32[1]{0:T(128)} %bitcast.blk_ref.refs_1_, bf16[256,512]{1,0:T(8,128)(2,1)S(1)} %copy-done.8, bf16[512,512]{1,0:T(8,128)(2,1)} %collective-permute-done.28.near_ref, bf16[512,512]{1,0:T(8,128)(2,1)S(1)} %collective-permute-done.27.far_ref), custom_call_target="tpu_custom_call" | custom-call | flops 10000000 | bytes 100000 | tf_op jit(solution)/shard_map/arrive/pallas_call | solution.py:222
  139.9 4.6 %collective-permute-done.34.refs_3_ = bf16[800,128]{1,0:T(8,128)(2,1)S(1)} collective-permute-done((bf16[800,128]{1,0:T(8,128)(2,1)S(1)}, bf16[800,128]{1,0:T(8,128)(2,1)S(1)}, u32[]{:S(2)}, u32[]{:S(2)}) %collective-permute-start.34) | collective-permute-done | bytes 204832 | tf_op jit(solution)/shard_map/ppermute | solution.py:544
  145.8 2.7 %finish_mid.1 = (f32[1024,512]{1,0:T(8,128)}, f32[512,1024]{1,0:T(8,128)}, f32[512,512]{1,0:T(8,128)}) custom-call(s32[1]{0:T(128)} %bitcast.2.core_ref.refs_0_, bf16[1280,512]{1,0:T(8,128)(2,1)S(1)} %join.10.own_ref, bf16[1280,512]{1,0:T(8,128)(2,1)S(1)} %collective-permute-done.31.got_ref), custom_call_target="tpu_custom_call" | custom-call | flops 100000000 | bytes 8000000 | tf_op jit(solution)/shard_map/finish_mid/pallas_call | solution.py:530
  148.5 2.1 %finish_last.1 = (f32[512,1536]{1,0:T(8,128)}, f32[1,512]{1,0:T(1,128)}, f32[1,1024]{1,0:T(1,128)}, f32[1,512]{1,0:T(1,128)}, f32[1,512]{1,0:T(1,128)}, /*index=...) custom-call(s32[1]{0:T(128)} %bitcast.2.core_ref.refs_0_, ...), custom_call_target="tpu_custom_call" | custom-call | flops 100000000 | bytes 8000000 | tf_op jit(solution)/shard_map/finish_last/pallas_call | solution.py:530
  (115 shorter events, 23.3 us)
Async XLA Ops:
  2.8 4.2 %collective-permute-start = (bf16[256,512]{1,0:T(8,128)(2,1)}, bf16[256,512]{1,0:T(8,128)(2,1)S(1)}, u32[]{:S(2)}, u32[]{:S(2)}) collective-permute-start(bf16[256,512]{1,0:T(8,128)(2,1)} %get-tuple-element.165), channel_id=1, source_target_pairs={{0,1},{1,0},{2,3},{3,2},{4,5},{5,4},{6,7},{7,6},{8,9},{9,8},{10,11... | collective-permute-start | bytes 786440 | tf_op jit(solution)/shard_map/ppermute | solution.py:544
  2.9 9.4 %collective-permute-start.1 = (bf16[256,512]{1,0:T(8,128)(2,1)S(1)}, bf16[256,512]{1,0:T(8,128)(2,1)S(1)}, u32[]{:S(2)}, u32[]{:S(2)}) collective-permute-start(bf16[256,512]{1,0:T(8,128)(2,1)S(1)} %get-tuple-element.167), channel_id=1, source_target_pairs={{0,2},{1,3},{2,0},{3,1},{4,6},{5,7},{6,4},{7,5},{8,10},{9,11},{10,... | collective-permute-start | bytes 786440 | tf_op jit(solution)/shard_map/ppermute | solution.py:544
  5.5 12.3 %collective-permute-start.2 = (bf16[256,512]{1,0:T(8,128)(2,1)S(1)}, bf16[256,512]{1,0:T(8,128)(2,1)S(1)}, u32[]{:S(2)}, u32[]{:S(2)}) collective-permute-start(bf16[256,512]{1,0:T(8,128)(2,1)S(1)} %get-tuple-element.164), channel_id=1, source_target_pairs={{0,3},{1,2},{2,1},{3,0},{4,7},{5,6},{6,5},{7,4},{8,11},{9,10},{10,... | collective-permute-start | bytes 786440 | tf_op jit(solution)/shard_map/ppermute | solution.py:544
  17.8 16.7 %collective-permute-start.3 = (bf16[256,512]{1,0:T(8,128)(2,1)S(1)}, bf16[256,512]{1,0:T(8,128)(2,1)S(1)}, u32[]{:S(2)}, u32[]{:S(2)}) collective-permute-start(bf16[256,512]{1,0:T(8,128)(2,1)S(1)} %get-tuple-element.90), channel_id=1, source_target_pairs={{0,1},{1,0},{2,3},{3,2},{4,5},{5,4},{6,7},{7,6},{8,9},{9,8},{10,11... | collective-permute-start | bytes 786440 | tf_op jit(solution)/shard_map/ppermute | solution.py:544
  18.2 16.3 %collective-permute-start.4 = (bf16[256,512]{1,0:T(8,128)(2,1)S(1)}, bf16[256,512]{1,0:T(8,128)(2,1)S(1)}, u32[]{:S(2)}, u32[]{:S(2)}) collective-permute-start(bf16[256,512]{1,0:T(8,128)(2,1)S(1)} %get-tuple-element.91), channel_id=1, source_target_pairs={{0,2},{1,3},{2,0},{3,1},{4,6},{5,7},{6,4},{7,5},{8,10},{9,11},{10,... | collective-permute-start | bytes 786440 | tf_op jit(solution)/shard_map/ppermute | solution.py:544
  19.5 15.0 %collective-permute-start.5 = (bf16[256,512]{1,0:T(8,128)(2,1)S(1)}, bf16[256,512]{1,0:T(8,128)(2,1)S(1)}, u32[]{:S(2)}, u32[]{:S(2)}) collective-permute-start(bf16[256,512]{1,0:T(8,128)(2,1)S(1)} %get-tuple-element.92), channel_id=1, source_target_pairs={{0,3},{1,2},{2,1},{3,0},{4,7},{5,6},{6,5},{7,4},{8,11},{9,10},{10,... | collective-permute-start | bytes 786440 | tf_op jit(solution)/shard_map/ppermute | solution.py:544
  53.2 19.2 %collective-permute-start.7 = (bf16[320,512]{1,0:T(8,128)(2,1)S(1)}, bf16[320,512]{1,0:T(8,128)(2,1)S(1)}, u32[]{:S(2)}, u32[]{:S(2)}) collective-permute-start(bf16[320,512]{1,0:T(8,128)(2,1)S(1)} %get-tuple-element.105), channel_id=1, source_target_pairs={{0,2},{1,3},{2,0},{3,1},{4,6},{5,7},{6,4},{7,5},{8,10},{9,11},{10,... | collective-permute-start | bytes 983048 | tf_op jit(solution)/shard_map/ppermute | solution.py:544
  54.6 17.8 %collective-permute-start.8 = (bf16[320,512]{1,0:T(8,128)(2,1)S(1)}, bf16[320,512]{1,0:T(8,128)(2,1)S(1)}, u32[]{:S(2)}, u32[]{:S(2)}) collective-permute-start(bf16[320,512]{1,0:T(8,128)(2,1)S(1)} %get-tuple-element.106), channel_id=1, source_target_pairs={{0,4},{1,5},{2,6},{3,7},{4,0},{5,1},{6,2},{7,3},{8,12},{9,13},{10,... | collective-permute-start | bytes 983048 | tf_op jit(solution)/shard_map/ppermute | solution.py:544
  55.8 16.6 %collective-permute-start.9 = (bf16[320,512]{1,0:T(8,128)(2,1)S(1)}, bf16[320,512]{1,0:T(8,128)(2,1)S(1)}, u32[]{:S(2)}, u32[]{:S(2)}) collective-permute-start(bf16[320,512]{1,0:T(8,128)(2,1)S(1)} %get-tuple-element.107), channel_id=1, source_target_pairs={{0,6},{1,7},{2,4},{3,5},{4,2},{5,3},{6,0},{7,1},{8,14},{9,15},{10,... | collective-permute-start | bytes 983048 | tf_op jit(solution)/shard_map/ppermute | solution.py:544
  73.2 12.5 %collective-permute-start.13 = (bf16[512,512]{1,0:T(8,128)(2,1)S(1)}, bf16[512,512]{1,0:T(8,128)(2,1)S(1)}, u32[]{:S(2)}, u32[]{:S(2)}) collective-permute-start(bf16[512,512]{1,0:T(8,128)(2,1)S(1)} %copy-done.22), channel_id=1, source_target_pairs={{0,2},{1,3},{2,0},{3,1},{4,6},{5,7},{6,4},{7,5},{8,10},{9,11},{10,... | collective-permute-start | bytes 1572872 | tf_op jit(solution)/shard_map/ppermute | solution.py:544
  74.6 9.2 %collective-permute-start.10 = (bf16[80,512]{1,0:T(8,128)(2,1)S(1)}, bf16[80,512]{1,0:T(8,128)(2,1)S(1)}, u32[]{:S(2)}, u32[]{:S(2)}) collective-permute-start(bf16[80,512]{1,0:T(8,128)(2,1)S(1)} %get-tuple-element.117), channel_id=1, source_target_pairs={{0,8},{1,9},{2,10},{3,11},{4,12},{5,13},{6,14},{7,15},{8,0},{9,1},... | collective-permute-start | bytes 245768 | tf_op jit(solution)/shard_map/ppermute | solution.py:544
  75.9 7.9 %collective-permute-start.11 = (bf16[80,512]{1,0:T(8,128)(2,1)S(1)}, bf16[80,512]{1,0:T(8,128)(2,1)S(1)}, u32[]{:S(2)}, u32[]{:S(2)}) collective-permute-start(bf16[80,512]{1,0:T(8,128)(2,1)S(1)} %get-tuple-element.118), channel_id=1, source_target_pairs={{0,16},{1,17},{2,18},{3,19},{4,20},{5,21},{6,22},{7,23},{8,24},{9,... | collective-permute-start | bytes 245768 | tf_op jit(solution)/shard_map/ppermute | solution.py:544
  78.2 5.6 %collective-permute-start.12 = (bf16[80,512]{1,0:T(8,128)(2,1)S(1)}, bf16[80,512]{1,0:T(8,128)(2,1)S(1)}, u32[]{:S(2)}, u32[]{:S(2)}) collective-permute-start(bf16[80,512]{1,0:T(8,128)(2,1)S(1)} %get-tuple-element.119), channel_id=1, source_target_pairs={{0,24},{1,25},{2,26},{3,27},{4,28},{5,29},{6,30},{7,31},{8,16},{9,... | collective-permute-start | bytes 245768 | tf_op jit(solution)/shard_map/ppermute | solution.py:544
  87.6 5.4 %collective-permute-start.25 = (bf16[80,512]{1,0:T(8,128)(2,1)S(1)}, bf16[80,512]{1,0:T(8,128)(2,1)S(1)}, u32[]{:S(2)}, u32[]{:S(2)}) collective-permute-start(bf16[80,512]{1,0:T(8,128)(2,1)S(1)} %add.35.refs_0_), channel_id=1, source_target_pairs={{0,8},{1,9},{2,10},{3,11},{4,12},{5,13},{6,14},{7,15},{8,0},{9,1},... | collective-permute-start | bytes 245768 | tf_op jit(solution)/shard_map/ppermute | solution.py:544
  90.3 12.3 %collective-permute-start.15 = (bf16[800,128]{1,0:T(8,128)(2,1)S(1)}, bf16[800,128]{1,0:T(8,128)(2,1)S(1)}, u32[]{:S(2)}, u32[]{:S(2)}) collective-permute-start(bf16[800,128]{1,0:T(8,128)(2,1)S(1)} %get-tuple-element.124), channel_id=1, source_target_pairs={{0,2},{1,3},{2,0},{3,1},{4,6},{5,7},{6,4},{7,5},{8,10},{9,11},{10,... | collective-permute-start | bytes 614408 | tf_op jit(solution)/shard_map/ppermute | solution.py:544
  91.7 10.9 %collective-permute-start.16 = (bf16[800,128]{1,0:T(8,128)(2,1)S(1)}, bf16[800,128]{1,0:T(8,128)(2,1)S(1)}, u32[]{:S(2)}, u32[]{:S(2)}) collective-permute-start(bf16[800,128]{1,0:T(8,128)(2,1)S(1)} %get-tuple-element.125), channel_id=1, source_target_pairs={{0,4},{1,5},{2,6},{3,7},{4,0},{5,1},{6,2},{7,3},{8,12},{9,13},{10,... | collective-permute-start | bytes 614408 | tf_op jit(solution)/shard_map/ppermute | solution.py:544
  92.9 9.7 %collective-permute-start.17 = (bf16[800,128]{1,0:T(8,128)(2,1)S(1)}, bf16[800,128]{1,0:T(8,128)(2,1)S(1)}, u32[]{:S(2)}, u32[]{:S(2)}) collective-permute-start(bf16[800,128]{1,0:T(8,128)(2,1)S(1)} %get-tuple-element.126), channel_id=1, source_target_pairs={{0,6},{1,7},{2,4},{3,5},{4,2},{5,3},{6,0},{7,1},{8,14},{9,15},{10,... | collective-permute-start | bytes 614408 | tf_op jit(solution)/shard_map/ppermute | solution.py:544
  93.0 9.5 %collective-permute-start.26 = (bf16[160,512]{1,0:T(8,128)(2,1)S(1)}, bf16[160,512]{1,0:T(8,128)(2,1)S(1)}, u32[]{:S(2)}, u32[]{:S(2)}) collective-permute-start(bf16[160,512]{1,0:T(8,128)(2,1)S(1)} %join.7.refs_0_), channel_id=1, source_target_pairs={{0,16},{1,17},{2,18},{3,19},{4,20},{5,21},{6,22},{7,23},{8,24},{9,... | collective-permute-start | bytes 491528 | tf_op jit(solution)/shard_map/ppermute | solution.py:544
  103.2 10.9 %collective-permute-start.29 = (bf16[320,512]{1,0:T(8,128)(2,1)S(1)}, bf16[320,512]{1,0:T(8,128)(2,1)S(1)}, u32[]{:S(2)}, u32[]{:S(2)}) collective-permute-start(bf16[320,512]{1,0:T(8,128)(2,1)S(1)} %join.8.refs_0_), channel_id=1, source_target_pairs={{0,2},{1,3},{2,0},{3,1},{4,6},{5,7},{6,4},{7,5},{8,10},{9,11},{10,... | collective-permute-start | bytes 983048 | tf_op jit(solution)/shard_map/ppermute | solution.py:544
  104.6 4.6 %collective-permute-start.18 = (bf16[200,128]{1,0:T(8,128)(2,1)S(1)}, bf16[200,128]{1,0:T(8,128)(2,1)S(1)}, u32[]{:S(2)}, u32[]{:S(2)}) collective-permute-start(bf16[200,128]{1,0:T(8,128)(2,1)S(1)} %get-tuple-element.128), channel_id=1, source_target_pairs={{0,8},{1,9},{2,10},{3,11},{4,12},{5,13},{6,14},{7,15},{8,0},{9,1},... | collective-permute-start | bytes 153608 | tf_op jit(solution)/shard_map/ppermute | solution.py:544
  106.1 5.2 %collective-permute-start.19 = (bf16[200,128]{1,0:T(8,128)(2,1)S(1)}, bf16[200,128]{1,0:T(8,128)(2,1)S(1)}, u32[]{:S(2)}, u32[]{:S(2)}) collective-permute-start(bf16[200,128]{1,0:T(8,128)(2,1)S(1)} %get-tuple-element.129), channel_id=1, source_target_pairs={{0,16},{1,17},{2,18},{3,19},{4,20},{5,21},{6,22},{7,23},{8,24},{9,... | collective-permute-start | bytes 153608 | tf_op jit(solution)/shard_map/ppermute | solution.py:544
  109.2 4.9 %collective-permute-start.20 = (bf16[200,128]{1,0:T(8,128)(2,1)S(1)}, bf16[200,128]{1,0:T(8,128)(2,1)S(1)}, u32[]{:S(2)}, u32[]{:S(2)}) collective-permute-start(bf16[200,128]{1,0:T(8,128)(2,1)S(1)} %get-tuple-element.130), channel_id=1, source_target_pairs={{0,24},{1,25},{2,26},{3,27},{4,28},{5,29},{6,30},{7,31},{8,16},{9,... | collective-permute-start | bytes 153608 | tf_op jit(solution)/shard_map/ppermute | solution.py:544
  114.2 17.6 %collective-permute-start.30 = (bf16[640,512]{1,0:T(8,128)(2,1)S(1)}, bf16[640,512]{1,0:T(8,128)(2,1)S(1)}, u32[]{:S(2)}, u32[]{:S(2)}) collective-permute-start(bf16[640,512]{1,0:T(8,128)(2,1)S(1)} %join.9.refs_0_), channel_id=1, source_target_pairs={{0,4},{1,5},{2,6},{3,7},{4,0},{5,1},{6,2},{7,3},{8,12},{9,13},{10,... | collective-permute-start | bytes 1966088 | tf_op jit(solution)/shard_map/ppermute | solution.py:544
  115.4 12.2 %collective-permute-start.27 = (bf16[512,512]{1,0:T(8,128)(2,1)}, bf16[512,512]{1,0:T(8,128)(2,1)S(1)}, u32[]{:S(2)}, u32[]{:S(2)}) collective-permute-start(bf16[512,512]{1,0:T(8,128)(2,1)} %get-tuple-element.142), channel_id=1, source_target_pairs={{0,2},{1,3},{2,0},{3,1},{4,6},{5,7},{6,4},{7,5},{8,10},{9,11},{10,... | collective-permute-start | bytes 1572872 | tf_op jit(solution)/shard_map/ppermute | solution.py:544
  116.5 17.7 %collective-permute-start.24 = (bf16[512,512]{1,0:T(8,128)(2,1)}, bf16[512,512]{1,0:T(8,128)(2,1)S(1)}, u32[]{:S(2)}, u32[]{:S(2)}) collective-permute-start(bf16[512,512]{1,0:T(8,128)(2,1)} %relay.2), channel_id=1, source_target_pairs={{0,1},{1,0},{2,3},{3,2},{4,5},{5,4},{6,7},{7,6},{8,9},{9,8},{10,11... | collective-permute-start | bytes 1572872 | tf_op jit(solution)/shard_map/ppermute | solution.py:544
  119.5 5.7 %collective-permute-start.22 = (bf16[200,128]{1,0:T(8,128)(2,1)S(1)}, bf16[200,128]{1,0:T(8,128)(2,1)S(1)}, u32[]{:S(2)}, u32[]{:S(2)}) collective-permute-start(bf16[200,128]{1,0:T(8,128)(2,1)S(1)} %add.38.refs_0_), channel_id=1, source_target_pairs={{0,16},{1,17},{2,18},{3,19},{4,20},{5,21},{6,22},{7,23},{8,24},{9,... | collective-permute-start | bytes 153608 | tf_op jit(solution)/shard_map/ppermute | solution.py:544
  122.9 4.8 %collective-permute-start.23 = (bf16[200,128]{1,0:T(8,128)(2,1)S(1)}, bf16[200,128]{1,0:T(8,128)(2,1)S(1)}, u32[]{:S(2)}, u32[]{:S(2)}) collective-permute-start(bf16[200,128]{1,0:T(8,128)(2,1)S(1)} %add.38.refs_0_), channel_id=1, source_target_pairs={{0,24},{1,25},{2,26},{3,27},{4,28},{5,29},{6,30},{7,31},{8,16},{9,... | collective-permute-start | bytes 153608 | tf_op jit(solution)/shard_map/ppermute | solution.py:544
  129.5 6.8 %collective-permute-start.28 = (bf16[512,512]{1,0:T(8,128)(2,1)}, bf16[512,512]{1,0:T(8,128)(2,1)}, u32[]{:S(2)}, u32[]{:S(2)}) collective-permute-start(bf16[512,512]{1,0:T(8,128)(2,1)} %relay.3), channel_id=1, source_target_pairs={{0,1},{1,0},{2,3},{3,2},{4,5},{5,4},{6,7},{7,6},{8,9},{9,8},{10,11... | collective-permute-start | bytes 1572872 | tf_op jit(solution)/shard_map/ppermute | solution.py:544
  131.9 13.9 %collective-permute-start.31 = (bf16[1280,512]{1,0:T(8,128)(2,1)S(1)}, bf16[1280,512]{1,0:T(8,128)(2,1)S(1)}, u32[]{:S(2)}, u32[]{:S(2)}) collective-permute-start(bf16[1280,512]{1,0:T(8,128)(2,1)S(1)} %join.10.own_ref), channel_id=1, source_target_pairs={{0,1},{1,0},{2,3},{3,2},{4,5},{5,4},{6,7},{7,6},{8,9},{9,8},{10,11... | collective-permute-start | bytes 3932168 | tf_op jit(solution)/shard_map/ppermute | solution.py:544
  132.0 7.1 %collective-permute-start.32 = (bf16[800,128]{1,0:T(8,128)(2,1)S(1)}, bf16[800,128]{1,0:T(8,128)(2,1)S(1)}, u32[]{:S(2)}, u32[]{:S(2)}) collective-permute-start(bf16[800,128]{1,0:T(8,128)(2,1)S(1)} %join.6.refs_0_), channel_id=1, source_target_pairs={{0,2},{1,3},{2,0},{3,1},{4,6},{5,7},{6,4},{7,5},{8,10},{9,11},{10,... | collective-permute-start | bytes 614408 | tf_op jit(solution)/shard_map/ppermute | solution.py:544
  134.0 5.9 %collective-permute-start.33 = (bf16[800,128]{1,0:T(8,128)(2,1)S(1)}, bf16[800,128]{1,0:T(8,128)(2,1)S(1)}, u32[]{:S(2)}, u32[]{:S(2)}) collective-permute-start(bf16[800,128]{1,0:T(8,128)(2,1)S(1)} %join.6.refs_0_), channel_id=1, source_target_pairs={{0,4},{1,5},{2,6},{3,7},{4,0},{5,1},{6,2},{7,3},{8,12},{9,13},{10,... | collective-permute-start | bytes 614408 | tf_op jit(solution)/shard_map/ppermute | solution.py:544
  134.3 10.2 %collective-permute-start.34 = (bf16[800,128]{1,0:T(8,128)(2,1)S(1)}, bf16[800,128]{1,0:T(8,128)(2,1)S(1)}, u32[]{:S(2)}, u32[]{:S(2)}) collective-permute-start(bf16[800,128]{1,0:T(8,128)(2,1)S(1)} %join.6.refs_0_), channel_id=1, source_target_pairs={{0,6},{1,7},{2,4},{3,5},{4,2},{5,3},{6,0},{7,1},{8,14},{9,15},{10,... | collective-permute-start | bytes 614408 | tf_op jit(solution)/shard_map/ppermute | solution.py:544
  (27 other events, 354.9 us)

commit v4 on v3

--- a/solution.py
+++ b/solution.py
@@ -234,7 +234,7 @@
 def split_halves(core_ref, whole_ref, keep_ref, send_ref):
     half = keep_ref.shape[0]
     core = core_ref[0]
-    keep_ref[...] = whole_ref[pl.ds(pl.multiple_of(core * half, half), half), :]
+    keep_ref[...] = whole_ref[pl.ds(pl.multiple_of(core * half, half), half), :].astype(BF16)
     send_ref[...] = whole_ref[pl.ds(pl.multiple_of((1 - core) * half, half), half), :].astype(BF16)
 
 
@@ -332,7 +332,7 @@
             pltpu.HBM((t, d), F32),
             pltpu.HBM((pairs, t, LANES), BF16),
             jax.ShapeDtypeStruct((HEADS, t), F32),
-            jax.ShapeDtypeStruct((half, d), F32),
+            jax.ShapeDtypeStruct((half, d), BF16),
             jax.ShapeDtypeStruct((half, d), BF16),
             jax.ShapeDtypeStruct((8, d), F32),
         ],
@@ -472,7 +472,7 @@
             pltpu.HBM((t // 4, d), BF16),
             pltpu.HBM((t // 4, d), BF16),
             pltpu.HBM((t // 2, d), BF16),
-            jax.ShapeDtypeStruct((half, LANES), F32),
+            jax.ShapeDtypeStruct((half, LANES), BF16),
             jax.ShapeDtypeStruct((half, LANES), BF16),
         ],
         scratch_shapes=[pltpu.VMEM((2 * half, LANES), F32), pltpu.VMEM((t, d), BF16)],

time: 151 us -> 153 us (1.013)
  local copies, waits for them, and re-layouts: 4.44 us -> 6.8 us
    unnamed x46 -> x48, local copies, waits for them, and re-layouts: 1.09 us -> 3.46 us
where the time goes in v4:
time: 153 us
  Pallas kernels  63.9 us (42%)
  starting transfers between devices  43.5 us (28%)
  waiting for transfers between devices  37.4 us (24%)
  local copies, waits for them, and re-layouts  6.8 us (4%)
    ppermute x36, starting transfers between devices, send_xor(): return lax.ppermute(values, BOTH, [(i, i ^ flip) for i in range(count)])  43.5 us
    ppermute x36, waiting for transfers between devices, send_xor(): return lax.ppermute(values, BOTH, [(i, i ^ flip) for i in range(count)])  37.4 us
    pallas_call x1, Pallas kernels, backward_call(): pl.pallas_call(functools.partial(backward_kernel, first), grid=(count,),...  16.5 us
    pallas_call x1, Pallas kernels, forward_call(): pl.pallas_call(forward_kernel, grid=(1,), in_specs=[SMEM_SPEC, SMEM_SPEC]...  14.3 us
    pallas_call x1, Pallas kernels, middle_call(): pl.pallas_call(middle_kernel, grid=(1,), in_specs=[SMEM_SPEC, SMEM_SPEC,...  13.6 us
    pallas_call x1, Pallas kernels, last_call(): pl.pallas_call(last_kernel, grid=(1,), in_specs=[SMEM_SPEC, SMEM_SPEC] +...  5.55 us
    pallas_call x2, Pallas kernels, finish_call(): pl.pallas_call(kernel, grid=(1,), in_specs=[SMEM_SPEC, whole(own.shape),...  4.79 us
    pallas_call x6, Pallas kernels, add_call(): pl.pallas_call(add_kernel, grid=(1,), in_specs=[SMEM_SPEC] + [whole(a.sha...  3.76 us
  transfers between devices with their start and end apart: 36, of which 13 were waited for; matrix products, arithmetic and copies ran while one was open for 1% of the time, Pallas kernels for 30%

profile of v4, /device:TPU:1, one launch (start us, length us, event | category | flops | bytes accessed | tf_op | source)
XLA Modules:
  0.0 152.9 jit_solution(12036485520506350394)
XLA Ops:
  0.7 2.1 %dynamic-slice_bitcast_fusion.4 = (bf16[256,512]{1,0:T(8,128)(2,1)S(1)}, bf16[256,512]{1,0:T(8,128)(2,1)}, bf16[256,512]{1,0:T(8,128)(2,1)S(1)}, bf16[256,512]{1,0:T(8,128)(2,1)S(1)}) fusion(bf16[4,256,512]{2,1,0:T(8,128)(2,1)} %param.15, s32[]{:T(128)S(6)} %select_n.22, s32[]{:T(128)S(6)} %select_n.20, s32[]{:T(128)S(6)} %select_n.19, s32[]{:T(128)S(6)} %select_n.21), kind=kLoop, calls=%fused_computation.4 | loop fusion | bytes 2097168 | tf_op jit(solution)/shard_map/jit(dynamic_index_in_dim)/squeeze | solution.py:626
  2.9 2.7 %collective-permute-start.1 = (bf16[256,512]{1,0:T(8,128)(2,1)S(1)}, bf16[256,512]{1,0:T(8,128)(2,1)S(1)}, u32[]{:S(2)}, u32[]{:S(2)}) collective-permute-start(bf16[256,512]{1,0:T(8,128)(2,1)S(1)} %get-tuple-element.167), channel_id=1, source_target_pairs={{0,2},{1,3},{2,0},{3,1},{4,6},{5,7},{6,4},{7,5},{8,10},{9,11},{10,... | collective-permute-start | bytes 786440 | tf_op jit(solution)/shard_map/ppermute | solution.py:544
  7.0 5.2 %collective-permute-done.1.x2_ref = bf16[256,512]{1,0:T(8,128)(2,1)S(1)} collective-permute-done((bf16[256,512]{1,0:T(8,128)(2,1)S(1)}, bf16[256,512]{1,0:T(8,128)(2,1)S(1)}, u32[]{:S(2)}, u32[]{:S(2)}) %collective-permute-start.1) | collective-permute-done | bytes 262176 | tf_op jit(solution)/shard_map/ppermute | solution.py:544
  12.2 5.6 %collective-permute-done.2.x3_ref = bf16[256,512]{1,0:T(8,128)(2,1)S(1)} collective-permute-done((bf16[256,512]{1,0:T(8,128)(2,1)S(1)}, bf16[256,512]{1,0:T(8,128)(2,1)S(1)}, u32[]{:S(2)}, u32[]{:S(2)}) %collective-permute-start.2) | collective-permute-done | bytes 262176 | tf_op jit(solution)/shard_map/ppermute | solution.py:544
  20.1 14.3 %forward.1 = (bf16[1024,512]{1,0:T(8,128)(2,1)S(1)}, bf16[4,1024,128]{2,1,0:T(8,128)(2,1)}, bf16[4,1024,128]{2,1,0:T(8,128)(2,1)}, bf16[4,1024,128]{2,1,0:T(8,12...) custom-call(s32[8]{0:T(128)S(1)} %fusion.ends_ref, ...), custom_call_target="tpu_custom_call" | custom-call | flops 20000000000 | bytes 10000000 | tf_op jit(solution)/shard_map/forward/pallas_call | solution.py:161
  34.5 13.6 %middle.1 = (bf16[256,512]{1,0:T(8,128)(2,1)}, bf16[256,512]{1,0:T(8,128)(2,1)}, bf16[512,512]{1,0:T(8,128)(2,1)}, f32[1024,512]{1,0:T(8,128)}, bf16[4,1024,128]...) custom-call(s32[1]{0:T(128)} %bitcast.2.core_ref.refs_0_, ...), custom_call_target="tpu_custom_call" | custom-call | flops 15000000512 | bytes 20000000 | tf_op jit(solution)/shard_map/middle/pallas_call | solution.py:316
  49.3 3.3 %collective-permute-done.6.refs_1_ = bf16[1280,512]{1,0:T(8,128)(2,1)} collective-permute-done((bf16[1280,512]{1,0:T(8,128)(2,1)}, bf16[1280,512]{1,0:T(8,128)(2,1)}, u32[]{:S(2)}, u32[]{:S(2)}) %collective-permute-start.6) | collective-permute-done | bytes 1310752 | tf_op jit(solution)/shard_map/ppermute | solution.py:544
  53.9 1.6 %add.33 = (f32[320,512]{1,0:T(8,128)S(1)}, bf16[320,512]{1,0:T(8,128)(2,1)S(1)}, bf16[320,512]{1,0:T(8,128)(2,1)S(1)}, bf16[320,512]{1,0:T(8,128)(2,1)S(1)}) custom-call(s32[4]{0:T(128)S(1)} %broadcast_in_dim.62.place_ref, bf16[1280,512]{1,0:T(8,128)(2,1)S(1)} %copy-done.3, bf16[1280,512]{1,0:T(8,128)(2,1)} %collective-permute-done.6.refs_1_), custom_call_target="tpu_custom_call" | custom-call | flops 100000000 | bytes 4000000 | tf_op jit(solution)/shard_map/add/pallas_call | solution.py:563
  55.6 1.4 collective-permute-start.7
  58.3 16.5 %backward.1 = (bf16[4,1024,128]{2,1,0:T(8,128)(2,1)S(1)}, bf16[4,1024,128]{2,1,0:T(8,128)(2,1)S(1)}, bf16[4,1024,128]{2,1,0:T(8,128)(2,1)S(1)}) custom-call(s32[8]{0:T(128)S(1)} %fusion.ends_ref, bf16[4,1024,128]{2,1,0:T(8,128)(2,1)} %get-tuple-element.97.q_ref, bf16[4,1024,128]{2,1,0:T(8,128)(2,1)} %get-tuple-element.98.k_ref, ...), custom_call_target="tpu_custom_call" | custom-call | flops 4000000000 | bytes 400000 | tf_op jit(solution)/shard_map/backward/pallas_call | solution.py:411
  75.5 1.4 collective-permute-start.13
  78.2 2.3 %collective-permute-start.11 = (bf16[80,512]{1,0:T(8,128)(2,1)S(1)}, bf16[80,512]{1,0:T(8,128)(2,1)S(1)}, u32[]{:S(2)}, u32[]{:S(2)}) collective-permute-start(bf16[80,512]{1,0:T(8,128)(2,1)S(1)} %get-tuple-element.118), channel_id=1, source_target_pairs={{0,16},{1,17},{2,18},{3,19},{4,20},{5,21},{6,22},{7,23},{8,24},{9,... | collective-permute-start | bytes 245768 | tf_op jit(solution)/shard_map/ppermute | solution.py:544
  80.5 5.6 %last.1 = (bf16[256,512]{1,0:T(8,128)(2,1)}, bf16[256,512]{1,0:T(8,128)(2,1)}, bf16[512,512]{1,0:T(8,128)(2,1)}, bf16[3200,128]{1,0:T(8,128)(2,1)S(1)}, bf16[3200,128]{1,0:T(8,128)(2,1)S(1)}) custom-call(s32[1]{0:T(128)} %bitcast.2.core_ref.refs_0_, s32[1]{0:T(128)} %bitcast.blk_ref.refs_1_, bf16[4,1024,128]{2,1,0:T(8,128)(2,1)S(1)} %get-tuple-element.103.refs_2_, ...), custom_call_target="tpu_custom_call" | custom-call | flops 1000000000 | bytes 100000 | tf_op jit(solution)/shard_map/last/pallas_call | solution.py:464
  86.2 1.8 %collective-permute-done.13.far_ref = bf16[512,512]{1,0:T(8,128)(2,1)S(1)} collective-permute-done((bf16[512,512]{1,0:T(8,128)(2,1)S(1)}, bf16[512,512]{1,0:T(8,128)(2,1)S(1)}, u32[]{:S(2)}, u32[]{:S(2)}) %collective-permute-start.13) | collective-permute-done | bytes 524320 | tf_op jit(solution)/shard_map/ppermute | solution.py:544
  88.0 1.9 %collective-permute-start.14 = (bf16[3200,128]{1,0:T(8,128)(2,1)S(1)}, bf16[3200,128]{1,0:T(8,128)(2,1)S(1)}, u32[]{:S(2)}, u32[]{:S(2)}) collective-permute-start(bf16[3200,128]{1,0:T(8,128)(2,1)S(1)} %get-tuple-element.122), channel_id=1, source_target_pairs={{0,1},{1,0},{2,3},{3,2},{4,5},{5,4},{6,7},{7,6},{8,9},{9,8},{10,11... | collective-permute-start | bytes 2457608 | tf_op jit(solution)/shard_map/ppermute | solution.py:544
  92.6 1.4 collective-permute-start.15
  95.3 2.5 %collective-permute-start.26 = (bf16[160,512]{1,0:T(8,128)(2,1)S(1)}, bf16[160,512]{1,0:T(8,128)(2,1)S(1)}, u32[]{:S(2)}, u32[]{:S(2)}) collective-permute-start(bf16[160,512]{1,0:T(8,128)(2,1)S(1)} %join.7.refs_0_), channel_id=1, source_target_pairs={{0,16},{1,17},{2,18},{3,19},{4,20},{5,21},{6,22},{7,23},{8,24},{9,... | collective-permute-start | bytes 491528 | tf_op jit(solution)/shard_map/ppermute | solution.py:544
  97.8 7.1 %collective-permute-done.26.refs_1_ = bf16[160,512]{1,0:T(8,128)(2,1)S(1)} collective-permute-done((bf16[160,512]{1,0:T(8,128)(2,1)S(1)}, bf16[160,512]{1,0:T(8,128)(2,1)S(1)}, u32[]{:S(2)}, u32[]{:S(2)}) %collective-permute-start.26) | collective-permute-done | bytes 163872 | tf_op jit(solution)/shard_map/ppermute | solution.py:544
  107.0 1.4 collective-permute-start.18
  108.4 3.1 %collective-permute-start.19 = (bf16[200,128]{1,0:T(8,128)(2,1)S(1)}, bf16[200,128]{1,0:T(8,128)(2,1)S(1)}, u32[]{:S(2)}, u32[]{:S(2)}) collective-permute-start(bf16[200,128]{1,0:T(8,128)(2,1)S(1)} %get-tuple-element.129), channel_id=1, source_target_pairs={{0,16},{1,17},{2,18},{3,19},{4,20},{5,21},{6,22},{7,23},{8,24},{9,... | collective-permute-start | bytes 153608 | tf_op jit(solution)/shard_map/ppermute | solution.py:544
  111.6 2.0 %collective-permute-done.19.refs_2_ = bf16[200,128]{1,0:T(8,128)(2,1)S(1)} collective-permute-done((bf16[200,128]{1,0:T(8,128)(2,1)S(1)}, bf16[200,128]{1,0:T(8,128)(2,1)S(1)}, u32[]{:S(2)}, u32[]{:S(2)}) %collective-permute-start.19) | collective-permute-done | bytes 51232 | tf_op jit(solution)/shard_map/ppermute | solution.py:544
  113.6 2.8 %collective-permute-done.20.refs_3_ = bf16[200,128]{1,0:T(8,128)(2,1)S(1)} collective-permute-done((bf16[200,128]{1,0:T(8,128)(2,1)S(1)}, bf16[200,128]{1,0:T(8,128)(2,1)S(1)}, u32[]{:S(2)}, u32[]{:S(2)}) %collective-permute-start.20) | collective-permute-done | bytes 51232 | tf_op jit(solution)/shard_map/ppermute | solution.py:544
  118.8 2.9 %collective-permute-start.24 = (bf16[512,512]{1,0:T(8,128)(2,1)}, bf16[512,512]{1,0:T(8,128)(2,1)S(1)}, u32[]{:S(2)}, u32[]{:S(2)}) collective-permute-start(bf16[512,512]{1,0:T(8,128)(2,1)} %relay.2), channel_id=1, source_target_pairs={{0,1},{1,0},{2,3},{3,2},{4,5},{5,4},{6,7},{7,6},{8,9},{9,8},{10,11... | collective-permute-start | bytes 1572872 | tf_op jit(solution)/shard_map/ppermute | solution.py:544
  121.8 2.6 %collective-permute-start.22 = (bf16[200,128]{1,0:T(8,128)(2,1)S(1)}, bf16[200,128]{1,0:T(8,128)(2,1)S(1)}, u32[]{:S(2)}, u32[]{:S(2)}) collective-permute-start(bf16[200,128]{1,0:T(8,128)(2,1)S(1)} %add.38.refs_0_), channel_id=1, source_target_pairs={{0,16},{1,17},{2,18},{3,19},{4,20},{5,21},{6,22},{7,23},{8,24},{9,... | collective-permute-start | bytes 153608 | tf_op jit(solution)/shard_map/ppermute | solution.py:544
  125.2 2.3 %collective-permute-start.23 = (bf16[200,128]{1,0:T(8,128)(2,1)S(1)}, bf16[200,128]{1,0:T(8,128)(2,1)S(1)}, u32[]{:S(2)}, u32[]{:S(2)}) collective-permute-start(bf16[200,128]{1,0:T(8,128)(2,1)S(1)} %add.38.refs_0_), channel_id=1, source_target_pairs={{0,24},{1,25},{2,26},{3,27},{4,28},{5,29},{6,30},{7,31},{8,16},{9,... | collective-permute-start | bytes 153608 | tf_op jit(solution)/shard_map/ppermute | solution.py:544
  127.5 2.4 %collective-permute-done.23.refs_3_ = bf16[200,128]{1,0:T(8,128)(2,1)S(1)} collective-permute-done((bf16[200,128]{1,0:T(8,128)(2,1)S(1)}, bf16[200,128]{1,0:T(8,128)(2,1)S(1)}, u32[]{:S(2)}, u32[]{:S(2)}) %collective-permute-start.23) | collective-permute-done | bytes 51232 | tf_op jit(solution)/shard_map/ppermute | solution.py:544
  131.8 2.3 %collective-permute-start.28 = (bf16[512,512]{1,0:T(8,128)(2,1)}, bf16[512,512]{1,0:T(8,128)(2,1)}, u32[]{:S(2)}, u32[]{:S(2)}) collective-permute-start(bf16[512,512]{1,0:T(8,128)(2,1)} %relay.3), channel_id=1, source_target_pairs={{0,1},{1,0},{2,3},{3,2},{4,5},{5,4},{6,7},{7,6},{8,9},{9,8},{10,11... | collective-permute-start | bytes 1572872 | tf_op jit(solution)/shard_map/ppermute | solution.py:544
  134.3 2.0 %collective-permute-start.32 = (bf16[800,128]{1,0:T(8,128)(2,1)S(1)}, bf16[800,128]{1,0:T(8,128)(2,1)S(1)}, u32[]{:S(2)}, u32[]{:S(2)}) collective-permute-start(bf16[800,128]{1,0:T(8,128)(2,1)S(1)} %join.6.refs_0_), channel_id=1, source_target_pairs={{0,2},{1,3},{2,0},{3,1},{4,6},{5,7},{6,4},{7,5},{8,10},{9,11},{10,... | collective-permute-start | bytes 614408 | tf_op jit(solution)/shard_map/ppermute | solution.py:544
  138.7 2.5 %arrive.3 = f32[4,256,512]{2,1,0:T(8,128)} custom-call(s32[1]{0:T(128)} %bitcast.blk_ref.refs_1_, bf16[256,512]{1,0:T(8,128)(2,1)S(1)} %copy-done.9, bf16[512,512]{1,0:T(8,128)(2,1)} %collective-permute-done.28.near_ref, bf16[512,512]{1,0:T(8,128)(2,1)S(1)} %collective-permute-done.27.far_ref), custom_call_target="tpu_custom_call" | custom-call | flops 10000000 | bytes 100000 | tf_op jit(solution)/shard_map/arrive/pallas_call | solution.py:222
  142.2 4.6 %collective-permute-done.34.refs_3_ = bf16[800,128]{1,0:T(8,128)(2,1)S(1)} collective-permute-done((bf16[800,128]{1,0:T(8,128)(2,1)S(1)}, bf16[800,128]{1,0:T(8,128)(2,1)S(1)}, u32[]{:S(2)}, u32[]{:S(2)}) %collective-permute-start.34) | collective-permute-done | bytes 204832 | tf_op jit(solution)/shard_map/ppermute | solution.py:544
  148.2 2.7 %finish_mid.1 = (f32[1024,512]{1,0:T(8,128)}, f32[512,1024]{1,0:T(8,128)}, f32[512,512]{1,0:T(8,128)}) custom-call(s32[1]{0:T(128)} %bitcast.2.core_ref.refs_0_, bf16[1280,512]{1,0:T(8,128)(2,1)S(1)} %join.10.own_ref, bf16[1280,512]{1,0:T(8,128)(2,1)S(1)} %collective-permute-done.31.got_ref), custom_call_target="tpu_custom_call" | custom-call | flops 100000000 | bytes 8000000 | tf_op jit(solution)/shard_map/finish_mid/pallas_call | solution.py:530
  150.8 2.1 %finish_last.1 = (f32[512,1536]{1,0:T(8,128)}, f32[1,512]{1,0:T(1,128)}, f32[1,1024]{1,0:T(1,128)}, f32[1,512]{1,0:T(1,128)}, f32[1,512]{1,0:T(1,128)}, /*index=...) custom-call(s32[1]{0:T(128)} %bitcast.2.core_ref.refs_0_, ...), custom_call_target="tpu_custom_call" | custom-call | flops 100000000 | bytes 8000000 | tf_op jit(solution)/shard_map/finish_last/pallas_call | solution.py:530
  (117 shorter events, 25.6 us)
Async XLA Ops:
  2.8 4.2 %collective-permute-start = (bf16[256,512]{1,0:T(8,128)(2,1)}, bf16[256,512]{1,0:T(8,128)(2,1)S(1)}, u32[]{:S(2)}, u32[]{:S(2)}) collective-permute-start(bf16[256,512]{1,0:T(8,128)(2,1)} %get-tuple-element.165), channel_id=1, source_target_pairs={{0,1},{1,0},{2,3},{3,2},{4,5},{5,4},{6,7},{7,6},{8,9},{9,8},{10,11... | collective-permute-start | bytes 786440 | tf_op jit(solution)/shard_map/ppermute | solution.py:544
  2.9 9.4 %collective-permute-start.1 = (bf16[256,512]{1,0:T(8,128)(2,1)S(1)}, bf16[256,512]{1,0:T(8,128)(2,1)S(1)}, u32[]{:S(2)}, u32[]{:S(2)}) collective-permute-start(bf16[256,512]{1,0:T(8,128)(2,1)S(1)} %get-tuple-element.167), channel_id=1, source_target_pairs={{0,2},{1,3},{2,0},{3,1},{4,6},{5,7},{6,4},{7,5},{8,10},{9,11},{10,... | collective-permute-start | bytes 786440 | tf_op jit(solution)/shard_map/ppermute | solution.py:544
  5.5 12.3 %collective-permute-start.2 = (bf16[256,512]{1,0:T(8,128)(2,1)S(1)}, bf16[256,512]{1,0:T(8,128)(2,1)S(1)}, u32[]{:S(2)}, u32[]{:S(2)}) collective-permute-start(bf16[256,512]{1,0:T(8,128)(2,1)S(1)} %get-tuple-element.164), channel_id=1, source_target_pairs={{0,3},{1,2},{2,1},{3,0},{4,7},{5,6},{6,5},{7,4},{8,11},{9,10},{10,... | collective-permute-start | bytes 786440 | tf_op jit(solution)/shard_map/ppermute | solution.py:544
  17.8 16.6 %collective-permute-start.3 = (bf16[256,512]{1,0:T(8,128)(2,1)S(1)}, bf16[256,512]{1,0:T(8,128)(2,1)S(1)}, u32[]{:S(2)}, u32[]{:S(2)}) collective-permute-start(bf16[256,512]{1,0:T(8,128)(2,1)S(1)} %get-tuple-element.90), channel_id=1, source_target_pairs={{0,1},{1,0},{2,3},{3,2},{4,5},{5,4},{6,7},{7,6},{8,9},{9,8},{10,11... | collective-permute-start | bytes 786440 | tf_op jit(solution)/shard_map/ppermute | solution.py:544
  18.2 16.2 %collective-permute-start.4 = (bf16[256,512]{1,0:T(8,128)(2,1)S(1)}, bf16[256,512]{1,0:T(8,128)(2,1)S(1)}, u32[]{:S(2)}, u32[]{:S(2)}) collective-permute-start(bf16[256,512]{1,0:T(8,128)(2,1)S(1)} %get-tuple-element.91), channel_id=1, source_target_pairs={{0,2},{1,3},{2,0},{3,1},{4,6},{5,7},{6,4},{7,5},{8,10},{9,11},{10,... | collective-permute-start | bytes 786440 | tf_op jit(solution)/shard_map/ppermute | solution.py:544
  19.5 15.0 %collective-permute-start.5 = (bf16[256,512]{1,0:T(8,128)(2,1)S(1)}, bf16[256,512]{1,0:T(8,128)(2,1)S(1)}, u32[]{:S(2)}, u32[]{:S(2)}) collective-permute-start(bf16[256,512]{1,0:T(8,128)(2,1)S(1)} %get-tuple-element.92), channel_id=1, source_target_pairs={{0,3},{1,2},{2,1},{3,0},{4,7},{5,6},{6,5},{7,4},{8,11},{9,10},{10,... | collective-permute-start | bytes 786440 | tf_op jit(solution)/shard_map/ppermute | solution.py:544
  55.6 19.2 %collective-permute-start.7 = (bf16[320,512]{1,0:T(8,128)(2,1)S(1)}, bf16[320,512]{1,0:T(8,128)(2,1)S(1)}, u32[]{:S(2)}, u32[]{:S(2)}) collective-permute-start(bf16[320,512]{1,0:T(8,128)(2,1)S(1)} %get-tuple-element.105), channel_id=1, source_target_pairs={{0,2},{1,3},{2,0},{3,1},{4,6},{5,7},{6,4},{7,5},{8,10},{9,11},{10,... | collective-permute-start | bytes 983048 | tf_op jit(solution)/shard_map/ppermute | solution.py:544
  57.0 17.8 %collective-permute-start.8 = (bf16[320,512]{1,0:T(8,128)(2,1)S(1)}, bf16[320,512]{1,0:T(8,128)(2,1)S(1)}, u32[]{:S(2)}, u32[]{:S(2)}) collective-permute-start(bf16[320,512]{1,0:T(8,128)(2,1)S(1)} %get-tuple-element.106), channel_id=1, source_target_pairs={{0,4},{1,5},{2,6},{3,7},{4,0},{5,1},{6,2},{7,3},{8,12},{9,13},{10,... | collective-permute-start | bytes 983048 | tf_op jit(solution)/shard_map/ppermute | solution.py:544
  58.1 16.6 %collective-permute-start.9 = (bf16[320,512]{1,0:T(8,128)(2,1)S(1)}, bf16[320,512]{1,0:T(8,128)(2,1)S(1)}, u32[]{:S(2)}, u32[]{:S(2)}) collective-permute-start(bf16[320,512]{1,0:T(8,128)(2,1)S(1)} %get-tuple-element.107), channel_id=1, source_target_pairs={{0,6},{1,7},{2,4},{3,5},{4,2},{5,3},{6,0},{7,1},{8,14},{9,15},{10,... | collective-permute-start | bytes 983048 | tf_op jit(solution)/shard_map/ppermute | solution.py:544
  75.5 12.5 %collective-permute-start.13 = (bf16[512,512]{1,0:T(8,128)(2,1)S(1)}, bf16[512,512]{1,0:T(8,128)(2,1)S(1)}, u32[]{:S(2)}, u32[]{:S(2)}) collective-permute-start(bf16[512,512]{1,0:T(8,128)(2,1)S(1)} %copy-done.23), channel_id=1, source_target_pairs={{0,2},{1,3},{2,0},{3,1},{4,6},{5,7},{6,4},{7,5},{8,10},{9,11},{10,... | collective-permute-start | bytes 1572872 | tf_op jit(solution)/shard_map/ppermute | solution.py:544
  76.9 9.2 %collective-permute-start.10 = (bf16[80,512]{1,0:T(8,128)(2,1)S(1)}, bf16[80,512]{1,0:T(8,128)(2,1)S(1)}, u32[]{:S(2)}, u32[]{:S(2)}) collective-permute-start(bf16[80,512]{1,0:T(8,128)(2,1)S(1)} %get-tuple-element.117), channel_id=1, source_target_pairs={{0,8},{1,9},{2,10},{3,11},{4,12},{5,13},{6,14},{7,15},{8,0},{9,1},... | collective-permute-start | bytes 245768 | tf_op jit(solution)/shard_map/ppermute | solution.py:544
  78.2 7.9 %collective-permute-start.11 = (bf16[80,512]{1,0:T(8,128)(2,1)S(1)}, bf16[80,512]{1,0:T(8,128)(2,1)S(1)}, u32[]{:S(2)}, u32[]{:S(2)}) collective-permute-start(bf16[80,512]{1,0:T(8,128)(2,1)S(1)} %get-tuple-element.118), channel_id=1, source_target_pairs={{0,16},{1,17},{2,18},{3,19},{4,20},{5,21},{6,22},{7,23},{8,24},{9,... | collective-permute-start | bytes 245768 | tf_op jit(solution)/shard_map/ppermute | solution.py:544
  80.5 5.6 %collective-permute-start.12 = (bf16[80,512]{1,0:T(8,128)(2,1)S(1)}, bf16[80,512]{1,0:T(8,128)(2,1)S(1)}, u32[]{:S(2)}, u32[]{:S(2)}) collective-permute-start(bf16[80,512]{1,0:T(8,128)(2,1)S(1)} %get-tuple-element.119), channel_id=1, source_target_pairs={{0,24},{1,25},{2,26},{3,27},{4,28},{5,29},{6,30},{7,31},{8,16},{9,... | collective-permute-start | bytes 245768 | tf_op jit(solution)/shard_map/ppermute | solution.py:544
  89.9 5.4 %collective-permute-start.25 = (bf16[80,512]{1,0:T(8,128)(2,1)S(1)}, bf16[80,512]{1,0:T(8,128)(2,1)S(1)}, u32[]{:S(2)}, u32[]{:S(2)}) collective-permute-start(bf16[80,512]{1,0:T(8,128)(2,1)S(1)} %add.35.refs_0_), channel_id=1, source_target_pairs={{0,8},{1,9},{2,10},{3,11},{4,12},{5,13},{6,14},{7,15},{8,0},{9,1},... | collective-permute-start | bytes 245768 | tf_op jit(solution)/shard_map/ppermute | solution.py:544
  92.6 12.3 %collective-permute-start.15 = (bf16[800,128]{1,0:T(8,128)(2,1)S(1)}, bf16[800,128]{1,0:T(8,128)(2,1)S(1)}, u32[]{:S(2)}, u32[]{:S(2)}) collective-permute-start(bf16[800,128]{1,0:T(8,128)(2,1)S(1)} %get-tuple-element.124), channel_id=1, source_target_pairs={{0,2},{1,3},{2,0},{3,1},{4,6},{5,7},{6,4},{7,5},{8,10},{9,11},{10,... | collective-permute-start | bytes 614408 | tf_op jit(solution)/shard_map/ppermute | solution.py:544
  94.0 10.9 %collective-permute-start.16 = (bf16[800,128]{1,0:T(8,128)(2,1)S(1)}, bf16[800,128]{1,0:T(8,128)(2,1)S(1)}, u32[]{:S(2)}, u32[]{:S(2)}) collective-permute-start(bf16[800,128]{1,0:T(8,128)(2,1)S(1)} %get-tuple-element.125), channel_id=1, source_target_pairs={{0,4},{1,5},{2,6},{3,7},{4,0},{5,1},{6,2},{7,3},{8,12},{9,13},{10,... | collective-permute-start | bytes 614408 | tf_op jit(solution)/shard_map/ppermute | solution.py:544
  95.2 9.7 %collective-permute-start.17 = (bf16[800,128]{1,0:T(8,128)(2,1)S(1)}, bf16[800,128]{1,0:T(8,128)(2,1)S(1)}, u32[]{:S(2)}, u32[]{:S(2)}) collective-permute-start(bf16[800,128]{1,0:T(8,128)(2,1)S(1)} %get-tuple-element.126), channel_id=1, source_target_pairs={{0,6},{1,7},{2,4},{3,5},{4,2},{5,3},{6,0},{7,1},{8,14},{9,15},{10,... | collective-permute-start | bytes 614408 | tf_op jit(solution)/shard_map/ppermute | solution.py:544
  95.3 9.5 %collective-permute-start.26 = (bf16[160,512]{1,0:T(8,128)(2,1)S(1)}, bf16[160,512]{1,0:T(8,128)(2,1)S(1)}, u32[]{:S(2)}, u32[]{:S(2)}) collective-permute-start(bf16[160,512]{1,0:T(8,128)(2,1)S(1)} %join.7.refs_0_), channel_id=1, source_target_pairs={{0,16},{1,17},{2,18},{3,19},{4,20},{5,21},{6,22},{7,23},{8,24},{9,... | collective-permute-start | bytes 491528 | tf_op jit(solution)/shard_map/ppermute | solution.py:544
  105.6 10.8 %collective-permute-start.29 = (bf16[320,512]{1,0:T(8,128)(2,1)S(1)}, bf16[320,512]{1,0:T(8,128)(2,1)S(1)}, u32[]{:S(2)}, u32[]{:S(2)}) collective-permute-start(bf16[320,512]{1,0:T(8,128)(2,1)S(1)} %join.8.refs_0_), channel_id=1, source_target_pairs={{0,2},{1,3},{2,0},{3,1},{4,6},{5,7},{6,4},{7,5},{8,10},{9,11},{10,... | collective-permute-start | bytes 983048 | tf_op jit(solution)/shard_map/ppermute | solution.py:544
  107.0 4.6 %collective-permute-start.18 = (bf16[200,128]{1,0:T(8,128)(2,1)S(1)}, bf16[200,128]{1,0:T(8,128)(2,1)S(1)}, u32[]{:S(2)}, u32[]{:S(2)}) collective-permute-start(bf16[200,128]{1,0:T(8,128)(2,1)S(1)} %get-tuple-element.128), channel_id=1, source_target_pairs={{0,8},{1,9},{2,10},{3,11},{4,12},{5,13},{6,14},{7,15},{8,0},{9,1},... | collective-permute-start | bytes 153608 | tf_op jit(solution)/shard_map/ppermute | solution.py:544
  108.4 5.2 %collective-permute-start.19 = (bf16[200,128]{1,0:T(8,128)(2,1)S(1)}, bf16[200,128]{1,0:T(8,128)(2,1)S(1)}, u32[]{:S(2)}, u32[]{:S(2)}) collective-permute-start(bf16[200,128]{1,0:T(8,128)(2,1)S(1)} %get-tuple-element.129), channel_id=1, source_target_pairs={{0,16},{1,17},{2,18},{3,19},{4,20},{5,21},{6,22},{7,23},{8,24},{9,... | collective-permute-start | bytes 153608 | tf_op jit(solution)/shard_map/ppermute | solution.py:544
  111.6 4.9 %collective-permute-start.20 = (bf16[200,128]{1,0:T(8,128)(2,1)S(1)}, bf16[200,128]{1,0:T(8,128)(2,1)S(1)}, u32[]{:S(2)}, u32[]{:S(2)}) collective-permute-start(bf16[200,128]{1,0:T(8,128)(2,1)S(1)} %get-tuple-element.130), channel_id=1, source_target_pairs={{0,24},{1,25},{2,26},{3,27},{4,28},{5,29},{6,30},{7,31},{8,16},{9,... | collective-permute-start | bytes 153608 | tf_op jit(solution)/shard_map/ppermute | solution.py:544
  116.5 17.6 %collective-permute-start.30 = (bf16[640,512]{1,0:T(8,128)(2,1)S(1)}, bf16[640,512]{1,0:T(8,128)(2,1)S(1)}, u32[]{:S(2)}, u32[]{:S(2)}) collective-permute-start(bf16[640,512]{1,0:T(8,128)(2,1)S(1)} %join.9.refs_0_), channel_id=1, source_target_pairs={{0,4},{1,5},{2,6},{3,7},{4,0},{5,1},{6,2},{7,3},{8,12},{9,13},{10,... | collective-permute-start | bytes 1966088 | tf_op jit(solution)/shard_map/ppermute | solution.py:544
  117.8 12.2 %collective-permute-start.27 = (bf16[512,512]{1,0:T(8,128)(2,1)}, bf16[512,512]{1,0:T(8,128)(2,1)S(1)}, u32[]{:S(2)}, u32[]{:S(2)}) collective-permute-start(bf16[512,512]{1,0:T(8,128)(2,1)} %get-tuple-element.142), channel_id=1, source_target_pairs={{0,2},{1,3},{2,0},{3,1},{4,6},{5,7},{6,4},{7,5},{8,10},{9,11},{10,... | collective-permute-start | bytes 1572872 | tf_op jit(solution)/shard_map/ppermute | solution.py:544
  118.8 17.7 %collective-permute-start.24 = (bf16[512,512]{1,0:T(8,128)(2,1)}, bf16[512,512]{1,0:T(8,128)(2,1)S(1)}, u32[]{:S(2)}, u32[]{:S(2)}) collective-permute-start(bf16[512,512]{1,0:T(8,128)(2,1)} %relay.2), channel_id=1, source_target_pairs={{0,1},{1,0},{2,3},{3,2},{4,5},{5,4},{6,7},{7,6},{8,9},{9,8},{10,11... | collective-permute-start | bytes 1572872 | tf_op jit(solution)/shard_map/ppermute | solution.py:544
  121.8 5.7 %collective-permute-start.22 = (bf16[200,128]{1,0:T(8,128)(2,1)S(1)}, bf16[200,128]{1,0:T(8,128)(2,1)S(1)}, u32[]{:S(2)}, u32[]{:S(2)}) collective-permute-start(bf16[200,128]{1,0:T(8,128)(2,1)S(1)} %add.38.refs_0_), channel_id=1, source_target_pairs={{0,16},{1,17},{2,18},{3,19},{4,20},{5,21},{6,22},{7,23},{8,24},{9,... | collective-permute-start | bytes 153608 | tf_op jit(solution)/shard_map/ppermute | solution.py:544
  125.2 4.8 %collective-permute-start.23 = (bf16[200,128]{1,0:T(8,128)(2,1)S(1)}, bf16[200,128]{1,0:T(8,128)(2,1)S(1)}, u32[]{:S(2)}, u32[]{:S(2)}) collective-permute-start(bf16[200,128]{1,0:T(8,128)(2,1)S(1)} %add.38.refs_0_), channel_id=1, source_target_pairs={{0,24},{1,25},{2,26},{3,27},{4,28},{5,29},{6,30},{7,31},{8,16},{9,... | collective-permute-start | bytes 153608 | tf_op jit(solution)/shard_map/ppermute | solution.py:544
  131.8 6.8 %collective-permute-start.28 = (bf16[512,512]{1,0:T(8,128)(2,1)}, bf16[512,512]{1,0:T(8,128)(2,1)}, u32[]{:S(2)}, u32[]{:S(2)}) collective-permute-start(bf16[512,512]{1,0:T(8,128)(2,1)} %relay.3), channel_id=1, source_target_pairs={{0,1},{1,0},{2,3},{3,2},{4,5},{5,4},{6,7},{7,6},{8,9},{9,8},{10,11... | collective-permute-start | bytes 1572872 | tf_op jit(solution)/shard_map/ppermute | solution.py:544
  134.2 13.9 %collective-permute-start.31 = (bf16[1280,512]{1,0:T(8,128)(2,1)S(1)}, bf16[1280,512]{1,0:T(8,128)(2,1)S(1)}, u32[]{:S(2)}, u32[]{:S(2)}) collective-permute-start(bf16[1280,512]{1,0:T(8,128)(2,1)S(1)} %join.10.own_ref), channel_id=1, source_target_pairs={{0,1},{1,0},{2,3},{3,2},{4,5},{5,4},{6,7},{7,6},{8,9},{9,8},{10,11... | collective-permute-start | bytes 3932168 | tf_op jit(solution)/shard_map/ppermute | solution.py:544
  134.3 7.1 %collective-permute-start.32 = (bf16[800,128]{1,0:T(8,128)(2,1)S(1)}, bf16[800,128]{1,0:T(8,128)(2,1)S(1)}, u32[]{:S(2)}, u32[]{:S(2)}) collective-permute-start(bf16[800,128]{1,0:T(8,128)(2,1)S(1)} %join.6.refs_0_), channel_id=1, source_target_pairs={{0,2},{1,3},{2,0},{3,1},{4,6},{5,7},{6,4},{7,5},{8,10},{9,11},{10,... | collective-permute-start | bytes 614408 | tf_op jit(solution)/shard_map/ppermute | solution.py:544
  136.3 5.9 %collective-permute-start.33 = (bf16[800,128]{1,0:T(8,128)(2,1)S(1)}, bf16[800,128]{1,0:T(8,128)(2,1)S(1)}, u32[]{:S(2)}, u32[]{:S(2)}) collective-permute-start(bf16[800,128]{1,0:T(8,128)(2,1)S(1)} %join.6.refs_0_), channel_id=1, source_target_pairs={{0,4},{1,5},{2,6},{3,7},{4,0},{5,1},{6,2},{7,3},{8,12},{9,13},{10,... | collective-permute-start | bytes 614408 | tf_op jit(solution)/shard_map/ppermute | solution.py:544
  136.6 10.2 %collective-permute-start.34 = (bf16[800,128]{1,0:T(8,128)(2,1)S(1)}, bf16[800,128]{1,0:T(8,128)(2,1)S(1)}, u32[]{:S(2)}, u32[]{:S(2)}) collective-permute-start(bf16[800,128]{1,0:T(8,128)(2,1)S(1)} %join.6.refs_0_), channel_id=1, source_target_pairs={{0,6},{1,7},{2,4},{3,5},{4,2},{5,3},{6,0},{7,1},{8,14},{9,15},{10,... | collective-permute-start | bytes 614408 | tf_op jit(solution)/shard_map/ppermute | solution.py:544
  (28 other events, 334.5 us)
